TPU v7x, 128 devices: a whole 4x4x4 slice. The times are simulated.
128 devices in a mesh: row: 8 (over y, core), col: 16 (over x, z).
Axes of the slice: x: 4, y: 4, z: 4, core: 2. Of those that a mesh axis runs over, the one named last changes fastest.
Arguments:
- noise: bfloat16 [8192, 4096], P('row', 'col'), may hold values from -6 to 6
- latents: bfloat16 [16384, 4096], P('col', 'row'), may hold values from -12 to 12
Outputs:
- transported: bfloat16 [8192, 4096], P('row', 'col')
- row_potential: float32 [8192], P('row')
- col_potential: float32 [16384], P('col')
All inputs are finite; a program needn't handle non-finite values.
Results may differ from a plain program's by a relative error of at most 0.018.
Values may be sent and summed in bfloat16 or wider, within the bound.
No kernel may reach another device: no remote copies, remote signals or barrier semaphores. Data moves between devices by JAX's collectives and lax.ppermute only.
A program may use at most 64 MiB of HBM per device.

v0:
```python
import functools
import math

import jax
import jax.numpy as jnp
from jax import lax
from jax.experimental import pallas as pl
from jax.experimental.pallas import tpu as pltpu
from jax.sharding import PartitionSpec as P

ITERS = 3
EPSILON = 0.01
LOG2E = math.log2(math.e)
LN2 = math.log(2.0)
NX, NY, NZ, NC = 4, 4, 4, 2

F32 = jnp.float32
BF16 = jnp.bfloat16


def shift_z(by):
    return [(x * NZ + z, x * NZ + (z + by) % NZ) for x in range(NX) for z in range(NZ)]


def shift_x(by):
    return [(x * NZ + z, (x + by) % NX * NZ + z) for x in range(NX) for z in range(NZ)]


def shift_y(by):
    return [(y * NC + c, (y + by) % NY * NC + c) for y in range(NY) for c in range(NC)]


def swap_core():
    return [(y * NC + c, y * NC + 1 - c) for y in range(NY) for c in range(NC)]


def logadd(parts):
    high = functools.reduce(jnp.maximum, parts)
    total = functools.reduce(jnp.add, [jnp.exp2(p - high) for p in parts])
    return high + jnp.log2(total)


BOTH = ("row", "col")


def spread_y():
    return [
        (y * NC + c, (y + 1 - 2 * c) % NY * NC + c) for y in range(NY) for c in range(NC)
    ]


def everywhere(perms):
    count = NX * NZ
    return [
        (row * count + a, row * count + b) for row in range(NY * NC) for a, b in perms[row % NC]
    ]


def around(value, axis, spread, opposite, combine):
    far = lax.ppermute(value, axis, opposite)
    near = lax.ppermute(value, axis, spread)
    return combine([value, far, near, lax.ppermute(near, "row", swap_core())])


def over_col(value, combine):
    mine = lax.axis_index("row") % NC == 0
    other = lax.ppermute(value, "row", swap_core())
    both = jnp.concatenate(
        [jnp.where(mine, value, other), jnp.where(mine, other, value)], axis=0
    )
    for shift in (shift_z, shift_x):
        both = around(both, BOTH, everywhere([shift(1), shift(-1)]), everywhere([shift(2)] * 2), combine)
    return jnp.where(mine, both[:1], both[1:])


def over_row(value, combine):
    value = combine([value, lax.ppermute(value, "row", swap_core())])
    return around(value, "row", spread_y(), shift_y(2), combine)


ORDER = (0, 1, 3, 2)


def hop_f(value, by):
    return lax.ppermute(value, BOTH, everywhere([shift_z(by), shift_x(by)]))


def hop_s(value, by):
    return lax.ppermute(value, BOTH, everywhere([shift_x(by), shift_z(by)]))


def gather(noise, latents):
    rows, width = noise.shape
    half = rows // 2
    swap = lambda v: lax.ppermute(v, "row", swap_core())
    opposite = hop_f(noise, 2)
    line = [noise, hop_f(noise, -1), hop_f(noise, 1), opposite]
    near = lax.ppermute(latents, "row", spread_y())
    away = lax.ppermute(latents, "row", [(b, a) for a, b in spread_y()])
    top, end = halves_call(line)
    after, _, _ = lax.optimization_barrier((near, top, end))
    top_m, end_p = hop_s(top, 1), hop_s(end, -1)
    end_m, top_p = hop_s(end, 1), hop_s(top, -1)
    far = lax.ppermute(after, "row", spread_y())
    first, last, other = lax.optimization_barrier((top_m, end_p, swap(latents)))
    top_far, end_far = hop_s(first, 1), hop_s(last, -1)
    end_m, top_p, here, there = lax.optimization_barrier((end_m, top_p, near, away))
    near_other, away_other = swap(here), swap(there)
    split = lambda v: v.reshape(4, half, width)
    lat = [latents, other, near, near_other, away, away_other, far, swap(far)]
    return (
        line,
        [split(v) for v in (top_p, end_p, top_m, end_m)],
        [split(top_far), split(end_far)],
        lat,
    )


def latent_spots():
    row, col = lax.axis_index("row"), lax.axis_index("col")
    y, core = row // NC, row % NC
    block = lambda dy, flip: (y + dy) % NY * NC + (core if not flip else 1 - core)
    back = jnp.where(core == 0, 3, 1)
    rows = [
        block(0, False), block(0, True), block(back, False), block(4 - back, True),
        block(4 - back, False), block(back, True), block(2, False), block(2, True),
    ]
    at = (jnp.stack(rows)[:, None] * 2 + jnp.arange(2)[None, :]).reshape(-1)
    dx, dz = (at // NZ - col // NZ) % NX, (at % NZ - col % NZ) % NZ
    df, ds = jnp.where(core == 0, dz, dx), jnp.where(core == 0, dx, dz)
    rank = lambda d: jnp.where(d < 2, d, 5 - d)
    return (rank(ds) * 4 + rank(df)).astype(jnp.int32)


def scatter_sum(plan, spots, lat, far_top, far_end, mass, rowpot, colpot):
    barrier = lax.optimization_barrier
    far_top, far_end = hop_s(far_top, 1), hop_s(far_end, -1)
    end, top, after, before = share_call(spots, lat, plan, mass)
    end_m, top_p = hop_s(end, 1), hop_s(top, -1)
    top, end = onward_call(plan, after, before, mass, far_top, far_end)
    top_m, end_p = hop_s(top, 1), hop_s(end, -1)
    plan, rowpot, colpot, _, _ = barrier((plan, rowpot, colpot, top, end))
    own, mass = own_call(spots, lat, plan, mass, top_p, end_m)
    rowpot, colpot = rowpot * LN2, colpot * LN2
    own, top_m, end_p, rowpot, colpot = barrier((own, top_m, end_p, rowpot, colpot))
    keep, mass, *parts = sum_call(own, mass, top_m, end_p)
    parts = [hop_f(v, ORDER[k]) for v, k in zip(parts, (3, 2, 1))]
    return finish_call(keep, mass, parts).astype(BF16), rowpot, colpot


def steps_of(total, step, body):
    def turn(i, _):
        body(pl.ds(pl.multiple_of(i * step, step), step))
        return 0

    lax.fori_loop(0, total // step, turn, 0)


def eye():
    return lax.broadcasted_iota(jnp.int32, (128, 128), 0) == lax.broadcasted_iota(
        jnp.int32, (128, 128), 1
    )


def to_lanes(column):
    mask = eye()
    return jnp.concatenate(
        [
            jnp.sum(jnp.where(mask, column[at : at + 128], 0.0), axis=0, keepdims=True)
            for at in range(0, column.shape[0], 128)
        ],
        axis=1,
    )


def to_sublanes(line):
    mask = eye()
    return jnp.concatenate(
        [
            jnp.sum(jnp.where(mask, line[:, at : at + 128], 0.0), axis=1, keepdims=True)
            for at in range(0, line.shape[1], 128)
        ],
        axis=0,
    )


TAIL = 16


def pack(mass, lanes):
    high = mass.astype(BF16).astype(F32)
    row = lax.broadcasted_iota(jnp.int32, (TAIL, lanes), 0)
    out = jnp.zeros((TAIL, lanes), F32)
    line = jnp.concatenate([high, mass - high], axis=1)
    for k in range(line.shape[1] // lanes):
        out = jnp.where(row == k, line[:, k * lanes : (k + 1) * lanes], out)
    return out.astype(BF16)


def unpack(tail, count):
    tail = tail.astype(F32)
    line = jnp.concatenate([tail[k : k + 1] for k in range(2 * count // tail.shape[1])], axis=1)
    return line[:, :count] + line[:, count:]


def row_lse_block(logits_ref, rows, colpot, lse_ref):
    step = 32
    columns = []
    for at in range(0, rows.size, step):
        t = logits_ref[pl.ds(rows.start + at, step), :] + colpot
        high = jnp.max(t, axis=1, keepdims=True)
        total = jnp.sum(jnp.exp2(t - high), axis=1, keepdims=True)
        columns.append(high + jnp.log2(total))
    lse_ref[:, rows] = to_lanes(jnp.concatenate(columns, axis=0))


WIDE = 512


def halves_kernel(*refs):
    blocks, outs, sem = refs[:4], refs[4:6], refs[6]
    half = blocks[0].shape[0] // 2
    copies = [
        pltpu.make_async_copy(
            block.at[pl.ds(part * half, half), :], out.at[pl.ds(k * half, half), :], sem.at[part, k]
        )
        for part, out in enumerate(outs)
        for k, block in enumerate(blocks)
    ]
    for copy in copies:
        copy.start()
    for copy in copies:
        copy.wait()


def halves_call(blocks):
    rows, width = blocks[0].shape
    return pl.pallas_call(
        halves_kernel,
        in_specs=[pl.BlockSpec(memory_space=pl.ANY)] * 4,
        out_specs=[pl.BlockSpec(memory_space=pl.ANY)] * 2,
        out_shape=[jax.ShapeDtypeStruct((2 * rows, width), BF16)] * 2,
        scratch_shapes=[pltpu.SemaphoreType.DMA((2, 4))],
        cost_estimate=pl.CostEstimate(
            flops=0, bytes_accessed=16 * rows * width, transcendentals=0
        ),
        compiler_params=pltpu.CompilerParams(vmem_limit_bytes=2 * 2**20),
        name="halves",
    )(*blocks)


def fetch(quarter, spot_ref, lat_refs, buf, sem):
    width = buf.shape[1] // 4
    for n in range(16):
        spot = spot_ref[n]

        @pl.when(spot // 4 == quarter)
        def start():
            lane = pl.multiple_of(lax.rem(spot, 4) * width, width)
            pltpu.make_async_copy(
                lat_refs[n // 2].at[:, pl.ds(n % 2 * width, width)], buf.at[:, pl.ds(lane, width)], sem
            ).start()


def arrive(buf, sem):
    pltpu.make_async_copy(buf, buf, sem).wait()


def near_kernel(spot_ref, *refs):
    line_refs, near_refs, lat_refs = refs[:4], refs[4:8], refs[8:16]
    cross_ref, last_ref, noise_buf, lat_buf, noise_sem, lat_sem, last_sem = refs[16:]
    half = cross_ref.shape[0] // 2
    width = line_refs[0].shape[1]

    def start(quarter):
        slot = lax.rem(quarter, 2)
        fetch(quarter, spot_ref, lat_refs, lat_buf.at[slot], lat_sem.at[slot])
        for k in range(4):
            lanes = pl.ds(k * width, width)

            @pl.when(quarter == 0)
            def whole():
                pltpu.make_async_copy(
                    line_refs[k], noise_buf.at[slot, :, lanes], noise_sem.at[slot]
                ).start()

            for part in range(4):

                @pl.when(quarter == 1 + part // 2)
                def halves():
                    pltpu.make_async_copy(
                        near_refs[part].at[k],
                        noise_buf.at[slot, pl.ds(part % 2 * half, half), lanes],
                        noise_sem.at[slot],
                    ).start()

    start(jnp.int32(0))
    fetch(3, spot_ref, lat_refs, last_ref, last_sem)

    def clear(rows):
        cross_ref[rows, :] = jnp.zeros((128, cross_ref.shape[1]), F32)

    steps_of(cross_ref.shape[0], 128, clear)

    def multiply(quarter, _):
        slot = lax.rem(quarter, 2)
        arrive(noise_buf.at[slot], noise_sem.at[slot])
        arrive(lat_buf.at[slot], lat_sem.at[slot])
        pl.when(quarter < 2)(lambda: start(quarter + 1))
        cross_ref[...] += lax.dot_general(
            noise_buf[slot], lat_buf[slot], (((1,), (1,)), ((), ())), preferred_element_type=F32
        )
        return 0

    lax.fori_loop(0, 3, multiply, 0)
    arrive(last_ref, last_sem)


def in_hbm(value):
    return pltpu.with_memory_space_constraint(value, pltpu.HBM)


def near_call(spots, line, near, lat):
    rows, width = line[0].shape
    cols = lat[0].shape[0]
    return pl.pallas_call(
        near_kernel,
        in_specs=[pl.BlockSpec(memory_space=pltpu.SMEM)] + [pl.BlockSpec(memory_space=pl.ANY)] * 16,
        out_specs=[pl.BlockSpec(memory_space=pltpu.VMEM)] * 2,
        out_shape=[
            jax.ShapeDtypeStruct((rows, cols), F32),
            jax.ShapeDtypeStruct((cols, 4 * width), BF16),
        ],
        scratch_shapes=[
            pltpu.VMEM((2, rows, 4 * width), BF16),
            pltpu.VMEM((2, cols, 4 * width), BF16),
            pltpu.SemaphoreType.DMA((2,)),
            pltpu.SemaphoreType.DMA((2,)),
            pltpu.SemaphoreType.DMA,
        ],
        cost_estimate=pl.CostEstimate(
            flops=8 * rows * cols * 12 * width,
            bytes_accessed=2 * (rows * 12 + cols * 16) * width + 4 * rows * cols,
            transcendentals=0,
        ),
        compiler_params=pltpu.CompilerParams(vmem_limit_bytes=14 * 2**20),
        name="cross_near",
    )(spots, *[in_hbm(v) for v in (*line, *near)], *[v if k % 2 else in_hbm(v) for k, v in enumerate(lat)])


def far_kernel(scale, top_ref, end_ref, lat_ref, cross_ref, logits_ref, lse_ref):
    half = top_ref.shape[1]

    def multiply(lanes):
        for start, part_ref in ((0, top_ref), (half, end_ref)):
            rows = pl.ds(start, half)
            noise = jnp.concatenate([part_ref[k] for k in range(4)], axis=1)
            cross = lax.dot_general(
                noise, lat_ref[lanes, :], (((1,), (1,)), ((), ())), preferred_element_type=F32
            )
            logits_ref[rows, lanes] = (cross_ref[rows, lanes] + cross) * scale

    steps_of(lat_ref.shape[0], WIDE, multiply)
    steps_of(logits_ref.shape[0], 256, lambda rows: row_lse_block(logits_ref, rows, 0.0, lse_ref))


def far_call(far, lat, cross, scale):
    rows, cols = cross.shape
    out_shape = [
        jax.ShapeDtypeStruct((rows, cols), F32),
        jax.ShapeDtypeStruct((1, rows), F32),
    ]
    return in_vmem(
        functools.partial(far_kernel, scale), "cross_far", out_shape,
        2 * rows * cols * lat.shape[1], *far, lat, cross,
    )


def row_kernel(logits_ref, colpot_ref, lse_ref):
    colpot = colpot_ref[...]
    steps_of(logits_ref.shape[0], 256, lambda rows: row_lse_block(logits_ref, rows, colpot, lse_ref))


def row_call(logits, colpot):
    out_shape = [jax.ShapeDtypeStruct((1, logits.shape[0]), F32)]
    return in_vmem(row_kernel, "row_lse", out_shape, 8 * logits.size, logits, colpot)[0]


def col_kernel(logits_ref, rowpot_ref, lse_ref):
    rows, cols = logits_ref.shape
    block = 256

    def some_rows(i, parts):
        first = pl.multiple_of(i * block, block)
        rowpot = to_sublanes(rowpot_ref[:, pl.ds(first, block)])
        rowpot = jnp.broadcast_to(rowpot, (block, 128))
        lines = []
        for at in range(0, cols, 128):
            t = logits_ref[pl.ds(first, block), pl.ds(at, 128)] + rowpot
            high = jnp.max(t, axis=0, keepdims=True)
            total = jnp.sum(jnp.exp2(t - high), axis=0, keepdims=True)
            lines.append(high + jnp.log2(total))
        part = jnp.concatenate(lines, axis=1)
        row = lax.broadcasted_iota(jnp.int32, parts.shape, 0)
        return jnp.where(row == i, part, parts)

    parts = lax.fori_loop(
        0, rows // block, some_rows, jnp.full((rows // block, cols), -jnp.inf, F32)
    )
    high = jnp.max(parts, axis=0, keepdims=True)
    lse_ref[...] = high + jnp.log2(jnp.sum(jnp.exp2(parts - high), axis=0, keepdims=True))


def col_call(logits, rowpot):
    out_shape = [jax.ShapeDtypeStruct((1, logits.shape[1]), F32)]
    return in_vmem(col_kernel, "col_lse", out_shape, 8 * logits.size, logits, rowpot)[0]


def plan_kernel(logits_ref, rowpot_ref, colpot_ref, lat_ref, plan_ref, mass_ref, top_ref, end_ref):
    rows = logits_ref.shape[0]
    half = rows // 2
    colpot = colpot_ref[...]

    def make_half(block):
        sums = []
        for k in range(0, half, 64):
            at = pl.ds(block.start + k, 64)
            if k % 128 == 0:
                rowpot = to_sublanes(rowpot_ref[:, pl.ds(block.start + k, 128)])
            plan = jnp.exp2(logits_ref[at, :] + rowpot[k % 128 : k % 128 + 64] + colpot).astype(BF16)
            plan_ref[at, :] = plan
            sums.append(jnp.sum(plan.astype(F32), axis=1, keepdims=True))
        mass = to_lanes(jnp.concatenate(sums, axis=0))
        mass_ref[:, block] = mass
        share = jnp.dot(plan_ref[block, :], lat_ref[...], preferred_element_type=F32).astype(BF16)
        tail = pack(mass, lat_ref.shape[1])
        for start, out_ref in ((0, top_ref), (half, end_ref)):

            @pl.when(block.start == start)
            def put():
                out_ref[:half, :] = share
                out_ref[half:, :] = tail

    steps_of(rows, half, make_half)


def multiply_into(out_ref, plan_ref, rows, lat_ref, more_ref=None):
    here = pl.ds(0, rows.size)

    def multiply(lanes):
        share = jnp.dot(plan_ref[rows, :], lat_ref[:, lanes], preferred_element_type=F32)
        if more_ref is not None:
            share = share + more_ref[here, lanes].astype(F32)
        out_ref[here, lanes] = share.astype(out_ref.dtype)

    steps_of(lat_ref.shape[1], WIDE, multiply)


def in_vmem(kernel, name, out_shape, flops, *args):
    return pl.pallas_call(
        kernel,
        in_specs=[pl.BlockSpec(memory_space=pltpu.VMEM)] * len(args),
        out_specs=jax.tree.map(lambda _: pl.BlockSpec(memory_space=pltpu.VMEM), out_shape),
        out_shape=out_shape,
        cost_estimate=pl.CostEstimate(
            flops=flops,
            bytes_accessed=sum(a.size * a.dtype.itemsize for a in args),
            transcendentals=0,
        ),
        compiler_params=pltpu.CompilerParams(vmem_limit_bytes=24 * 2**20),
        name=name,
    )(*args)


def plan_call(logits, rowpot, colpot, lat):
    rows, cols = logits.shape
    depth = lat.shape[1]
    share = jax.ShapeDtypeStruct((rows // 2 + TAIL, depth), BF16)
    out_shape = [
        jax.ShapeDtypeStruct((rows, cols), BF16),
        jax.ShapeDtypeStruct((1, rows), F32),
        share,
        share,
    ]
    return in_vmem(
        plan_kernel, "plan", out_shape, 2 * rows * cols * depth, logits, rowpot, colpot, lat
    )


def lat_call(kernel, name, out_shape, flops, spots, lat, scratch, *args):
    space = [pltpu.SMEM] + [pl.ANY] * len(lat) + [pltpu.VMEM] * len(args)
    return pl.pallas_call(
        kernel,
        in_specs=[pl.BlockSpec(memory_space=m) for m in space],
        out_specs=[pl.BlockSpec(memory_space=pltpu.VMEM)] * len(out_shape),
        out_shape=out_shape,
        scratch_shapes=scratch,
        cost_estimate=pl.CostEstimate(
            flops=flops,
            bytes_accessed=sum(a.size * a.dtype.itemsize for a in args),
            transcendentals=0,
        ),
        compiler_params=pltpu.CompilerParams(vmem_limit_bytes=24 * 2**20),
        name=name,
    )(spots, *lat, *args)


def share_kernel(spot_ref, *refs):
    lat_refs, plan_ref, mass_ref = refs[:8], refs[8], refs[9]
    end_ref, top_ref, after_ref, before_ref, sem = refs[10:]
    half = plan_ref.shape[0] // 2
    fetch(1, spot_ref, lat_refs, after_ref, sem.at[0])
    fetch(2, spot_ref, lat_refs, before_ref, sem.at[1])
    for n, (lat_ref, out_ref, rows) in enumerate(
        ((after_ref, end_ref, pl.ds(half, half)), (before_ref, top_ref, pl.ds(0, half)))
    ):
        out_ref[half:, :] = pack(mass_ref[:, rows], out_ref.shape[1])
        arrive(lat_ref, sem.at[n])
        multiply_into(out_ref, plan_ref, rows, lat_ref)


def share_call(spots, lat, plan, mass):
    rows, cols = plan.shape
    depth = 2 * lat[0].shape[1]
    share = jax.ShapeDtypeStruct((rows // 2 + TAIL, depth), BF16)
    quarter = jax.ShapeDtypeStruct((cols, depth), BF16)
    return lat_call(
        share_kernel, "share", [share, share, quarter, quarter], 2 * rows * cols * depth,
        spots, lat, [pltpu.SemaphoreType.DMA((2,))], plan, mass,
    )


def onward_kernel(plan_ref, after_ref, before_ref, mass_ref, top_more, end_more, top_ref, end_ref):
    half = plan_ref.shape[0] // 2
    for lat_ref, more, rows, out_ref in (
        (after_ref, top_more, pl.ds(0, half), top_ref),
        (before_ref, end_more, pl.ds(half, half), end_ref),
    ):
        multiply_into(out_ref, plan_ref, rows, lat_ref, more)
        out_ref[half:, :] = pack(mass_ref[:, rows] + unpack(more[half:, :], half), out_ref.shape[1])


def onward_call(plan, after, before, mass, top_more, end_more):
    rows, cols = plan.shape
    depth = after.shape[1]
    out_shape = [jax.ShapeDtypeStruct((rows // 2 + TAIL, depth), BF16)] * 2
    return in_vmem(
        onward_kernel, "onward", out_shape, 2 * rows * cols * depth,
        plan, after, before, mass, top_more, end_more,
    )


def sum_kernel(own_ref, mass_ref, top_ref, end_ref, keep_ref, total_ref, *part_refs):
    rows = own_ref.shape[0]
    half, width = rows // 2, keep_ref.shape[1]
    for start, more in ((0, top_ref), (half, end_ref)):
        there = pl.ds(start, half)
        total_ref[:, there] = mass_ref[:, there] + unpack(more[half:, :], half)
    tail = pack(total_ref[...], width)
    for start, more in ((0, top_ref), (half, end_ref)):

        def add(here):
            there = pl.ds(start + here.start, here.size)
            for k, out_ref in zip((3, 2, 1, 0), (*part_refs, keep_ref)):
                lanes = pl.ds(k * width, width)
                value = own_ref[there, lanes] + more[here, lanes].astype(F32)
                out_ref[there, :] = value.astype(out_ref.dtype)

        steps_of(half, 128, add)
    for out_ref in part_refs:
        out_ref[rows:, :] = tail


def sum_call(own, mass, *received):
    rows, depth = own.shape
    width = depth // 4
    part = jax.ShapeDtypeStruct((rows + TAIL, width), BF16)
    out_shape = [
        jax.ShapeDtypeStruct((rows, width), F32),
        jax.ShapeDtypeStruct((1, rows), F32),
        part, part, part,
    ]
    return in_vmem(sum_kernel, "sum_s", out_shape, 2 * rows * depth, own, mass, *received)


def finish_kernel(keep_ref, total_ref, *refs):
    part_refs, out_ref, mass_ref = refs[:-2], refs[-2], refs[-1]
    mass = total_ref[...]
    for part in part_refs:
        mass = mass + unpack(part[keep_ref.shape[0] :, :], keep_ref.shape[0])
    mass_ref[...] = mass

    def divide(rows):
        value = keep_ref[rows, :]
        for part in part_refs:
            value = value + part[rows, :].astype(F32)
        out_ref[rows, :] = value / to_sublanes(mass_ref[:, rows])

    steps_of(keep_ref.shape[0], 128, divide)


def finish_call(keep, mass, parts):
    out_shape = [jax.ShapeDtypeStruct(keep.shape, F32), jax.ShapeDtypeStruct(mass.shape, F32)]
    return in_vmem(finish_kernel, "finish", out_shape, 4 * keep.size, keep, mass, *parts)[0]


def own_kernel(spot_ref, *refs):
    lat_refs, (plan_ref, mass_ref, top_ref, end_ref) = refs[:8], refs[8:12]
    out_ref, total_ref, lat_buf, sem = refs[12:]
    half = plan_ref.shape[0] // 2
    fetch(0, spot_ref, lat_refs, lat_buf, sem)
    arrive(lat_buf, sem)
    for rows, more in ((pl.ds(0, half), top_ref), (pl.ds(half, half), end_ref)):
        multiply_into(out_ref.at[rows, :], plan_ref, rows, lat_buf, more)
        total_ref[:, rows] = mass_ref[:, rows] + unpack(more[half:, :], half)


def own_call(spots, lat, plan, mass, top, end):
    rows, cols = plan.shape
    depth = 2 * lat[0].shape[1]
    return lat_call(
        own_kernel,
        "own",
        [jax.ShapeDtypeStruct((rows, depth), F32), jax.ShapeDtypeStruct((1, rows), F32)],
        2 * rows * cols * depth,
        spots, lat, [pltpu.VMEM((cols, depth), BF16), pltpu.SemaphoreType.DMA],
        plan, mass, top, end,
    )


def on_device(noise, latents):
    width = latents.shape[1] * lax.axis_size("row")
    noise_count = noise.shape[0] * lax.axis_size("row")
    latent_count = latents.shape[0] * lax.axis_size("col")
    line, near, far, pieces = gather(noise, latents)
    spots = latent_spots()
    cross, last = near_call(spots, line, near, pieces)
    logits, lse = far_call(far, last, cross, 2.0 / (width * EPSILON) * LOG2E)
    for step in range(ITERS):
        if step:
            lse = row_call(logits, colpot)
        rowpot = -math.log2(noise_count) - over_col(lse, logadd)
        colpot = -math.log2(latent_count) - over_row(col_call(logits, rowpot), logadd)
    plan, mass, far_top, far_end = plan_call(logits, rowpot, colpot, last)
    transported, rowpot, colpot = scatter_sum(
        plan, spots, pieces, far_top, far_end, mass, rowpot, colpot
    )
    return (transported, rowpot.reshape(-1), colpot.reshape(-1))


def solution(mesh):
    in_specs = (P("row", "col"), P("col", "row"))
    out_specs = (P("row", "col"), P("row"), P("col"))
    return jax.shard_map(
        on_device, mesh=mesh, in_specs=in_specs, out_specs=out_specs, check_vma=False
    )
```

profile of v0, /device:TPU:54, one launch (start us, length us, event | category | flops | bytes accessed | tf_op | source)
XLA Modules:
  0.0 219.6 jit_solution(4738112728484713527)
XLA Ops:
  0.6 1.4 collective-permute-start.6
  2.1 1.9 collective-permute-start.1
  4.0 4.2 %collective-permute-start.2 = (bf16[1024,256]{1,0:T(8,128)(2,1)}, bf16[1024,256]{1,0:T(8,128)(2,1)S(1)}, u32[]{:S(2)}, u32[]{:S(2)}) collective-permute-start(bf16[1024,256]{1,0:T(8,128)(2,1)} %refs_0_.5), channel_id=1, source_target_pairs={{0,2},{1,3},{2,0},{3,1},{4,6},{5,7},{6,4},{7,5},{8,10},{9,11},{10,... | collective-permute-start | bytes 1572872 | tf_op jit(solution)/shard_map/ppermute | solution.py:85
  9.0 2.4 %collective-permute-done.refs_1_ = bf16[1024,256]{1,0:T(8,128)(2,1)S(1)} collective-permute-done((bf16[1024,256]{1,0:T(8,128)(2,1)}, bf16[1024,256]{1,0:T(8,128)(2,1)S(1)}, u32[]{:S(2)}, u32[]{:S(2)}) %collective-permute-start) | collective-permute-done | bytes 524320 | tf_op jit(solution)/shard_map/ppermute | solution.py:85
  11.4 2.2 collective-permute-done.1.refs_2_
  13.5 4.8 %collective-permute-done.2.refs_3_ = bf16[1024,256]{1,0:T(8,128)(2,1)S(1)} collective-permute-done((bf16[1024,256]{1,0:T(8,128)(2,1)}, bf16[1024,256]{1,0:T(8,128)(2,1)S(1)}, u32[]{:S(2)}, u32[]{:S(2)}) %collective-permute-start.2) | collective-permute-done | bytes 524320 | tf_op jit(solution)/shard_map/ppermute | solution.py:85
  19.4 1.5 halves.1
  21.4 1.5 collective-permute-start.8
  23.0 2.2 collective-permute-done.6.refs_10_.refs_2_
  26.3 9.7 %collective-permute-done.7 = bf16[2048,256]{1,0:T(8,128)(2,1)S(1)} collective-permute-done((bf16[2048,256]{1,0:T(8,128)(2,1)}, bf16[2048,256]{1,0:T(8,128)(2,1)S(1)}, u32[]{:S(2)}, u32[]{:S(2)}) %collective-permute-start.7) | collective-permute-done | bytes 1048608 | tf_op jit(solution)/shard_map/ppermute | solution.py:89
  40.5 6.8 %collective-permute-done.3 = bf16[2048,256]{1,0:T(8,128)(2,1)} collective-permute-done((bf16[2048,256]{1,0:T(8,128)(2,1)}, bf16[2048,256]{1,0:T(8,128)(2,1)}, u32[]{:S(2)}, u32[]{:S(2)}) %collective-permute-start.3) | collective-permute-done | bytes 1048608 | tf_op jit(solution)/shard_map/ppermute | solution.py:89
  47.3 5.0 %collective-permute-done.4 = bf16[2048,256]{1,0:T(8,128)(2,1)} collective-permute-done((bf16[2048,256]{1,0:T(8,128)(2,1)}, bf16[2048,256]{1,0:T(8,128)(2,1)}, u32[]{:S(2)}, u32[]{:S(2)}) %collective-permute-start.4) | collective-permute-done | bytes 1048608 | tf_op jit(solution)/shard_map/ppermute | solution.py:89
  52.8 1.5 collective-permute-start.15
  55.6 10.2 %cross_near.1 = (f32[1024,1024]{1,0:T(8,128)S(1)}, bf16[1024,1024]{1,0:T(8,128)(2,1)S(1)}) custom-call(s32[16]{0:T(128)S(1)} %fusion.6.spot_ref, bf16[1024,256]{1,0:T(8,128)(2,1)} %refs_0_.5, bf16[1024,256]{1,0:T(8,128)(2,1)} %copy-done.10, bf16[1024,256]{1,0:T(8,128)(2,1)} %copy-done.11, bf16[1024,256]{1,0:T(8,128)(2,1)} %copy-done.12, ...), custom_call_target="tpu_custom_call" | custom-call | flops 25769803776 | bytes 18874368 | tf_op jit(solution)/shard_map/cross_near/pallas_call | solution.py:326
  65.8 1.5 collective-permute-done.14
  67.3 1.7 collective-permute-done.15
  69.0 4.2 %cross_far.1 = (f32[1024,1024]{1,0:T(8,128)S(1)}, f32[1,1024]{1,0:T(1,128)S(1)}) custom-call(bf16[4,512,256]{2,1,0:T(8,128)(2,1)S(1)} %bitcast.16, bf16[4,512,256]{2,1,0:T(8,128)(2,1)S(1)} %bitcast.17, bf16[1024,1024]{1,0:T(8,128)(2,1)S(1)} %get-tuple-element.53.lat_ref, f32[1024,1024]{1,0:T(8,128)S(1)} %get-tuple-element.54.cross_ref), custom_call_target="tpu_custom_call" | custom-call | flops 2147483648 | bytes 8388608 | tf_op jit(solution)/shard_map/cross_far/pallas_call | solution.py:460
  74.5 2.3 %collective-permute-start.18 = (f32[2,1024]{1,0:T(2,128)S(1)}, f32[2,1024]{1,0:T(2,128)S(1)}, u32[]{:S(2)}, u32[]{:S(2)}) collective-permute-start(f32[2,1024]{1,0:T(2,128)S(1)} %pad_maximum_fusion), channel_id=1, source_target_pairs={{0,1},{1,2},{2,3},{3,0},{4,5},{5,6},{6,7},{7,4},{8,9},{9,10},{10,1... | collective-permute-start | bytes 24584 | tf_op jit(solution)/shard_map/ppermute | solution.py:61
  76.8 4.0 %collective-permute-start.17 = (f32[2,1024]{1,0:T(2,128)S(1)}, f32[2,1024]{1,0:T(2,128)S(1)}, u32[]{:S(2)}, u32[]{:S(2)}) collective-permute-start(f32[2,1024]{1,0:T(2,128)S(1)} %pad_maximum_fusion), channel_id=1, source_target_pairs={{0,2},{1,3},{2,0},{3,1},{4,6},{5,7},{6,4},{7,5},{8,10},{9,11},{10,... | collective-permute-start | bytes 24584 | tf_op jit(solution)/shard_map/ppermute | solution.py:60
  80.8 1.6 collective-permute-done.17
  82.6 2.4 %collective-permute-start.20 = (f32[2,1024]{1,0:T(2,128)S(1)}, f32[2,1024]{1,0:T(2,128)S(1)}, u32[]{:S(2)}, u32[]{:S(2)}) collective-permute-start(f32[2,1024]{1,0:T(2,128)S(1)} %multiply_add_fusion.5), channel_id=1, source_target_pairs={{0,8},{1,9},{2,10},{3,11},{4,12},{5,13},{6,14},{7,15},{8,0},{9,1},... | collective-permute-start | bytes 24584 | tf_op jit(solution)/shard_map/ppermute | solution.py:60
  85.0 1.2 collective-permute-done.21
  86.5 1.3 collective-permute-done.20
  87.9 1.7 col_lse.3
  91.1 2.0 collective-permute-start.24
  93.1 1.4 collective-permute-done.25
  94.5 1.7 collective-permute-done.24
  96.3 1.7 row_lse.2
  100.4 3.3 %collective-permute-start.28 = (f32[2,1024]{1,0:T(2,128)S(1)}, f32[2,1024]{1,0:T(2,128)S(1)}, u32[]{:S(2)}, u32[]{:S(2)}) collective-permute-start(f32[2,1024]{1,0:T(2,128)S(1)} %pad_maximum_fusion.1), channel_id=1, source_target_pairs={{0,2},{1,3},{2,0},{3,1},{4,6},{5,7},{6,4},{7,5},{8,10},{9,11},{10,... | collective-permute-start | bytes 24584 | tf_op jit(solution)/shard_map/ppermute | solution.py:60
  103.7 1.8 collective-permute-done.28
  105.6 1.4 collective-permute-start.32
  107.0 2.7 %collective-permute-start.31 = (f32[2,1024]{1,0:T(2,128)S(1)}, f32[2,1024]{1,0:T(2,128)S(1)}, u32[]{:S(2)}, u32[]{:S(2)}) collective-permute-start(f32[2,1024]{1,0:T(2,128)S(1)} %multiply_add_fusion.3), channel_id=1, source_target_pairs={{0,8},{1,9},{2,10},{3,11},{4,12},{5,13},{6,14},{7,15},{8,0},{9,1},... | collective-permute-start | bytes 24584 | tf_op jit(solution)/shard_map/ppermute | solution.py:60
  109.7 2.5 %collective-permute-done.31 = f32[2,1024]{1,0:T(2,128)S(1)} collective-permute-done((f32[2,1024]{1,0:T(2,128)S(1)}, f32[2,1024]{1,0:T(2,128)S(1)}, u32[]{:S(2)}, u32[]{:S(2)}) %collective-permute-start.31) | collective-permute-done | bytes 8224 | tf_op jit(solution)/shard_map/ppermute | solution.py:60
  112.2 1.7 col_lse.4
  115.2 1.6 collective-permute-start.36
  116.8 1.7 collective-permute-start.35
  118.8 3.1 %collective-permute-done.35 = f32[1,1024]{1,0:T(1,128)S(1)} collective-permute-done((f32[1,1024]{1,0:T(1,128)S(1)}, f32[1,1024]{1,0:T(1,128)S(1)}, u32[]{:S(2)}, u32[]{:S(2)}) %collective-permute-start.35) | collective-permute-done | bytes 4128 | tf_op jit(solution)/shard_map/ppermute | solution.py:60
  122.0 1.7 row_lse.3
  124.9 2.9 %collective-permute-start.40 = (f32[2,1024]{1,0:T(2,128)S(1)}, f32[2,1024]{1,0:T(2,128)S(1)}, u32[]{:S(2)}, u32[]{:S(2)}) collective-permute-start(f32[2,1024]{1,0:T(2,128)S(1)} %pad_maximum_fusion.2), channel_id=1, source_target_pairs={{0,1},{1,2},{2,3},{3,0},{4,5},{5,6},{6,7},{7,4},{8,9},{9,10},{10,1... | collective-permute-start | bytes 24584 | tf_op jit(solution)/shard_map/ppermute | solution.py:61
  127.8 1.6 collective-permute-start.39
  129.4 3.6 %collective-permute-done.39 = f32[2,1024]{1,0:T(2,128)S(1)} collective-permute-done((f32[2,1024]{1,0:T(2,128)S(1)}, f32[2,1024]{1,0:T(2,128)S(1)}, u32[]{:S(2)}, u32[]{:S(2)}) %collective-permute-start.39) | collective-permute-done | bytes 8224 | tf_op jit(solution)/shard_map/ppermute | solution.py:60
  133.0 1.8 collective-permute-start.43
  134.8 1.2 collective-permute-start.42
  136.8 3.2 %collective-permute-done.42 = f32[2,1024]{1,0:T(2,128)S(1)} collective-permute-done((f32[2,1024]{1,0:T(2,128)S(1)}, f32[2,1024]{1,0:T(2,128)S(1)}, u32[]{:S(2)}, u32[]{:S(2)}) %collective-permute-start.42) | collective-permute-done | bytes 8224 | tf_op jit(solution)/shard_map/ppermute | solution.py:60
  140.0 1.7 col_lse.5
  143.0 1.7 collective-permute-start.47
  145.0 1.7 collective-permute-done.47
  146.7 3.1 %collective-permute-done.46 = f32[1,1024]{1,0:T(1,128)S(1)} collective-permute-done((f32[1,1024]{1,0:T(1,128)S(1)}, f32[1,1024]{1,0:T(1,128)S(1)}, u32[]{:S(2)}, u32[]{:S(2)}) %collective-permute-start.46) | collective-permute-done | bytes 4128 | tf_op jit(solution)/shard_map/ppermute | solution.py:60
  149.8 3.8 %plan.1 = (bf16[1024,1024]{1,0:T(8,128)(2,1)S(1)}, f32[1,1024]{1,0:T(1,128)S(1)}, bf16[528,1024]{1,0:T(8,128)(2,1)S(1)}, bf16[528,1024]{1,0:T(8,128)(2,1)S(1)}) custom-call(f32[1024,1024]{1,0:T(8,128)S(1)} %get-tuple-element.55.logits_ref, f32[1,1024]{1,0:T(1,128)S(1)} %fusion.2.rowpot_ref, f32[1,1024]{1,0:T(1,128)S(1)} %add_subtract_fusion.colpot_ref, ...), custom_call_target="tpu_custom_call" | custom-call | flops 2147483648 | bytes 6299648 | tf_op jit(solution)/shard_map/plan/pallas_call | solution.py:460
  153.6 2.0 collective-permute-start.49
  155.9 5.1 %share.1 = (bf16[528,1024]{1,0:T(8,128)(2,1)S(1)}, bf16[528,1024]{1,0:T(8,128)(2,1)S(1)}, bf16[1024,1024]{1,0:T(8,128)(2,1)S(1)}, bf16[1024,1024]{1,0:T(8,128)(2,1)S(1)}) custom-call(s32[16]{0:T(128)S(1)} %fusion.6.spot_ref, bf16[1024,512]{1,0:T(8,128)(2,1)S(1)} %copy-done.1, bf16[1024,512]{1,0:T(8,128)(2,1)S(1)} %copy-done.8, ...), custom_call_target="tpu_custom_call" | custom-call | flops 2147483648 | bytes 2101248 | tf_op jit(solution)/shard_map/share/pallas_call | solution.py:492
  161.1 3.2 %collective-permute-start.52 = (bf16[528,1024]{1,0:T(8,128)(2,1)S(1)}, bf16[528,1024]{1,0:T(8,128)(2,1)S(1)}, u32[]{:S(2)}, u32[]{:S(2)}) collective-permute-start(bf16[528,1024]{1,0:T(8,128)(2,1)S(1)} %get-tuple-element.67), channel_id=1, source_target_pairs={{0,4},{1,5},{2,6},{3,7},{4,8},{5,9},{6,10},{7,11},{8,12},{9,13},{1... | collective-permute-start | bytes 3244040 | tf_op jit(solution)/shard_map/ppermute | solution.py:89
  164.4 4.7 %collective-permute-done.49.top_more = bf16[528,1024]{1,0:T(8,128)(2,1)S(1)} collective-permute-done((bf16[528,1024]{1,0:T(8,128)(2,1)S(1)}, bf16[528,1024]{1,0:T(8,128)(2,1)S(1)}, u32[]{:S(2)}, u32[]{:S(2)}) %collective-permute-start.49) | collective-permute-done | bytes 1081376 | tf_op jit(solution)/shard_map/ppermute | solution.py:89
  169.0 2.9 %collective-permute-done.50.end_more = bf16[528,1024]{1,0:T(8,128)(2,1)S(1)} collective-permute-done((bf16[528,1024]{1,0:T(8,128)(2,1)S(1)}, bf16[528,1024]{1,0:T(8,128)(2,1)S(1)}, u32[]{:S(2)}, u32[]{:S(2)}) %collective-permute-start.50) | collective-permute-done | bytes 1081376 | tf_op jit(solution)/shard_map/ppermute | solution.py:89
  171.9 2.9 %onward.1 = (bf16[528,1024]{1,0:T(8,128)(2,1)S(1)}, bf16[528,1024]{1,0:T(8,128)(2,1)S(1)}) custom-call(bf16[1024,1024]{1,0:T(8,128)(2,1)S(1)} %get-tuple-element.65.refs_8_.plan_ref, bf16[1024,1024]{1,0:T(8,128)(2,1)S(1)} %get-tuple-element.59.after_ref, bf16[1024,1024]{1,0:T(8,128)(2,1)S(1)} %get-tuple-element.60.before_ref, ...), custom_call_target="tpu_custom_call" | custom-call | flops 2147483648 | bytes 8458240 | tf_op jit(solution)/shard_map/onward/pallas_call | solution.py:460
  174.9 2.0 collective-permute-start.54
  176.9 6.6 %collective-permute-done.51.refs_10_ = bf16[528,1024]{1,0:T(8,128)(2,1)S(1)} collective-permute-done((bf16[528,1024]{1,0:T(8,128)(2,1)S(1)}, bf16[528,1024]{1,0:T(8,128)(2,1)S(1)}, u32[]{:S(2)}, u32[]{:S(2)}) %collective-permute-start.51) | collective-permute-done | bytes 1081376 | tf_op jit(solution)/shard_map/ppermute | solution.py:89
  183.5 4.7 %own.1 = (f32[1024,1024]{1,0:T(8,128)S(1)}, f32[1,1024]{1,0:T(1,128)S(1)}) custom-call(s32[16]{0:T(128)S(1)} %fusion.6.spot_ref, bf16[1024,512]{1,0:T(8,128)(2,1)S(1)} %copy-done.1, bf16[1024,512]{1,0:T(8,128)(2,1)S(1)} %copy-done.8, bf16[1024,512]{1,0:T(8,128)(2,1)S(1)} %copy-done.3, bf16[1024,512]{1,0:T(8,128)(2,1)} %collective-permute-done.10.refs_11_.refs_3_, ...), custom_call_target="tpu_custom_call" | custom-call | flops 2147483648 | bytes 4263936 | tf_op jit(solution)/shard_map/own/pallas_call | solution.py:492
  188.9 3.3 %collective-permute-done.53.top_ref = bf16[528,1024]{1,0:T(8,128)(2,1)S(1)} collective-permute-done((bf16[528,1024]{1,0:T(8,128)(2,1)S(1)}, bf16[528,1024]{1,0:T(8,128)(2,1)S(1)}, u32[]{:S(2)}, u32[]{:S(2)}) %collective-permute-start.53) | collective-permute-done | bytes 1081376 | tf_op jit(solution)/shard_map/ppermute | solution.py:89
  192.2 8.6 %collective-permute-done.54.end_ref = bf16[528,1024]{1,0:T(8,128)(2,1)S(1)} collective-permute-done((bf16[528,1024]{1,0:T(8,128)(2,1)S(1)}, bf16[528,1024]{1,0:T(8,128)(2,1)S(1)}, u32[]{:S(2)}, u32[]{:S(2)}) %collective-permute-start.54) | collective-permute-done | bytes 1081376 | tf_op jit(solution)/shard_map/ppermute | solution.py:89
  201.5 2.9 %collective-permute-start.56 = (bf16[1040,256]{1,0:T(8,128)(2,1)S(1)}, bf16[1040,256]{1,0:T(8,128)(2,1)S(1)}, u32[]{:S(2)}, u32[]{:S(2)}) collective-permute-start(bf16[1040,256]{1,0:T(8,128)(2,1)S(1)} %get-tuple-element.78), channel_id=1, source_target_pairs={{0,3},{1,0},{2,1},{3,2},{4,7},{5,4},{6,5},{7,6},{8,11},{9,8},{10,9... | collective-permute-start | bytes 1597448 | tf_op jit(solution)/shard_map/ppermute | solution.py:85
  204.4 7.9 %collective-permute-done.55.refs_0_ = bf16[1040,256]{1,0:T(8,128)(2,1)S(1)} collective-permute-done((bf16[1040,256]{1,0:T(8,128)(2,1)S(1)}, bf16[1040,256]{1,0:T(8,128)(2,1)S(1)}, u32[]{:S(2)}, u32[]{:S(2)}) %collective-permute-start.55) | collective-permute-done | bytes 532512 | tf_op jit(solution)/shard_map/ppermute | solution.py:85
  212.3 4.2 %collective-permute-done.56.refs_1_ = bf16[1040,256]{1,0:T(8,128)(2,1)S(1)} collective-permute-done((bf16[1040,256]{1,0:T(8,128)(2,1)S(1)}, bf16[1040,256]{1,0:T(8,128)(2,1)S(1)}, u32[]{:S(2)}, u32[]{:S(2)}) %collective-permute-start.56) | collective-permute-done | bytes 532512 | tf_op jit(solution)/shard_map/ppermute | solution.py:85
  217.4 1.3 finish.1
  (124 shorter events, 24.4 us)
Async XLA Ops:
  0.6 22.4 %copy-start = (bf16[1024,512]{1,0:T(8,128)(2,1)S(1)}, bf16[1024,512]{1,0:T(8,128)(2,1)}, u32[]{:S(2)}) copy-start(bf16[1024,512]{1,0:T(8,128)(2,1)} %refs_0_.7) | copy-start | bytes 3145732
  0.6 24.5 %collective-permute-start.6 = (bf16[1024,512]{1,0:T(8,128)(2,1)}, bf16[1024,512]{1,0:T(8,128)(2,1)S(1)}, u32[]{:S(2)}, u32[]{:S(2)}) collective-permute-start(bf16[1024,512]{1,0:T(8,128)(2,1)} %refs_0_.7), channel_id=1, source_target_pairs={{0,32},{16,112},{32,64},{48,16},{64,96},{80,48},{96,0},{112,80},{1... | collective-permute-start | bytes 3145736 | tf_op jit(solution)/shard_map/ppermute | solution.py:98
  2.0 9.4 %collective-permute-start = (bf16[1024,256]{1,0:T(8,128)(2,1)}, bf16[1024,256]{1,0:T(8,128)(2,1)S(1)}, u32[]{:S(2)}, u32[]{:S(2)}) collective-permute-start(bf16[1024,256]{1,0:T(8,128)(2,1)} %refs_0_.5), channel_id=1, source_target_pairs={{0,3},{1,0},{2,1},{3,2},{4,7},{5,4},{6,5},{7,6},{8,11},{9,8},{10,9... | collective-permute-start | bytes 1572872 | tf_op jit(solution)/shard_map/ppermute | solution.py:85
  2.1 11.4 %collective-permute-start.1 = (bf16[1024,256]{1,0:T(8,128)(2,1)}, bf16[1024,256]{1,0:T(8,128)(2,1)S(1)}, u32[]{:S(2)}, u32[]{:S(2)}) collective-permute-start(bf16[1024,256]{1,0:T(8,128)(2,1)} %refs_0_.5), channel_id=1, source_target_pairs={{0,1},{1,2},{2,3},{3,0},{4,5},{5,6},{6,7},{7,4},{8,9},{9,10},{10,1... | collective-permute-start | bytes 1572872 | tf_op jit(solution)/shard_map/ppermute | solution.py:85
  4.0 14.3 %collective-permute-start.2 = (bf16[1024,256]{1,0:T(8,128)(2,1)}, bf16[1024,256]{1,0:T(8,128)(2,1)S(1)}, u32[]{:S(2)}, u32[]{:S(2)}) collective-permute-start(bf16[1024,256]{1,0:T(8,128)(2,1)} %refs_0_.5), channel_id=1, source_target_pairs={{0,2},{1,3},{2,0},{3,1},{4,6},{5,7},{6,4},{7,5},{8,10},{9,11},{10,... | collective-permute-start | bytes 1572872 | tf_op jit(solution)/shard_map/ppermute | solution.py:85
  8.2 18.0 %collective-permute-start.9 = (bf16[1024,512]{1,0:T(8,128)(2,1)}, bf16[1024,512]{1,0:T(8,128)(2,1)S(1)}, u32[]{:S(2)}, u32[]{:S(2)}) collective-permute-start(bf16[1024,512]{1,0:T(8,128)(2,1)} %refs_0_.7), channel_id=1, source_target_pairs={{32,0},{112,16},{64,32},{16,48},{96,64},{48,80},{0,96},{80,112},{3... | collective-permute-start | bytes 3145736 | tf_op jit(solution)/shard_map/ppermute | solution.py:99
  11.4 28.7 %copy-start.10 = (bf16[1024,256]{1,0:T(8,128)(2,1)}, bf16[1024,256]{1,0:T(8,128)(2,1)S(1)}, u32[]{:S(2)}) copy-start(bf16[1024,256]{1,0:T(8,128)(2,1)S(1)} %collective-permute-done.refs_1_) | copy-start | bytes 1572868
  13.5 7.9 %copy-start.11 = (bf16[1024,256]{1,0:T(8,128)(2,1)}, bf16[1024,256]{1,0:T(8,128)(2,1)S(1)}, u32[]{:S(2)}) copy-start(bf16[1024,256]{1,0:T(8,128)(2,1)S(1)} %collective-permute-done.1.refs_2_) | copy-start | bytes 1572868
  19.4 20.7 %copy-start.12 = (bf16[1024,256]{1,0:T(8,128)(2,1)}, bf16[1024,256]{1,0:T(8,128)(2,1)S(1)}, u32[]{:S(2)}) copy-start(bf16[1024,256]{1,0:T(8,128)(2,1)S(1)} %collective-permute-done.2.refs_3_) | copy-start | bytes 1572868
  20.9 15.1 %collective-permute-start.7 = (bf16[2048,256]{1,0:T(8,128)(2,1)}, bf16[2048,256]{1,0:T(8,128)(2,1)S(1)}, u32[]{:S(2)}, u32[]{:S(2)}) collective-permute-start(bf16[2048,256]{1,0:T(8,128)(2,1)} %get-tuple-element.44), channel_id=1, source_target_pairs={{0,4},{1,5},{2,6},{3,7},{4,8},{5,9},{6,10},{7,11},{8,12},{9,13},{1... | collective-permute-start | bytes 3145736 | tf_op jit(solution)/shard_map/ppermute | solution.py:89
  21.4 16.2 %collective-permute-start.8 = (bf16[2048,256]{1,0:T(8,128)(2,1)}, bf16[2048,256]{1,0:T(8,128)(2,1)S(1)}, u32[]{:S(2)}, u32[]{:S(2)}) collective-permute-start(bf16[2048,256]{1,0:T(8,128)(2,1)} %get-tuple-element.43), channel_id=1, source_target_pairs={{0,12},{1,13},{2,14},{3,15},{4,0},{5,1},{6,2},{7,3},{8,4},{9,5},{1... | collective-permute-start | bytes 3145736 | tf_op jit(solution)/shard_map/ppermute | solution.py:89
  23.0 14.7 %collective-permute-start.5 = (bf16[1024,512]{1,0:T(8,128)(2,1)S(1)}, bf16[1024,512]{1,0:T(8,128)(2,1)S(1)}, u32[]{:S(2)}, u32[]{:S(2)}) collective-permute-start(bf16[1024,512]{1,0:T(8,128)(2,1)S(1)} %copy-done), channel_id=1, source_target_pairs={{0,16},{16,0},{32,48},{48,32},{64,80},{80,64},{96,112},{112,96},{1... | collective-permute-start | bytes 3145736 | tf_op jit(solution)/shard_map/ppermute | solution.py:95
  25.2 29.2 %copy-start.2 = (bf16[1024,512]{1,0:T(8,128)(2,1)}, bf16[1024,512]{1,0:T(8,128)(2,1)S(1)}, u32[]{:S(2)}) copy-start(bf16[1024,512]{1,0:T(8,128)(2,1)S(1)} %collective-permute-done.6.refs_10_.refs_2_) | copy-start | bytes 3145732
  25.2 14.9 %collective-permute-start.12 = (bf16[1024,512]{1,0:T(8,128)(2,1)S(1)}, bf16[1024,512]{1,0:T(8,128)(2,1)}, u32[]{:S(2)}, u32[]{:S(2)}) collective-permute-start(bf16[1024,512]{1,0:T(8,128)(2,1)S(1)} %collective-permute-done.6.refs_10_.refs_2_), channel_id=1, source_target_pairs={{0,32},{16,112},{32,64},{48,16},{64,96},{80,48},{96,0},{112,80},{1... | collective-permute-start | bytes 3145736 | tf_op jit(solution)/shard_map/ppermute | solution.py:104
  26.2 28.2 %copy-start.4 = (bf16[1024,512]{1,0:T(8,128)(2,1)}, bf16[1024,512]{1,0:T(8,128)(2,1)S(1)}, u32[]{:S(2)}) copy-start(bf16[1024,512]{1,0:T(8,128)(2,1)S(1)} %collective-permute-done.9.refs_12_.refs_4_) | copy-start | bytes 3145732
  26.2 21.1 %collective-permute-start.3 = (bf16[2048,256]{1,0:T(8,128)(2,1)}, bf16[2048,256]{1,0:T(8,128)(2,1)}, u32[]{:S(2)}, u32[]{:S(2)}) collective-permute-start(bf16[2048,256]{1,0:T(8,128)(2,1)} %get-tuple-element.43), channel_id=1, source_target_pairs={{0,4},{1,5},{2,6},{3,7},{4,8},{5,9},{6,10},{7,11},{8,12},{9,13},{1... | collective-permute-start | bytes 3145736 | tf_op jit(solution)/shard_map/ppermute | solution.py:89
  36.0 16.3 %collective-permute-start.4 = (bf16[2048,256]{1,0:T(8,128)(2,1)}, bf16[2048,256]{1,0:T(8,128)(2,1)}, u32[]{:S(2)}, u32[]{:S(2)}) collective-permute-start(bf16[2048,256]{1,0:T(8,128)(2,1)} %get-tuple-element.44), channel_id=1, source_target_pairs={{0,12},{1,13},{2,14},{3,15},{4,0},{5,1},{6,2},{7,3},{8,4},{9,5},{1... | collective-permute-start | bytes 3145736 | tf_op jit(solution)/shard_map/ppermute | solution.py:89
  37.7 16.7 %collective-permute-start.10 = (bf16[1024,512]{1,0:T(8,128)(2,1)S(1)}, bf16[1024,512]{1,0:T(8,128)(2,1)}, u32[]{:S(2)}, u32[]{:S(2)}) collective-permute-start(bf16[1024,512]{1,0:T(8,128)(2,1)S(1)} %collective-permute-done.6.refs_10_.refs_2_), channel_id=1, source_target_pairs={{0,16},{16,0},{32,48},{48,32},{64,80},{80,64},{96,112},{112,96},{1... | collective-permute-start | bytes 3145736 | tf_op jit(solution)/shard_map/ppermute | solution.py:95
  38.7 15.6 %collective-permute-start.11 = (bf16[1024,512]{1,0:T(8,128)(2,1)S(1)}, bf16[1024,512]{1,0:T(8,128)(2,1)S(1)}, u32[]{:S(2)}, u32[]{:S(2)}) collective-permute-start(bf16[1024,512]{1,0:T(8,128)(2,1)S(1)} %collective-permute-done.9.refs_12_.refs_4_), channel_id=1, source_target_pairs={{0,16},{16,0},{32,48},{48,32},{64,80},{80,64},{96,112},{112,96},{1... | collective-permute-start | bytes 3145736 | tf_op jit(solution)/shard_map/ppermute | solution.py:95
  40.1 14.2 %collective-permute-start.13 = (bf16[1024,512]{1,0:T(8,128)(2,1)}, bf16[1024,512]{1,0:T(8,128)(2,1)}, u32[]{:S(2)}, u32[]{:S(2)}) collective-permute-start(bf16[1024,512]{1,0:T(8,128)(2,1)} %collective-permute-done.12.refs_14_.refs_6_), channel_id=1, source_target_pairs={{0,16},{16,0},{32,48},{48,32},{64,80},{80,64},{96,112},{112,96},{1... | collective-permute-start | bytes 3145736 | tf_op jit(solution)/shard_map/ppermute | solution.py:95
  52.3 15.0 %collective-permute-start.14 = (bf16[2048,256]{1,0:T(8,128)(2,1)}, bf16[2048,256]{1,0:T(8,128)(2,1)S(1)}, u32[]{:S(2)}, u32[]{:S(2)}) collective-permute-start(bf16[2048,256]{1,0:T(8,128)(2,1)} %collective-permute-done.3), channel_id=1, source_target_pairs={{0,4},{1,5},{2,6},{3,7},{4,8},{5,9},{6,10},{7,11},{8,12},{9,13},{1... | collective-permute-start | bytes 3145736 | tf_op jit(solution)/shard_map/ppermute | solution.py:89
  52.8 16.2 %collective-permute-start.15 = (bf16[2048,256]{1,0:T(8,128)(2,1)}, bf16[2048,256]{1,0:T(8,128)(2,1)S(1)}, u32[]{:S(2)}, u32[]{:S(2)}) collective-permute-start(bf16[2048,256]{1,0:T(8,128)(2,1)} %collective-permute-done.4), channel_id=1, source_target_pairs={{0,12},{1,13},{2,14},{3,15},{4,0},{5,1},{6,2},{7,3},{8,4},{9,5},{1... | collective-permute-start | bytes 3145736 | tf_op jit(solution)/shard_map/ppermute | solution.py:89
  73.2 1.2 collective-permute-start.16
  74.5 6.3 %collective-permute-start.18 = (f32[2,1024]{1,0:T(2,128)S(1)}, f32[2,1024]{1,0:T(2,128)S(1)}, u32[]{:S(2)}, u32[]{:S(2)}) collective-permute-start(f32[2,1024]{1,0:T(2,128)S(1)} %pad_maximum_fusion), channel_id=1, source_target_pairs={{0,1},{1,2},{2,3},{3,0},{4,5},{5,6},{6,7},{7,4},{8,9},{9,10},{10,1... | collective-permute-start | bytes 24584 | tf_op jit(solution)/shard_map/ppermute | solution.py:61
  76.8 5.6 %collective-permute-start.17 = (f32[2,1024]{1,0:T(2,128)S(1)}, f32[2,1024]{1,0:T(2,128)S(1)}, u32[]{:S(2)}, u32[]{:S(2)}) collective-permute-start(f32[2,1024]{1,0:T(2,128)S(1)} %pad_maximum_fusion), channel_id=1, source_target_pairs={{0,2},{1,3},{2,0},{3,1},{4,6},{5,7},{6,4},{7,5},{8,10},{9,11},{10,... | collective-permute-start | bytes 24584 | tf_op jit(solution)/shard_map/ppermute | solution.py:60
  80.8 1.6 collective-permute-start.19
  82.5 3.7 %collective-permute-start.21 = (f32[2,1024]{1,0:T(2,128)S(1)}, f32[2,1024]{1,0:T(2,128)S(1)}, u32[]{:S(2)}, u32[]{:S(2)}) collective-permute-start(f32[2,1024]{1,0:T(2,128)S(1)} %multiply_add_fusion.5), channel_id=1, source_target_pairs={{0,4},{1,5},{2,6},{3,7},{4,8},{5,9},{6,10},{7,11},{8,12},{9,13},{1... | collective-permute-start | bytes 24584 | tf_op jit(solution)/shard_map/ppermute | solution.py:61
  82.6 5.2 %collective-permute-start.20 = (f32[2,1024]{1,0:T(2,128)S(1)}, f32[2,1024]{1,0:T(2,128)S(1)}, u32[]{:S(2)}, u32[]{:S(2)}) collective-permute-start(f32[2,1024]{1,0:T(2,128)S(1)} %multiply_add_fusion.5), channel_id=1, source_target_pairs={{0,8},{1,9},{2,10},{3,11},{4,12},{5,13},{6,14},{7,15},{8,0},{9,1},... | collective-permute-start | bytes 24584 | tf_op jit(solution)/shard_map/ppermute | solution.py:60
  86.2 1.6 collective-permute-start.22
  89.6 1.2 collective-permute-start.23
  90.8 3.7 %collective-permute-start.25 = (f32[1,1024]{1,0:T(1,128)S(1)}, f32[1,1024]{1,0:T(1,128)S(1)}, u32[]{:S(2)}, u32[]{:S(2)}) collective-permute-start(f32[1,1024]{1,0:T(1,128)S(1)} %multiply_add_fusion.8), channel_id=1, source_target_pairs={{0,32},{16,112},{32,64},{48,16},{64,96},{80,48},{96,0},{112,80},{1... | collective-permute-start | bytes 12296 | tf_op jit(solution)/shard_map/ppermute | solution.py:61
  91.1 5.1 %collective-permute-start.24 = (f32[1,1024]{1,0:T(1,128)S(1)}, f32[1,1024]{1,0:T(1,128)S(1)}, u32[]{:S(2)}, u32[]{:S(2)}) collective-permute-start(f32[1,1024]{1,0:T(1,128)S(1)} %multiply_add_fusion.8), channel_id=1, source_target_pairs={{0,64},{16,80},{32,96},{48,112},{64,0},{80,16},{96,32},{112,48},{1... | collective-permute-start | bytes 12296 | tf_op jit(solution)/shard_map/ppermute | solution.py:60
  94.5 1.7 collective-permute-start.26
  98.0 1.2 collective-permute-start.27
  99.2 4.5 %collective-permute-start.29 = (f32[2,1024]{1,0:T(2,128)S(1)}, f32[2,1024]{1,0:T(2,128)S(1)}, u32[]{:S(2)}, u32[]{:S(2)}) collective-permute-start(f32[2,1024]{1,0:T(2,128)S(1)} %pad_maximum_fusion.1), channel_id=1, source_target_pairs={{0,1},{1,2},{2,3},{3,0},{4,5},{5,6},{6,7},{7,4},{8,9},{9,10},{10,1... | collective-permute-start | bytes 24584 | tf_op jit(solution)/shard_map/ppermute | solution.py:61
  100.4 5.2 %collective-permute-start.28 = (f32[2,1024]{1,0:T(2,128)S(1)}, f32[2,1024]{1,0:T(2,128)S(1)}, u32[]{:S(2)}, u32[]{:S(2)}) collective-permute-start(f32[2,1024]{1,0:T(2,128)S(1)} %pad_maximum_fusion.1), channel_id=1, source_target_pairs={{0,2},{1,3},{2,0},{3,1},{4,6},{5,7},{6,4},{7,5},{8,10},{9,11},{10,... | collective-permute-start | bytes 24584 | tf_op jit(solution)/shard_map/ppermute | solution.py:60
  103.7 1.8 collective-permute-start.30
  105.6 4.1 %collective-permute-start.32 = (f32[2,1024]{1,0:T(2,128)S(1)}, f32[2,1024]{1,0:T(2,128)S(1)}, u32[]{:S(2)}, u32[]{:S(2)}) collective-permute-start(f32[2,1024]{1,0:T(2,128)S(1)} %multiply_add_fusion.3), channel_id=1, source_target_pairs={{0,4},{1,5},{2,6},{3,7},{4,8},{5,9},{6,10},{7,11},{8,12},{9,13},{1... | collective-permute-start | bytes 24584 | tf_op jit(solution)/shard_map/ppermute | solution.py:61
  107.0 5.2 %collective-permute-start.31 = (f32[2,1024]{1,0:T(2,128)S(1)}, f32[2,1024]{1,0:T(2,128)S(1)}, u32[]{:S(2)}, u32[]{:S(2)}) collective-permute-start(f32[2,1024]{1,0:T(2,128)S(1)} %multiply_add_fusion.3), channel_id=1, source_target_pairs={{0,8},{1,9},{2,10},{3,11},{4,12},{5,13},{6,14},{7,15},{8,0},{9,1},... | collective-permute-start | bytes 24584 | tf_op jit(solution)/shard_map/ppermute | solution.py:60
  109.7 2.5 %collective-permute-start.33 = (f32[2,1024]{1,0:T(2,128)S(1)}, f32[2,1024]{1,0:T(2,128)S(1)}, u32[]{:S(2)}, u32[]{:S(2)}) collective-permute-start(f32[2,1024]{1,0:T(2,128)S(1)} %collective-permute-done.32), channel_id=1, source_target_pairs={{0,16},{16,0},{32,48},{48,32},{64,80},{80,64},{96,112},{112,96},{1... | collective-permute-start | bytes 24584 | tf_op jit(solution)/shard_map/ppermute | solution.py:62
  113.9 1.2 collective-permute-start.34
  115.2 3.7 %collective-permute-start.36 = (f32[1,1024]{1,0:T(1,128)S(1)}, f32[1,1024]{1,0:T(1,128)S(1)}, u32[]{:S(2)}, u32[]{:S(2)}) collective-permute-start(f32[1,1024]{1,0:T(1,128)S(1)} %multiply_add_fusion.7), channel_id=1, source_target_pairs={{0,32},{16,112},{32,64},{48,16},{64,96},{80,48},{96,0},{112,80},{1... | collective-permute-start | bytes 12296 | tf_op jit(solution)/shard_map/ppermute | solution.py:61
  116.8 5.1 %collective-permute-start.35 = (f32[1,1024]{1,0:T(1,128)S(1)}, f32[1,1024]{1,0:T(1,128)S(1)}, u32[]{:S(2)}, u32[]{:S(2)}) collective-permute-start(f32[1,1024]{1,0:T(1,128)S(1)} %multiply_add_fusion.7), channel_id=1, source_target_pairs={{0,64},{16,80},{32,96},{48,112},{64,0},{80,16},{96,32},{112,48},{1... | collective-permute-start | bytes 12296 | tf_op jit(solution)/shard_map/ppermute | solution.py:60
  118.8 3.1 %collective-permute-start.37 = (f32[1,1024]{1,0:T(1,128)S(1)}, f32[1,1024]{1,0:T(1,128)S(1)}, u32[]{:S(2)}, u32[]{:S(2)}) collective-permute-start(f32[1,1024]{1,0:T(1,128)S(1)} %collective-permute-done.36), channel_id=1, source_target_pairs={{0,16},{16,0},{32,48},{48,32},{64,80},{80,64},{96,112},{112,96},{1... | collective-permute-start | bytes 12296 | tf_op jit(solution)/shard_map/ppermute | solution.py:62
  123.6 1.2 collective-permute-start.38
  124.9 4.5 %collective-permute-start.40 = (f32[2,1024]{1,0:T(2,128)S(1)}, f32[2,1024]{1,0:T(2,128)S(1)}, u32[]{:S(2)}, u32[]{:S(2)}) collective-permute-start(f32[2,1024]{1,0:T(2,128)S(1)} %pad_maximum_fusion.2), channel_id=1, source_target_pairs={{0,1},{1,2},{2,3},{3,0},{4,5},{5,6},{6,7},{7,4},{8,9},{9,10},{10,1... | collective-permute-start | bytes 24584 | tf_op jit(solution)/shard_map/ppermute | solution.py:61
  127.8 5.2 %collective-permute-start.39 = (f32[2,1024]{1,0:T(2,128)S(1)}, f32[2,1024]{1,0:T(2,128)S(1)}, u32[]{:S(2)}, u32[]{:S(2)}) collective-permute-start(f32[2,1024]{1,0:T(2,128)S(1)} %pad_maximum_fusion.2), channel_id=1, source_target_pairs={{0,2},{1,3},{2,0},{3,1},{4,6},{5,7},{6,4},{7,5},{8,10},{9,11},{10,... | collective-permute-start | bytes 24584 | tf_op jit(solution)/shard_map/ppermute | solution.py:60
  129.4 3.6 %collective-permute-start.41 = (f32[2,1024]{1,0:T(2,128)S(1)}, f32[2,1024]{1,0:T(2,128)S(1)}, u32[]{:S(2)}, u32[]{:S(2)}) collective-permute-start(f32[2,1024]{1,0:T(2,128)S(1)} %collective-permute-done.40), channel_id=1, source_target_pairs={{0,16},{16,0},{32,48},{48,32},{64,80},{80,64},{96,112},{112,96},{1... | collective-permute-start | bytes 24584 | tf_op jit(solution)/shard_map/ppermute | solution.py:62
  133.0 3.7 %collective-permute-start.43 = (f32[2,1024]{1,0:T(2,128)S(1)}, f32[2,1024]{1,0:T(2,128)S(1)}, u32[]{:S(2)}, u32[]{:S(2)}) collective-permute-start(f32[2,1024]{1,0:T(2,128)S(1)} %multiply_add_fusion.1), channel_id=1, source_target_pairs={{0,4},{1,5},{2,6},{3,7},{4,8},{5,9},{6,10},{7,11},{8,12},{9,13},{1... | collective-permute-start | bytes 24584 | tf_op jit(solution)/shard_map/ppermute | solution.py:61
  134.8 5.2 %collective-permute-start.42 = (f32[2,1024]{1,0:T(2,128)S(1)}, f32[2,1024]{1,0:T(2,128)S(1)}, u32[]{:S(2)}, u32[]{:S(2)}) collective-permute-start(f32[2,1024]{1,0:T(2,128)S(1)} %multiply_add_fusion.1), channel_id=1, source_target_pairs={{0,8},{1,9},{2,10},{3,11},{4,12},{5,13},{6,14},{7,15},{8,0},{9,1},... | collective-permute-start | bytes 24584 | tf_op jit(solution)/shard_map/ppermute | solution.py:60
  136.8 3.2 %collective-permute-start.44 = (f32[2,1024]{1,0:T(2,128)S(1)}, f32[2,1024]{1,0:T(2,128)S(1)}, u32[]{:S(2)}, u32[]{:S(2)}) collective-permute-start(f32[2,1024]{1,0:T(2,128)S(1)} %collective-permute-done.43), channel_id=1, source_target_pairs={{0,16},{16,0},{32,48},{48,32},{64,80},{80,64},{96,112},{112,96},{1... | collective-permute-start | bytes 24584 | tf_op jit(solution)/shard_map/ppermute | solution.py:62
  141.7 1.2 collective-permute-start.45
  143.0 3.7 %collective-permute-start.47 = (f32[1,1024]{1,0:T(1,128)S(1)}, f32[1,1024]{1,0:T(1,128)S(1)}, u32[]{:S(2)}, u32[]{:S(2)}) collective-permute-start(f32[1,1024]{1,0:T(1,128)S(1)} %multiply_add_fusion.6), channel_id=1, source_target_pairs={{0,32},{16,112},{32,64},{48,16},{64,96},{80,48},{96,0},{112,80},{1... | collective-permute-start | bytes 12296 | tf_op jit(solution)/shard_map/ppermute | solution.py:61
  144.6 5.1 %collective-permute-start.46 = (f32[1,1024]{1,0:T(1,128)S(1)}, f32[1,1024]{1,0:T(1,128)S(1)}, u32[]{:S(2)}, u32[]{:S(2)}) collective-permute-start(f32[1,1024]{1,0:T(1,128)S(1)} %multiply_add_fusion.6), channel_id=1, source_target_pairs={{0,64},{16,80},{32,96},{48,112},{64,0},{80,16},{96,32},{112,48},{1... | collective-permute-start | bytes 12296 | tf_op jit(solution)/shard_map/ppermute | solution.py:60
  146.7 3.1 %collective-permute-start.48 = (f32[1,1024]{1,0:T(1,128)S(1)}, f32[1,1024]{1,0:T(1,128)S(1)}, u32[]{:S(2)}, u32[]{:S(2)}) collective-permute-start(f32[1,1024]{1,0:T(1,128)S(1)} %collective-permute-done.47), channel_id=1, source_target_pairs={{0,16},{16,0},{32,48},{48,32},{64,80},{80,64},{96,112},{112,96},{1... | collective-permute-start | bytes 12296 | tf_op jit(solution)/shard_map/ppermute | solution.py:62
  153.6 15.4 %collective-permute-start.49 = (bf16[528,1024]{1,0:T(8,128)(2,1)S(1)}, bf16[528,1024]{1,0:T(8,128)(2,1)S(1)}, u32[]{:S(2)}, u32[]{:S(2)}) collective-permute-start(bf16[528,1024]{1,0:T(8,128)(2,1)S(1)} %get-tuple-element.61), channel_id=1, source_target_pairs={{0,4},{1,5},{2,6},{3,7},{4,8},{5,9},{6,10},{7,11},{8,12},{9,13},{1... | collective-permute-start | bytes 3244040 | tf_op jit(solution)/shard_map/ppermute | solution.py:89
  155.6 16.4 %collective-permute-start.50 = (bf16[528,1024]{1,0:T(8,128)(2,1)S(1)}, bf16[528,1024]{1,0:T(8,128)(2,1)S(1)}, u32[]{:S(2)}, u32[]{:S(2)}) collective-permute-start(bf16[528,1024]{1,0:T(8,128)(2,1)S(1)} %get-tuple-element.62), channel_id=1, source_target_pairs={{0,12},{1,13},{2,14},{3,15},{4,0},{5,1},{6,2},{7,3},{8,4},{9,5},{1... | collective-permute-start | bytes 3244040 | tf_op jit(solution)/shard_map/ppermute | solution.py:89
  161.1 22.5 %collective-permute-start.51 = (bf16[528,1024]{1,0:T(8,128)(2,1)S(1)}, bf16[528,1024]{1,0:T(8,128)(2,1)S(1)}, u32[]{:S(2)}, u32[]{:S(2)}) collective-permute-start(bf16[528,1024]{1,0:T(8,128)(2,1)S(1)} %get-tuple-element.66), channel_id=1, source_target_pairs={{0,12},{1,13},{2,14},{3,15},{4,0},{5,1},{6,2},{7,3},{8,4},{9,5},{1... | collective-permute-start | bytes 3244040 | tf_op jit(solution)/shard_map/ppermute | solution.py:89
  161.1 22.4 %collective-permute-start.52 = (bf16[528,1024]{1,0:T(8,128)(2,1)S(1)}, bf16[528,1024]{1,0:T(8,128)(2,1)S(1)}, u32[]{:S(2)}, u32[]{:S(2)}) collective-permute-start(bf16[528,1024]{1,0:T(8,128)(2,1)S(1)} %get-tuple-element.67), channel_id=1, source_target_pairs={{0,4},{1,5},{2,6},{3,7},{4,8},{5,9},{6,10},{7,11},{8,12},{9,13},{1... | collective-permute-start | bytes 3244040 | tf_op jit(solution)/shard_map/ppermute | solution.py:89
  174.8 17.4 %collective-permute-start.53 = (bf16[528,1024]{1,0:T(8,128)(2,1)S(1)}, bf16[528,1024]{1,0:T(8,128)(2,1)S(1)}, u32[]{:S(2)}, u32[]{:S(2)}) collective-permute-start(bf16[528,1024]{1,0:T(8,128)(2,1)S(1)} %get-tuple-element.63), channel_id=1, source_target_pairs={{0,4},{1,5},{2,6},{3,7},{4,8},{5,9},{6,10},{7,11},{8,12},{9,13},{1... | collective-permute-start | bytes 3244040 | tf_op jit(solution)/shard_map/ppermute | solution.py:89
  174.9 25.9 %collective-permute-start.54 = (bf16[528,1024]{1,0:T(8,128)(2,1)S(1)}, bf16[528,1024]{1,0:T(8,128)(2,1)S(1)}, u32[]{:S(2)}, u32[]{:S(2)}) collective-permute-start(bf16[528,1024]{1,0:T(8,128)(2,1)S(1)} %get-tuple-element.64), channel_id=1, source_target_pairs={{0,12},{1,13},{2,14},{3,15},{4,0},{5,1},{6,2},{7,3},{8,4},{9,5},{1... | collective-permute-start | bytes 3244040 | tf_op jit(solution)/shard_map/ppermute | solution.py:89
  201.4 11.0 %collective-permute-start.55 = (bf16[1040,256]{1,0:T(8,128)(2,1)S(1)}, bf16[1040,256]{1,0:T(8,128)(2,1)S(1)}, u32[]{:S(2)}, u32[]{:S(2)}) collective-permute-start(bf16[1040,256]{1,0:T(8,128)(2,1)S(1)} %get-tuple-element.77), channel_id=1, source_target_pairs={{0,2},{1,3},{2,0},{3,1},{4,6},{5,7},{6,4},{7,5},{8,10},{9,11},{10,... | collective-permute-start | bytes 1597448 | tf_op jit(solution)/shard_map/ppermute | solution.py:85
  201.5 15.0 %collective-permute-start.56 = (bf16[1040,256]{1,0:T(8,128)(2,1)S(1)}, bf16[1040,256]{1,0:T(8,128)(2,1)S(1)}, u32[]{:S(2)}, u32[]{:S(2)}) collective-permute-start(bf16[1040,256]{1,0:T(8,128)(2,1)S(1)} %get-tuple-element.78), channel_id=1, source_target_pairs={{0,3},{1,0},{2,1},{3,2},{4,7},{5,4},{6,5},{7,6},{8,11},{9,8},{10,9... | collective-permute-start | bytes 1597448 | tf_op jit(solution)/shard_map/ppermute | solution.py:85
  204.4 13.0 %collective-permute-start.57 = (bf16[1040,256]{1,0:T(8,128)(2,1)S(1)}, bf16[1040,256]{1,0:T(8,128)(2,1)S(1)}, u32[]{:S(2)}, u32[]{:S(2)}) collective-permute-start(bf16[1040,256]{1,0:T(8,128)(2,1)S(1)} %get-tuple-element.79), channel_id=1, source_target_pairs={{0,1},{1,2},{2,3},{3,0},{4,5},{5,6},{6,7},{7,4},{8,9},{9,10},{10,1... | collective-permute-start | bytes 1597448 | tf_op jit(solution)/shard_map/ppermute | solution.py:85
  (9 other events, 34.4 us)
where the time goes:
time: 220 us
  waiting for transfers between devices  111 us (50%)
  starting transfers between devices  58.8 us (27%)
  Pallas kernels  42.6 us (19%)
  local copies, waits for them, and re-layouts  3.55 us (2%)
    ppermute x12, waiting for transfers between devices, hop_s(): return lax.ppermute(value, BOTH, everywhere([shift_x(by), shift_z(by)]))  51.6 us
    ppermute x6, waiting for transfers between devices, hop_f(): return lax.ppermute(value, BOTH, everywhere([shift_z(by), shift_x(by)]))  22.4 us
    ppermute x9, waiting for transfers between devices, around(): far = lax.ppermute(value, axis, opposite)  22 us
    pallas_call x10, Pallas kernels, in_vmem(): pl.pallas_call(kernel, in_specs=[pl.BlockSpec(memory_space=pltpu.VMEM)] *...  21 us
    ppermute x9, starting transfers between devices, around(): far = lax.ppermute(value, axis, opposite)  19.2 us
    ppermute x9, starting transfers between devices, around(): near = lax.ppermute(value, axis, spread)  13.2 us
    ppermute x12, starting transfers between devices, hop_s(): return lax.ppermute(value, BOTH, everywhere([shift_x(by), shift_z(by)]))  12.8 us
    pallas_call x1, Pallas kernels, near_call(): pl.pallas_call(near_kernel, in_specs=[pl.BlockSpec(memory_space=pltpu.SME...  10.2 us
  transfers between devices with their start and end apart: 58, of which 39 were waited for; matrix products, arithmetic and copies ran while one was open for 0% of the time, Pallas kernels for 11%

commit v1 on v0

--- a/solution.py
+++ b/solution.py
@@ -94,20 +94,21 @@
     half = rows // 2
     swap = lambda v: lax.ppermute(v, "row", swap_core())
     opposite = hop_f(noise, 2)
-    line = [noise, hop_f(noise, -1), hop_f(noise, 1), opposite]
+    after, before, opposite, other = lax.optimization_barrier(
+        (hop_f(noise, -1), hop_f(noise, 1), opposite, swap(latents))
+    )
+    line = [noise, after, before, opposite]
     near = lax.ppermute(latents, "row", spread_y())
     away = lax.ppermute(latents, "row", [(b, a) for a, b in spread_y()])
     top, end = halves_call(line)
-    after, _, _ = lax.optimization_barrier((near, top, end))
+    ready, _, _ = lax.optimization_barrier((near, top, end))
+    far = lax.ppermute(ready, "row", spread_y())
     top_m, end_p = hop_s(top, 1), hop_s(end, -1)
     end_m, top_p = hop_s(end, 1), hop_s(top, -1)
-    far = lax.ppermute(after, "row", spread_y())
-    first, last, other = lax.optimization_barrier((top_m, end_p, swap(latents)))
-    top_far, end_far = hop_s(first, 1), hop_s(last, -1)
-    end_m, top_p, here, there = lax.optimization_barrier((end_m, top_p, near, away))
-    near_other, away_other = swap(here), swap(there)
+    top_far, end_far = hop_s(top_m, 1), hop_s(end_p, -1)
+    near_other, away_other, far_other = map(swap, lax.optimization_barrier((near, away, far)))
     split = lambda v: v.reshape(4, half, width)
-    lat = [latents, other, near, near_other, away, away_other, far, swap(far)]
+    lat = [latents, other, near, near_other, away, away_other, far, far_other]
     return (
         line,
         [split(v) for v in (top_p, end_p, top_m, end_m)],
@@ -145,7 +146,7 @@
     own, top_m, end_p, rowpot, colpot = barrier((own, top_m, end_p, rowpot, colpot))
     keep, mass, *parts = sum_call(own, mass, top_m, end_p)
     parts = [hop_f(v, ORDER[k]) for v, k in zip(parts, (3, 2, 1))]
-    return finish_call(keep, mass, parts).astype(BF16), rowpot, colpot
+    return finish_call(keep, mass, parts), rowpot, colpot
 
 
 def steps_of(total, step, body):
@@ -351,16 +352,13 @@
 def far_kernel(scale, top_ref, end_ref, lat_ref, cross_ref, logits_ref, lse_ref):
     half = top_ref.shape[1]
 
-    def multiply(lanes):
-        for start, part_ref in ((0, top_ref), (half, end_ref)):
-            rows = pl.ds(start, half)
-            noise = jnp.concatenate([part_ref[k] for k in range(4)], axis=1)
-            cross = lax.dot_general(
-                noise, lat_ref[lanes, :], (((1,), (1,)), ((), ())), preferred_element_type=F32
-            )
-            logits_ref[rows, lanes] = (cross_ref[rows, lanes] + cross) * scale
-
-    steps_of(lat_ref.shape[0], WIDE, multiply)
+    for start, part_ref in ((0, top_ref), (half, end_ref)):
+        rows = pl.ds(start, half)
+        noise = jnp.concatenate([part_ref[k] for k in range(4)], axis=1)
+        cross = lax.dot_general(
+            noise, lat_ref[...], (((1,), (1,)), ((), ())), preferred_element_type=F32
+        )
+        logits_ref[rows, :] = (cross_ref[rows, :] + cross) * scale
     steps_of(logits_ref.shape[0], 256, lambda rows: row_lse_block(logits_ref, rows, 0.0, lse_ref))
 
 
@@ -584,23 +582,22 @@
 
 
 def finish_kernel(keep_ref, total_ref, *refs):
-    part_refs, out_ref, mass_ref = refs[:-2], refs[-2], refs[-1]
+    part_refs, out_ref = refs[:-1], refs[-1]
+    rows = keep_ref.shape[0]
     mass = total_ref[...]
     for part in part_refs:
-        mass = mass + unpack(part[keep_ref.shape[0] :, :], keep_ref.shape[0])
-    mass_ref[...] = mass
-
-    def divide(rows):
-        value = keep_ref[rows, :]
+        mass = mass + unpack(part[rows:, :], rows)
+    step = 128
+    for at in range(0, rows, step):
+        there = pl.ds(at, step)
+        value = keep_ref[there, :]
         for part in part_refs:
-            value = value + part[rows, :].astype(F32)
-        out_ref[rows, :] = value / to_sublanes(mass_ref[:, rows])
-
-    steps_of(keep_ref.shape[0], 128, divide)
+            value = value + part[there, :].astype(F32)
+        out_ref[there, :] = (value / to_sublanes(mass[:, at : at + step])).astype(BF16)
 
 
 def finish_call(keep, mass, parts):
-    out_shape = [jax.ShapeDtypeStruct(keep.shape, F32), jax.ShapeDtypeStruct(mass.shape, F32)]
+    out_shape = [jax.ShapeDtypeStruct(keep.shape, BF16)]
     return in_vmem(finish_kernel, "finish", out_shape, 4 * keep.size, keep, mass, *parts)[0]
 
 

time: 220 us -> 218 us (level)
  the two profiles are of different devices: /device:TPU:54 before, /device:TPU:0 now
where the time goes in v1:
time: 218 us; the launch traced here: 217 us
  waiting for transfers between devices  100 us (46%)
  starting transfers between devices  72.1 us (33%)
  Pallas kernels  40.5 us (19%)
  local copies, waits for them, and re-layouts  2.55 us (1%)
    ppermute x12, waiting for transfers between devices, hop_s(): return lax.ppermute(value, BOTH, everywhere([shift_x(by), shift_z(by)]))  31.8 us
    ppermute x6, waiting for transfers between devices, hop_f(): return lax.ppermute(value, BOTH, everywhere([shift_z(by), shift_x(by)]))  25.8 us
    ppermute x12, starting transfers between devices, hop_s(): return lax.ppermute(value, BOTH, everywhere([shift_x(by), shift_z(by)]))  22.6 us
    ppermute x9, starting transfers between devices, around(): far = lax.ppermute(value, axis, opposite)  21.3 us
    pallas_call x10, Pallas kernels, in_vmem(): pl.pallas_call(kernel, in_specs=[pl.BlockSpec(memory_space=pltpu.VMEM)] *...  20.6 us
    ppermute x9, waiting for transfers between devices, around(): far = lax.ppermute(value, axis, opposite)  14.2 us
    ppermute x9, waiting for transfers between devices, around(): near = lax.ppermute(value, axis, spread)  12.2 us
    ppermute x9, starting transfers between devices, around(): near = lax.ppermute(value, axis, spread)  11.1 us
  transfers between devices with their start and end apart: 58, of which 40 were waited for; matrix products, arithmetic and copies ran while one was open for 0% of the time, Pallas kernels for 10%

profile of v1, /device:TPU:0, one launch (start us, length us, event | category | flops | bytes accessed | tf_op | source)
XLA Modules:
  0.0 217.5 jit_solution(16646247866117018902)
XLA Ops:
  0.7 1.7 collective-permute-start.4
  2.5 4.0 %collective-permute-start = (bf16[1024,256]{1,0:T(8,128)(2,1)}, bf16[1024,256]{1,0:T(8,128)(2,1)S(1)}, u32[]{:S(2)}, u32[]{:S(2)}) collective-permute-start(bf16[1024,256]{1,0:T(8,128)(2,1)} %refs_0_.5), channel_id=1, source_target_pairs={{0,3},{1,0},{2,1},{3,2},{4,7},{5,4},{6,5},{7,6},{8,11},{9,8},{10,9... | collective-permute-start | bytes 1572872 | tf_op jit(solution)/shard_map/ppermute | solution.py:85
  6.5 1.9 collective-permute-start.2
  8.4 10.8 %collective-permute-done.refs_1_ = bf16[1024,256]{1,0:T(8,128)(2,1)S(1)} collective-permute-done((bf16[1024,256]{1,0:T(8,128)(2,1)}, bf16[1024,256]{1,0:T(8,128)(2,1)S(1)}, u32[]{:S(2)}, u32[]{:S(2)}) %collective-permute-start) | collective-permute-done | bytes 524320 | tf_op jit(solution)/shard_map/ppermute | solution.py:85
  19.1 1.7 collective-permute-start.5
  20.8 1.9 collective-permute-done.1.refs_2_
  22.7 1.4 copy-done.5
  24.1 1.5 halves.1
  25.6 1.6 collective-permute-start.6
  27.3 2.8 %collective-permute-start.12 = (bf16[2048,256]{1,0:T(8,128)(2,1)}, bf16[2048,256]{1,0:T(8,128)(2,1)S(1)}, u32[]{:S(2)}, u32[]{:S(2)}) collective-permute-start(bf16[2048,256]{1,0:T(8,128)(2,1)} %get-tuple-element.47), channel_id=1, source_target_pairs={{0,12},{1,13},{2,14},{3,15},{4,0},{5,1},{6,2},{7,3},{8,4},{9,5},{1... | collective-permute-start | bytes 3145736 | tf_op jit(solution)/shard_map/ppermute | solution.py:89
  30.0 3.2 %collective-permute-start.14 = (bf16[2048,256]{1,0:T(8,128)(2,1)}, bf16[2048,256]{1,0:T(8,128)(2,1)}, u32[]{:S(2)}, u32[]{:S(2)}) collective-permute-start(bf16[2048,256]{1,0:T(8,128)(2,1)} %get-tuple-element.46), channel_id=1, source_target_pairs={{0,12},{1,13},{2,14},{3,15},{4,0},{5,1},{6,2},{7,3},{8,4},{9,5},{1... | collective-permute-start | bytes 3145736 | tf_op jit(solution)/shard_map/ppermute | solution.py:89
  33.3 7.6 %collective-permute-done.5.refs_12_.refs_4_ = bf16[1024,512]{1,0:T(8,128)(2,1)S(1)} collective-permute-done((bf16[1024,512]{1,0:T(8,128)(2,1)}, bf16[1024,512]{1,0:T(8,128)(2,1)S(1)}, u32[]{:S(2)}, u32[]{:S(2)}) %collective-permute-start.5) | collective-permute-done | bytes 1048608 | tf_op jit(solution)/shard_map/ppermute | solution.py:102
  40.9 4.6 %collective-permute-start.15 = (bf16[2048,256]{1,0:T(8,128)(2,1)}, bf16[2048,256]{1,0:T(8,128)(2,1)}, u32[]{:S(2)}, u32[]{:S(2)}) collective-permute-start(bf16[2048,256]{1,0:T(8,128)(2,1)} %get-tuple-element.47), channel_id=1, source_target_pairs={{0,4},{1,5},{2,6},{3,7},{4,8},{5,9},{6,10},{7,11},{8,12},{9,13},{1... | collective-permute-start | bytes 3145736 | tf_op jit(solution)/shard_map/ppermute | solution.py:89
  47.9 6.0 %collective-permute-done.14 = bf16[2048,256]{1,0:T(8,128)(2,1)} collective-permute-done((bf16[2048,256]{1,0:T(8,128)(2,1)}, bf16[2048,256]{1,0:T(8,128)(2,1)}, u32[]{:S(2)}, u32[]{:S(2)}) %collective-permute-start.14) | collective-permute-done | bytes 1048608 | tf_op jit(solution)/shard_map/ppermute | solution.py:89
  55.1 3.9 %collective-permute-done.15 = bf16[2048,256]{1,0:T(8,128)(2,1)} collective-permute-done((bf16[2048,256]{1,0:T(8,128)(2,1)}, bf16[2048,256]{1,0:T(8,128)(2,1)}, u32[]{:S(2)}, u32[]{:S(2)}) %collective-permute-start.15) | collective-permute-done | bytes 1048608 | tf_op jit(solution)/shard_map/ppermute | solution.py:89
  59.0 2.0 collective-permute-start.13
  61.1 9.9 %cross_near.1 = (f32[1024,1024]{1,0:T(8,128)S(1)}, bf16[1024,1024]{1,0:T(8,128)(2,1)S(1)}) custom-call(s32[16]{0:T(128)S(1)} %fusion.6.spot_ref, bf16[1024,256]{1,0:T(8,128)(2,1)} %refs_0_.5, bf16[1024,256]{1,0:T(8,128)(2,1)} %copy-done.6, bf16[1024,256]{1,0:T(8,128)(2,1)} %copy-done.7, bf16[1024,256]{1,0:T(8,128)(2,1)} %copy-done.8, ...), custom_call_target="tpu_custom_call" | custom-call | flops 25769803776 | bytes 18874368 | tf_op jit(solution)/shard_map/cross_near/pallas_call | solution.py:327
  71.0 3.1 %collective-permute-done.13 = bf16[2048,256]{1,0:T(8,128)(2,1)S(1)} collective-permute-done((bf16[2048,256]{1,0:T(8,128)(2,1)}, bf16[2048,256]{1,0:T(8,128)(2,1)S(1)}, u32[]{:S(2)}, u32[]{:S(2)}) %collective-permute-start.13) | collective-permute-done | bytes 1048608 | tf_op jit(solution)/shard_map/ppermute | solution.py:89
  74.0 4.0 %cross_far.1 = (f32[1024,1024]{1,0:T(8,128)S(1)}, f32[1,1024]{1,0:T(1,128)S(1)}) custom-call(bf16[4,512,256]{2,1,0:T(8,128)(2,1)S(1)} %bitcast.16, bf16[4,512,256]{2,1,0:T(8,128)(2,1)S(1)} %bitcast.17, bf16[1024,1024]{1,0:T(8,128)(2,1)S(1)} %get-tuple-element.52.lat_ref, f32[1024,1024]{1,0:T(8,128)S(1)} %get-tuple-element.53.cross_ref), custom_call_target="tpu_custom_call" | custom-call | flops 2147483648 | bytes 8388608 | tf_op jit(solution)/shard_map/cross_far/pallas_call | solution.py:458
  79.4 4.9 %collective-permute-start.17 = (f32[2,1024]{1,0:T(2,128)S(1)}, f32[2,1024]{1,0:T(2,128)S(1)}, u32[]{:S(2)}, u32[]{:S(2)}) collective-permute-start(f32[2,1024]{1,0:T(2,128)S(1)} %pad_maximum_fusion), channel_id=1, source_target_pairs={{0,2},{1,3},{2,0},{3,1},{4,6},{5,7},{6,4},{7,5},{8,10},{9,11},{10,... | collective-permute-start | bytes 24584 | tf_op jit(solution)/shard_map/ppermute | solution.py:60
  84.5 1.5 collective-permute-done.17
  86.1 1.5 collective-permute-start.21
  87.6 3.4 %collective-permute-start.20 = (f32[2,1024]{1,0:T(2,128)S(1)}, f32[2,1024]{1,0:T(2,128)S(1)}, u32[]{:S(2)}, u32[]{:S(2)}) collective-permute-start(f32[2,1024]{1,0:T(2,128)S(1)} %multiply_add_fusion.5), channel_id=1, source_target_pairs={{0,8},{1,9},{2,10},{3,11},{4,12},{5,13},{6,14},{7,15},{8,0},{9,1},... | collective-permute-start | bytes 24584 | tf_op jit(solution)/shard_map/ppermute | solution.py:60
  91.2 1.6 collective-permute-done.20
  92.8 1.7 col_lse.3
  94.5 1.3 collective-permute-start.23
  96.6 2.7 %collective-permute-start.25 = (f32[1,1024]{1,0:T(1,128)S(1)}, f32[1,1024]{1,0:T(1,128)S(1)}, u32[]{:S(2)}, u32[]{:S(2)}) collective-permute-start(f32[1,1024]{1,0:T(1,128)S(1)} %multiply_add_fusion.8), channel_id=1, source_target_pairs={{0,32},{16,112},{32,64},{48,16},{64,96},{80,48},{96,0},{112,80},{1... | collective-permute-start | bytes 12296 | tf_op jit(solution)/shard_map/ppermute | solution.py:61
  99.3 1.5 collective-permute-start.24
  101.5 2.9 %collective-permute-done.24 = f32[1,1024]{1,0:T(1,128)S(1)} collective-permute-done((f32[1,1024]{1,0:T(1,128)S(1)}, f32[1,1024]{1,0:T(1,128)S(1)}, u32[]{:S(2)}, u32[]{:S(2)}) %collective-permute-start.24) | collective-permute-done | bytes 4128 | tf_op jit(solution)/shard_map/ppermute | solution.py:60
  104.5 1.7 row_lse.2
  107.5 2.9 %collective-permute-start.28 = (f32[2,1024]{1,0:T(2,128)S(1)}, f32[2,1024]{1,0:T(2,128)S(1)}, u32[]{:S(2)}, u32[]{:S(2)}) collective-permute-start(f32[2,1024]{1,0:T(2,128)S(1)} %pad_maximum_fusion.1), channel_id=1, source_target_pairs={{0,2},{1,3},{2,0},{3,1},{4,6},{5,7},{6,4},{7,5},{8,10},{9,11},{10,... | collective-permute-start | bytes 24584 | tf_op jit(solution)/shard_map/ppermute | solution.py:60
  110.4 1.9 collective-permute-done.29
  113.6 1.3 collective-permute-start.32
  114.9 1.4 collective-permute-start.31
  116.3 2.2 %collective-permute-done.32 = f32[2,1024]{1,0:T(2,128)S(1)} collective-permute-done((f32[2,1024]{1,0:T(2,128)S(1)}, f32[2,1024]{1,0:T(2,128)S(1)}, u32[]{:S(2)}, u32[]{:S(2)}) %collective-permute-start.32) | collective-permute-done | bytes 8224 | tf_op jit(solution)/shard_map/ppermute | solution.py:61
  118.5 1.5 collective-permute-done.31
  120.1 1.7 col_lse.4
  123.1 1.4 collective-permute-start.36
  125.0 2.9 %collective-permute-done.36 = f32[1,1024]{1,0:T(1,128)S(1)} collective-permute-done((f32[1,1024]{1,0:T(1,128)S(1)}, f32[1,1024]{1,0:T(1,128)S(1)}, u32[]{:S(2)}, u32[]{:S(2)}) %collective-permute-start.36) | collective-permute-done | bytes 4128 | tf_op jit(solution)/shard_map/ppermute | solution.py:61
  128.0 1.6 collective-permute-done.35
  129.6 1.7 row_lse.3
  132.5 2.6 %collective-permute-start.40 = (f32[2,1024]{1,0:T(2,128)S(1)}, f32[2,1024]{1,0:T(2,128)S(1)}, u32[]{:S(2)}, u32[]{:S(2)}) collective-permute-start(f32[2,1024]{1,0:T(2,128)S(1)} %pad_maximum_fusion.2), channel_id=1, source_target_pairs={{0,1},{1,2},{2,3},{3,0},{4,5},{5,6},{6,7},{7,4},{8,9},{9,10},{10,1... | collective-permute-start | bytes 24584 | tf_op jit(solution)/shard_map/ppermute | solution.py:61
  137.5 2.8 %collective-permute-done.39 = f32[2,1024]{1,0:T(2,128)S(1)} collective-permute-done((f32[2,1024]{1,0:T(2,128)S(1)}, f32[2,1024]{1,0:T(2,128)S(1)}, u32[]{:S(2)}, u32[]{:S(2)}) %collective-permute-start.39) | collective-permute-done | bytes 8224 | tf_op jit(solution)/shard_map/ppermute | solution.py:60
  141.6 1.9 collective-permute-start.42
  143.6 1.7 collective-permute-done.43
  145.3 1.5 collective-permute-done.42
  146.9 1.7 col_lse.5
  150.0 3.3 %collective-permute-start.46 = (f32[1,1024]{1,0:T(1,128)S(1)}, f32[1,1024]{1,0:T(1,128)S(1)}, u32[]{:S(2)}, u32[]{:S(2)}) collective-permute-start(f32[1,1024]{1,0:T(1,128)S(1)} %multiply_add_fusion.6), channel_id=1, source_target_pairs={{0,64},{16,80},{32,96},{48,112},{64,0},{80,16},{96,32},{112,48},{1... | collective-permute-start | bytes 12296 | tf_op jit(solution)/shard_map/ppermute | solution.py:60
  153.3 1.4 collective-permute-done.47
  155.9 3.8 %plan.1 = (bf16[1024,1024]{1,0:T(8,128)(2,1)S(1)}, f32[1,1024]{1,0:T(1,128)S(1)}, bf16[528,1024]{1,0:T(8,128)(2,1)S(1)}, bf16[528,1024]{1,0:T(8,128)(2,1)S(1)}) custom-call(f32[1024,1024]{1,0:T(8,128)S(1)} %get-tuple-element.54.logits_ref, f32[1,1024]{1,0:T(1,128)S(1)} %fusion.2.rowpot_ref, f32[1,1024]{1,0:T(1,128)S(1)} %add_subtract_fusion.colpot_ref, ...), custom_call_target="tpu_custom_call" | custom-call | flops 2147483648 | bytes 6299648 | tf_op jit(solution)/shard_map/plan/pallas_call | solution.py:458
  159.8 3.1 %collective-permute-start.50 = (bf16[528,1024]{1,0:T(8,128)(2,1)S(1)}, bf16[528,1024]{1,0:T(8,128)(2,1)S(1)}, u32[]{:S(2)}, u32[]{:S(2)}) collective-permute-start(bf16[528,1024]{1,0:T(8,128)(2,1)S(1)} %get-tuple-element.61), channel_id=1, source_target_pairs={{0,12},{1,13},{2,14},{3,15},{4,0},{5,1},{6,2},{7,3},{8,4},{9,5},{1... | collective-permute-start | bytes 3244040 | tf_op jit(solution)/shard_map/ppermute | solution.py:89
  163.0 4.7 %share.1 = (bf16[528,1024]{1,0:T(8,128)(2,1)S(1)}, bf16[528,1024]{1,0:T(8,128)(2,1)S(1)}, bf16[1024,1024]{1,0:T(8,128)(2,1)S(1)}, bf16[1024,1024]{1,0:T(8,128)(2,1)S(1)}) custom-call(s32[16]{0:T(128)S(1)} %fusion.6.spot_ref, bf16[1024,512]{1,0:T(8,128)(2,1)S(1)} %copy-done, bf16[1024,512]{1,0:T(8,128)(2,1)S(1)} %collective-permute-done.3.refs_9_.refs_1_, ...), custom_call_target="tpu_custom_call" | custom-call | flops 2147483648 | bytes 2101248 | tf_op jit(solution)/shard_map/share/pallas_call | solution.py:490
  167.9 1.9 collective-permute-start.52
  169.8 6.3 %collective-permute-done.49.top_more = bf16[528,1024]{1,0:T(8,128)(2,1)S(1)} collective-permute-done((bf16[528,1024]{1,0:T(8,128)(2,1)S(1)}, bf16[528,1024]{1,0:T(8,128)(2,1)S(1)}, u32[]{:S(2)}, u32[]{:S(2)}) %collective-permute-start.49) | collective-permute-done | bytes 1081376 | tf_op jit(solution)/shard_map/ppermute | solution.py:89
  176.1 2.9 %onward.1 = (bf16[528,1024]{1,0:T(8,128)(2,1)S(1)}, bf16[528,1024]{1,0:T(8,128)(2,1)S(1)}) custom-call(bf16[1024,1024]{1,0:T(8,128)(2,1)S(1)} %get-tuple-element.64.refs_8_.plan_ref, bf16[1024,1024]{1,0:T(8,128)(2,1)S(1)} %get-tuple-element.58.after_ref, bf16[1024,1024]{1,0:T(8,128)(2,1)S(1)} %get-tuple-element.59.before_ref, ...), custom_call_target="tpu_custom_call" | custom-call | flops 2147483648 | bytes 8458240 | tf_op jit(solution)/shard_map/onward/pallas_call | solution.py:458
  179.8 2.7 %collective-permute-start.54 = (bf16[528,1024]{1,0:T(8,128)(2,1)S(1)}, bf16[528,1024]{1,0:T(8,128)(2,1)S(1)}, u32[]{:S(2)}, u32[]{:S(2)}) collective-permute-start(bf16[528,1024]{1,0:T(8,128)(2,1)S(1)} %get-tuple-element.63), channel_id=1, source_target_pairs={{0,12},{1,13},{2,14},{3,15},{4,0},{5,1},{6,2},{7,3},{8,4},{9,5},{1... | collective-permute-start | bytes 3244040 | tf_op jit(solution)/shard_map/ppermute | solution.py:89
  182.4 4.8 %collective-permute-done.51.refs_10_ = bf16[528,1024]{1,0:T(8,128)(2,1)S(1)} collective-permute-done((bf16[528,1024]{1,0:T(8,128)(2,1)S(1)}, bf16[528,1024]{1,0:T(8,128)(2,1)S(1)}, u32[]{:S(2)}, u32[]{:S(2)}) %collective-permute-start.51) | collective-permute-done | bytes 1081376 | tf_op jit(solution)/shard_map/ppermute | solution.py:89
  187.7 3.8 %own.1 = (f32[1024,1024]{1,0:T(8,128)S(1)}, f32[1,1024]{1,0:T(1,128)S(1)}) custom-call(s32[16]{0:T(128)S(1)} %fusion.6.spot_ref, bf16[1024,512]{1,0:T(8,128)(2,1)S(1)} %copy-done, bf16[1024,512]{1,0:T(8,128)(2,1)S(1)} %collective-permute-done.3.refs_9_.refs_1_, bf16[1024,512]{1,0:T(8,128)(2,1)S(1)} %copy-done.2, ...), custom_call_target="tpu_custom_call" | custom-call | flops 2147483648 | bytes 4263936 | tf_op jit(solution)/shard_map/own/pallas_call | solution.py:490
  192.1 7.2 %collective-permute-done.53.top_ref = bf16[528,1024]{1,0:T(8,128)(2,1)S(1)} collective-permute-done((bf16[528,1024]{1,0:T(8,128)(2,1)S(1)}, bf16[528,1024]{1,0:T(8,128)(2,1)S(1)}, u32[]{:S(2)}, u32[]{:S(2)}) %collective-permute-start.53) | collective-permute-done | bytes 1081376 | tf_op jit(solution)/shard_map/ppermute | solution.py:89
  199.8 1.4 collective-permute-start.55
  201.2 1.5 collective-permute-start.56
  203.2 7.6 %collective-permute-done.55.refs_0_ = bf16[1040,256]{1,0:T(8,128)(2,1)S(1)} collective-permute-done((bf16[1040,256]{1,0:T(8,128)(2,1)S(1)}, bf16[1040,256]{1,0:T(8,128)(2,1)S(1)}, u32[]{:S(2)}, u32[]{:S(2)}) %collective-permute-start.55) | collective-permute-done | bytes 532512 | tf_op jit(solution)/shard_map/ppermute | solution.py:85
  210.8 3.7 %collective-permute-done.56.refs_1_ = bf16[1040,256]{1,0:T(8,128)(2,1)S(1)} collective-permute-done((bf16[1040,256]{1,0:T(8,128)(2,1)S(1)}, bf16[1040,256]{1,0:T(8,128)(2,1)S(1)}, u32[]{:S(2)}, u32[]{:S(2)}) %collective-permute-start.56) | collective-permute-done | bytes 532512 | tf_op jit(solution)/shard_map/ppermute | solution.py:85
  214.4 1.9 collective-permute-done.57.refs_2_
  (115 shorter events, 23.6 us)
Async XLA Ops:
  0.6 22.1 %collective-permute-start.3 = (bf16[1024,512]{1,0:T(8,128)(2,1)}, bf16[1024,512]{1,0:T(8,128)(2,1)S(1)}, u32[]{:S(2)}, u32[]{:S(2)}) collective-permute-start(bf16[1024,512]{1,0:T(8,128)(2,1)} %refs_0_.7), channel_id=1, source_target_pairs={{0,16},{16,0},{32,48},{48,32},{64,80},{80,64},{96,112},{112,96},{1... | collective-permute-start | bytes 3145736 | tf_op jit(solution)/shard_map/ppermute | solution.py:95
  0.7 24.9 %collective-permute-start.4 = (bf16[1024,512]{1,0:T(8,128)(2,1)}, bf16[1024,512]{1,0:T(8,128)(2,1)S(1)}, u32[]{:S(2)}, u32[]{:S(2)}) collective-permute-start(bf16[1024,512]{1,0:T(8,128)(2,1)} %refs_0_.7), channel_id=1, source_target_pairs={{0,32},{16,112},{32,64},{48,16},{64,96},{80,48},{96,0},{112,80},{1... | collective-permute-start | bytes 3145736 | tf_op jit(solution)/shard_map/ppermute | solution.py:101
  2.5 16.7 %collective-permute-start = (bf16[1024,256]{1,0:T(8,128)(2,1)}, bf16[1024,256]{1,0:T(8,128)(2,1)S(1)}, u32[]{:S(2)}, u32[]{:S(2)}) collective-permute-start(bf16[1024,256]{1,0:T(8,128)(2,1)} %refs_0_.5), channel_id=1, source_target_pairs={{0,3},{1,0},{2,1},{3,2},{4,7},{5,4},{6,5},{7,6},{8,11},{9,8},{10,9... | collective-permute-start | bytes 1572872 | tf_op jit(solution)/shard_map/ppermute | solution.py:85
  6.5 16.2 %collective-permute-start.1 = (bf16[1024,256]{1,0:T(8,128)(2,1)}, bf16[1024,256]{1,0:T(8,128)(2,1)S(1)}, u32[]{:S(2)}, u32[]{:S(2)}) collective-permute-start(bf16[1024,256]{1,0:T(8,128)(2,1)} %refs_0_.5), channel_id=1, source_target_pairs={{0,1},{1,2},{2,3},{3,0},{4,5},{5,6},{6,7},{7,4},{8,9},{9,10},{10,1... | collective-permute-start | bytes 1572872 | tf_op jit(solution)/shard_map/ppermute | solution.py:85
  6.5 16.2 %collective-permute-start.2 = (bf16[1024,256]{1,0:T(8,128)(2,1)}, bf16[1024,256]{1,0:T(8,128)(2,1)S(1)}, u32[]{:S(2)}, u32[]{:S(2)}) collective-permute-start(bf16[1024,256]{1,0:T(8,128)(2,1)} %refs_0_.5), channel_id=1, source_target_pairs={{0,2},{1,3},{2,0},{3,1},{4,6},{5,7},{6,4},{7,5},{8,10},{9,11},{10,... | collective-permute-start | bytes 1572872 | tf_op jit(solution)/shard_map/ppermute | solution.py:85
  19.1 26.5 %copy-start.6 = (bf16[1024,256]{1,0:T(8,128)(2,1)}, bf16[1024,256]{1,0:T(8,128)(2,1)S(1)}, u32[]{:S(2)}) copy-start(bf16[1024,256]{1,0:T(8,128)(2,1)S(1)} %collective-permute-done.refs_1_) | copy-start | bytes 1572868
  19.1 21.8 %collective-permute-start.5 = (bf16[1024,512]{1,0:T(8,128)(2,1)}, bf16[1024,512]{1,0:T(8,128)(2,1)S(1)}, u32[]{:S(2)}, u32[]{:S(2)}) collective-permute-start(bf16[1024,512]{1,0:T(8,128)(2,1)} %refs_0_.7), channel_id=1, source_target_pairs={{32,0},{112,16},{64,32},{16,48},{96,64},{48,80},{0,96},{80,112},{3... | collective-permute-start | bytes 3145736 | tf_op jit(solution)/shard_map/ppermute | solution.py:102
  22.7 22.9 %copy-start.7 = (bf16[1024,256]{1,0:T(8,128)(2,1)}, bf16[1024,256]{1,0:T(8,128)(2,1)S(1)}, u32[]{:S(2)}) copy-start(bf16[1024,256]{1,0:T(8,128)(2,1)S(1)} %collective-permute-done.1.refs_2_) | copy-start | bytes 1572868
  22.7 23.4 %copy-start.8 = (bf16[1024,256]{1,0:T(8,128)(2,1)}, bf16[1024,256]{1,0:T(8,128)(2,1)S(1)}, u32[]{:S(2)}) copy-start(bf16[1024,256]{1,0:T(8,128)(2,1)S(1)} %collective-permute-done.2.refs_3_) | copy-start | bytes 1572868
  25.6 35.4 %copy-start.1 = (bf16[1024,512]{1,0:T(8,128)(2,1)}, bf16[1024,512]{1,0:T(8,128)(2,1)S(1)}, u32[]{:S(2)}) copy-start(bf16[1024,512]{1,0:T(8,128)(2,1)S(1)} %collective-permute-done.4.refs_10_.refs_2_) | copy-start | bytes 3145732
  25.6 19.9 %collective-permute-start.6 = (bf16[1024,512]{1,0:T(8,128)(2,1)S(1)}, bf16[1024,512]{1,0:T(8,128)(2,1)}, u32[]{:S(2)}, u32[]{:S(2)}) collective-permute-start(bf16[1024,512]{1,0:T(8,128)(2,1)S(1)} %collective-permute-done.4.refs_10_.refs_2_), channel_id=1, source_target_pairs={{0,32},{16,112},{32,64},{48,16},{64,96},{80,48},{96,0},{112,80},{1... | collective-permute-start | bytes 3145736 | tf_op jit(solution)/shard_map/ppermute | solution.py:105
  27.3 18.3 %collective-permute-start.12 = (bf16[2048,256]{1,0:T(8,128)(2,1)}, bf16[2048,256]{1,0:T(8,128)(2,1)S(1)}, u32[]{:S(2)}, u32[]{:S(2)}) collective-permute-start(bf16[2048,256]{1,0:T(8,128)(2,1)} %get-tuple-element.47), channel_id=1, source_target_pairs={{0,12},{1,13},{2,14},{3,15},{4,0},{5,1},{6,2},{7,3},{8,4},{9,5},{1... | collective-permute-start | bytes 3145736 | tf_op jit(solution)/shard_map/ppermute | solution.py:89
  30.0 16.2 %collective-permute-start.10 = (bf16[2048,256]{1,0:T(8,128)(2,1)}, bf16[2048,256]{1,0:T(8,128)(2,1)S(1)}, u32[]{:S(2)}, u32[]{:S(2)}) collective-permute-start(bf16[2048,256]{1,0:T(8,128)(2,1)} %get-tuple-element.46), channel_id=1, source_target_pairs={{0,4},{1,5},{2,6},{3,7},{4,8},{5,9},{6,10},{7,11},{8,12},{9,13},{1... | collective-permute-start | bytes 3145736 | tf_op jit(solution)/shard_map/ppermute | solution.py:89
  30.0 23.9 %collective-permute-start.14 = (bf16[2048,256]{1,0:T(8,128)(2,1)}, bf16[2048,256]{1,0:T(8,128)(2,1)}, u32[]{:S(2)}, u32[]{:S(2)}) collective-permute-start(bf16[2048,256]{1,0:T(8,128)(2,1)} %get-tuple-element.46), channel_id=1, source_target_pairs={{0,12},{1,13},{2,14},{3,15},{4,0},{5,1},{6,2},{7,3},{8,4},{9,5},{1... | collective-permute-start | bytes 3145736 | tf_op jit(solution)/shard_map/ppermute | solution.py:89
  40.9 20.1 %copy-start.3 = (bf16[1024,512]{1,0:T(8,128)(2,1)}, bf16[1024,512]{1,0:T(8,128)(2,1)S(1)}, u32[]{:S(2)}) copy-start(bf16[1024,512]{1,0:T(8,128)(2,1)S(1)} %collective-permute-done.5.refs_12_.refs_4_) | copy-start | bytes 3145732
  40.9 18.1 %collective-permute-start.15 = (bf16[2048,256]{1,0:T(8,128)(2,1)}, bf16[2048,256]{1,0:T(8,128)(2,1)}, u32[]{:S(2)}, u32[]{:S(2)}) collective-permute-start(bf16[2048,256]{1,0:T(8,128)(2,1)} %get-tuple-element.47), channel_id=1, source_target_pairs={{0,4},{1,5},{2,6},{3,7},{4,8},{5,9},{6,10},{7,11},{8,12},{9,13},{1... | collective-permute-start | bytes 3145736 | tf_op jit(solution)/shard_map/ppermute | solution.py:89
  45.5 15.5 %collective-permute-start.7 = (bf16[1024,512]{1,0:T(8,128)(2,1)S(1)}, bf16[1024,512]{1,0:T(8,128)(2,1)}, u32[]{:S(2)}, u32[]{:S(2)}) collective-permute-start(bf16[1024,512]{1,0:T(8,128)(2,1)S(1)} %collective-permute-done.4.refs_10_.refs_2_), channel_id=1, source_target_pairs={{0,16},{16,0},{32,48},{48,32},{64,80},{80,64},{96,112},{112,96},{1... | collective-permute-start | bytes 3145736 | tf_op jit(solution)/shard_map/ppermute | solution.py:95
  45.6 15.4 %collective-permute-start.8 = (bf16[1024,512]{1,0:T(8,128)(2,1)S(1)}, bf16[1024,512]{1,0:T(8,128)(2,1)}, u32[]{:S(2)}, u32[]{:S(2)}) collective-permute-start(bf16[1024,512]{1,0:T(8,128)(2,1)S(1)} %collective-permute-done.5.refs_12_.refs_4_), channel_id=1, source_target_pairs={{0,16},{16,0},{32,48},{48,32},{64,80},{80,64},{96,112},{112,96},{1... | collective-permute-start | bytes 3145736 | tf_op jit(solution)/shard_map/ppermute | solution.py:95
  46.6 14.5 %collective-permute-start.9 = (bf16[1024,512]{1,0:T(8,128)(2,1)}, bf16[1024,512]{1,0:T(8,128)(2,1)}, u32[]{:S(2)}, u32[]{:S(2)}) collective-permute-start(bf16[1024,512]{1,0:T(8,128)(2,1)} %collective-permute-done.6.refs_14_.refs_6_), channel_id=1, source_target_pairs={{0,16},{16,0},{32,48},{48,32},{64,80},{80,64},{96,112},{112,96},{1... | collective-permute-start | bytes 3145736 | tf_op jit(solution)/shard_map/ppermute | solution.py:95
  53.9 17.0 %collective-permute-start.11 = (bf16[2048,256]{1,0:T(8,128)(2,1)}, bf16[2048,256]{1,0:T(8,128)(2,1)S(1)}, u32[]{:S(2)}, u32[]{:S(2)}) collective-permute-start(bf16[2048,256]{1,0:T(8,128)(2,1)} %copy-done.10), channel_id=1, source_target_pairs={{0,4},{1,5},{2,6},{3,7},{4,8},{5,9},{6,10},{7,11},{8,12},{9,13},{1... | collective-permute-start | bytes 3145736 | tf_op jit(solution)/shard_map/ppermute | solution.py:89
  59.0 15.0 %collective-permute-start.13 = (bf16[2048,256]{1,0:T(8,128)(2,1)}, bf16[2048,256]{1,0:T(8,128)(2,1)S(1)}, u32[]{:S(2)}, u32[]{:S(2)}) collective-permute-start(bf16[2048,256]{1,0:T(8,128)(2,1)} %copy-done.9), channel_id=1, source_target_pairs={{0,12},{1,13},{2,14},{3,15},{4,0},{5,1},{6,2},{7,3},{8,4},{9,5},{1... | collective-permute-start | bytes 3145736 | tf_op jit(solution)/shard_map/ppermute | solution.py:89
  78.0 1.2 collective-permute-start.16
  79.3 5.1 %collective-permute-start.18 = (f32[2,1024]{1,0:T(2,128)S(1)}, f32[2,1024]{1,0:T(2,128)S(1)}, u32[]{:S(2)}, u32[]{:S(2)}) collective-permute-start(f32[2,1024]{1,0:T(2,128)S(1)} %pad_maximum_fusion), channel_id=1, source_target_pairs={{0,1},{1,2},{2,3},{3,0},{4,5},{5,6},{6,7},{7,4},{8,9},{9,10},{10,1... | collective-permute-start | bytes 24584 | tf_op jit(solution)/shard_map/ppermute | solution.py:61
  79.4 6.6 %collective-permute-start.17 = (f32[2,1024]{1,0:T(2,128)S(1)}, f32[2,1024]{1,0:T(2,128)S(1)}, u32[]{:S(2)}, u32[]{:S(2)}) collective-permute-start(f32[2,1024]{1,0:T(2,128)S(1)} %pad_maximum_fusion), channel_id=1, source_target_pairs={{0,2},{1,3},{2,0},{3,1},{4,6},{5,7},{6,4},{7,5},{8,10},{9,11},{10,... | collective-permute-start | bytes 24584 | tf_op jit(solution)/shard_map/ppermute | solution.py:60
  84.4 1.5 collective-permute-start.19
  86.1 5.1 %collective-permute-start.21 = (f32[2,1024]{1,0:T(2,128)S(1)}, f32[2,1024]{1,0:T(2,128)S(1)}, u32[]{:S(2)}, u32[]{:S(2)}) collective-permute-start(f32[2,1024]{1,0:T(2,128)S(1)} %multiply_add_fusion.5), channel_id=1, source_target_pairs={{0,4},{1,5},{2,6},{3,7},{4,8},{5,9},{6,10},{7,11},{8,12},{9,13},{1... | collective-permute-start | bytes 24584 | tf_op jit(solution)/shard_map/ppermute | solution.py:61
  87.6 5.2 %collective-permute-start.20 = (f32[2,1024]{1,0:T(2,128)S(1)}, f32[2,1024]{1,0:T(2,128)S(1)}, u32[]{:S(2)}, u32[]{:S(2)}) collective-permute-start(f32[2,1024]{1,0:T(2,128)S(1)} %multiply_add_fusion.5), channel_id=1, source_target_pairs={{0,8},{1,9},{2,10},{3,11},{4,12},{5,13},{6,14},{7,15},{8,0},{9,1},... | collective-permute-start | bytes 24584 | tf_op jit(solution)/shard_map/ppermute | solution.py:60
  91.2 1.6 collective-permute-start.22
  94.5 2.1 collective-permute-start.23
  96.6 4.9 %collective-permute-start.25 = (f32[1,1024]{1,0:T(1,128)S(1)}, f32[1,1024]{1,0:T(1,128)S(1)}, u32[]{:S(2)}, u32[]{:S(2)}) collective-permute-start(f32[1,1024]{1,0:T(1,128)S(1)} %multiply_add_fusion.8), channel_id=1, source_target_pairs={{0,32},{16,112},{32,64},{48,16},{64,96},{80,48},{96,0},{112,80},{1... | collective-permute-start | bytes 12296 | tf_op jit(solution)/shard_map/ppermute | solution.py:61
  99.3 5.1 %collective-permute-start.24 = (f32[1,1024]{1,0:T(1,128)S(1)}, f32[1,1024]{1,0:T(1,128)S(1)}, u32[]{:S(2)}, u32[]{:S(2)}) collective-permute-start(f32[1,1024]{1,0:T(1,128)S(1)} %multiply_add_fusion.8), channel_id=1, source_target_pairs={{0,64},{16,80},{32,96},{48,112},{64,0},{80,16},{96,32},{112,48},{1... | collective-permute-start | bytes 12296 | tf_op jit(solution)/shard_map/ppermute | solution.py:60
  101.5 2.9 %collective-permute-start.26 = (f32[1,1024]{1,0:T(1,128)S(1)}, f32[1,1024]{1,0:T(1,128)S(1)}, u32[]{:S(2)}, u32[]{:S(2)}) collective-permute-start(f32[1,1024]{1,0:T(1,128)S(1)} %collective-permute-done.25), channel_id=1, source_target_pairs={{0,16},{16,0},{32,48},{48,32},{64,80},{80,64},{96,112},{112,96},{1... | collective-permute-start | bytes 12296 | tf_op jit(solution)/shard_map/ppermute | solution.py:62
  106.2 1.2 collective-permute-start.27
  107.4 4.9 %collective-permute-start.29 = (f32[2,1024]{1,0:T(2,128)S(1)}, f32[2,1024]{1,0:T(2,128)S(1)}, u32[]{:S(2)}, u32[]{:S(2)}) collective-permute-start(f32[2,1024]{1,0:T(2,128)S(1)} %pad_maximum_fusion.1), channel_id=1, source_target_pairs={{0,1},{1,2},{2,3},{3,0},{4,5},{5,6},{6,7},{7,4},{8,9},{9,10},{10,1... | collective-permute-start | bytes 24584 | tf_op jit(solution)/shard_map/ppermute | solution.py:61
  107.5 5.2 %collective-permute-start.28 = (f32[2,1024]{1,0:T(2,128)S(1)}, f32[2,1024]{1,0:T(2,128)S(1)}, u32[]{:S(2)}, u32[]{:S(2)}) collective-permute-start(f32[2,1024]{1,0:T(2,128)S(1)} %pad_maximum_fusion.1), channel_id=1, source_target_pairs={{0,2},{1,3},{2,0},{3,1},{4,6},{5,7},{6,4},{7,5},{8,10},{9,11},{10,... | collective-permute-start | bytes 24584 | tf_op jit(solution)/shard_map/ppermute | solution.py:60
  112.4 1.2 collective-permute-start.30
  113.6 4.9 %collective-permute-start.32 = (f32[2,1024]{1,0:T(2,128)S(1)}, f32[2,1024]{1,0:T(2,128)S(1)}, u32[]{:S(2)}, u32[]{:S(2)}) collective-permute-start(f32[2,1024]{1,0:T(2,128)S(1)} %multiply_add_fusion.3), channel_id=1, source_target_pairs={{0,4},{1,5},{2,6},{3,7},{4,8},{5,9},{6,10},{7,11},{8,12},{9,13},{1... | collective-permute-start | bytes 24584 | tf_op jit(solution)/shard_map/ppermute | solution.py:61
  114.9 5.2 %collective-permute-start.31 = (f32[2,1024]{1,0:T(2,128)S(1)}, f32[2,1024]{1,0:T(2,128)S(1)}, u32[]{:S(2)}, u32[]{:S(2)}) collective-permute-start(f32[2,1024]{1,0:T(2,128)S(1)} %multiply_add_fusion.3), channel_id=1, source_target_pairs={{0,8},{1,9},{2,10},{3,11},{4,12},{5,13},{6,14},{7,15},{8,0},{9,1},... | collective-permute-start | bytes 24584 | tf_op jit(solution)/shard_map/ppermute | solution.py:60
  118.5 1.5 collective-permute-start.33
  121.8 1.2 collective-permute-start.34
  123.1 4.9 %collective-permute-start.36 = (f32[1,1024]{1,0:T(1,128)S(1)}, f32[1,1024]{1,0:T(1,128)S(1)}, u32[]{:S(2)}, u32[]{:S(2)}) collective-permute-start(f32[1,1024]{1,0:T(1,128)S(1)} %multiply_add_fusion.7), channel_id=1, source_target_pairs={{0,32},{16,112},{32,64},{48,16},{64,96},{80,48},{96,0},{112,80},{1... | collective-permute-start | bytes 12296 | tf_op jit(solution)/shard_map/ppermute | solution.py:61
  124.4 5.1 %collective-permute-start.35 = (f32[1,1024]{1,0:T(1,128)S(1)}, f32[1,1024]{1,0:T(1,128)S(1)}, u32[]{:S(2)}, u32[]{:S(2)}) collective-permute-start(f32[1,1024]{1,0:T(1,128)S(1)} %multiply_add_fusion.7), channel_id=1, source_target_pairs={{0,64},{16,80},{32,96},{48,112},{64,0},{80,16},{96,32},{112,48},{1... | collective-permute-start | bytes 12296 | tf_op jit(solution)/shard_map/ppermute | solution.py:60
  128.0 1.6 collective-permute-start.37
  131.3 1.2 collective-permute-start.38
  132.5 4.9 %collective-permute-start.40 = (f32[2,1024]{1,0:T(2,128)S(1)}, f32[2,1024]{1,0:T(2,128)S(1)}, u32[]{:S(2)}, u32[]{:S(2)}) collective-permute-start(f32[2,1024]{1,0:T(2,128)S(1)} %pad_maximum_fusion.2), channel_id=1, source_target_pairs={{0,1},{1,2},{2,3},{3,0},{4,5},{5,6},{6,7},{7,4},{8,9},{9,10},{10,1... | collective-permute-start | bytes 24584 | tf_op jit(solution)/shard_map/ppermute | solution.py:61
  135.1 5.2 %collective-permute-start.39 = (f32[2,1024]{1,0:T(2,128)S(1)}, f32[2,1024]{1,0:T(2,128)S(1)}, u32[]{:S(2)}, u32[]{:S(2)}) collective-permute-start(f32[2,1024]{1,0:T(2,128)S(1)} %pad_maximum_fusion.2), channel_id=1, source_target_pairs={{0,2},{1,3},{2,0},{3,1},{4,6},{5,7},{6,4},{7,5},{8,10},{9,11},{10,... | collective-permute-start | bytes 24584 | tf_op jit(solution)/shard_map/ppermute | solution.py:60
  137.5 2.8 %collective-permute-start.41 = (f32[2,1024]{1,0:T(2,128)S(1)}, f32[2,1024]{1,0:T(2,128)S(1)}, u32[]{:S(2)}, u32[]{:S(2)}) collective-permute-start(f32[2,1024]{1,0:T(2,128)S(1)} %collective-permute-done.40), channel_id=1, source_target_pairs={{0,16},{16,0},{32,48},{48,32},{64,80},{80,64},{96,112},{112,96},{1... | collective-permute-start | bytes 24584 | tf_op jit(solution)/shard_map/ppermute | solution.py:62
  140.4 4.9 %collective-permute-start.43 = (f32[2,1024]{1,0:T(2,128)S(1)}, f32[2,1024]{1,0:T(2,128)S(1)}, u32[]{:S(2)}, u32[]{:S(2)}) collective-permute-start(f32[2,1024]{1,0:T(2,128)S(1)} %multiply_add_fusion.1), channel_id=1, source_target_pairs={{0,4},{1,5},{2,6},{3,7},{4,8},{5,9},{6,10},{7,11},{8,12},{9,13},{1... | collective-permute-start | bytes 24584 | tf_op jit(solution)/shard_map/ppermute | solution.py:61
  141.6 5.2 %collective-permute-start.42 = (f32[2,1024]{1,0:T(2,128)S(1)}, f32[2,1024]{1,0:T(2,128)S(1)}, u32[]{:S(2)}, u32[]{:S(2)}) collective-permute-start(f32[2,1024]{1,0:T(2,128)S(1)} %multiply_add_fusion.1), channel_id=1, source_target_pairs={{0,8},{1,9},{2,10},{3,11},{4,12},{5,13},{6,14},{7,15},{8,0},{9,1},... | collective-permute-start | bytes 24584 | tf_op jit(solution)/shard_map/ppermute | solution.py:60
  145.3 1.5 collective-permute-start.44
  148.5 1.2 collective-permute-start.45
  149.8 4.9 %collective-permute-start.47 = (f32[1,1024]{1,0:T(1,128)S(1)}, f32[1,1024]{1,0:T(1,128)S(1)}, u32[]{:S(2)}, u32[]{:S(2)}) collective-permute-start(f32[1,1024]{1,0:T(1,128)S(1)} %multiply_add_fusion.6), channel_id=1, source_target_pairs={{0,32},{16,112},{32,64},{48,16},{64,96},{80,48},{96,0},{112,80},{1... | collective-permute-start | bytes 12296 | tf_op jit(solution)/shard_map/ppermute | solution.py:61
  150.0 5.1 %collective-permute-start.46 = (f32[1,1024]{1,0:T(1,128)S(1)}, f32[1,1024]{1,0:T(1,128)S(1)}, u32[]{:S(2)}, u32[]{:S(2)}) collective-permute-start(f32[1,1024]{1,0:T(1,128)S(1)} %multiply_add_fusion.6), channel_id=1, source_target_pairs={{0,64},{16,80},{32,96},{48,112},{64,0},{80,16},{96,32},{112,48},{1... | collective-permute-start | bytes 12296 | tf_op jit(solution)/shard_map/ppermute | solution.py:60
  154.7 1.2 collective-permute-start.48
  155.9 7.1 %copy-start = (bf16[1024,512]{1,0:T(8,128)(2,1)S(1)}, bf16[1024,512]{1,0:T(8,128)(2,1)}, u32[]{:S(2)}) copy-start(bf16[1024,512]{1,0:T(8,128)(2,1)} %refs_0_.7) | copy-start | bytes 3145732
  159.7 16.4 %collective-permute-start.49 = (bf16[528,1024]{1,0:T(8,128)(2,1)S(1)}, bf16[528,1024]{1,0:T(8,128)(2,1)S(1)}, u32[]{:S(2)}, u32[]{:S(2)}) collective-permute-start(bf16[528,1024]{1,0:T(8,128)(2,1)S(1)} %get-tuple-element.60), channel_id=1, source_target_pairs={{0,4},{1,5},{2,6},{3,7},{4,8},{5,9},{6,10},{7,11},{8,12},{9,13},{1... | collective-permute-start | bytes 3244040 | tf_op jit(solution)/shard_map/ppermute | solution.py:89
  159.8 16.3 %collective-permute-start.50 = (bf16[528,1024]{1,0:T(8,128)(2,1)S(1)}, bf16[528,1024]{1,0:T(8,128)(2,1)S(1)}, u32[]{:S(2)}, u32[]{:S(2)}) collective-permute-start(bf16[528,1024]{1,0:T(8,128)(2,1)S(1)} %get-tuple-element.61), channel_id=1, source_target_pairs={{0,12},{1,13},{2,14},{3,15},{4,0},{5,1},{6,2},{7,3},{8,4},{9,5},{1... | collective-permute-start | bytes 3244040 | tf_op jit(solution)/shard_map/ppermute | solution.py:89
  167.8 19.5 %collective-permute-start.51 = (bf16[528,1024]{1,0:T(8,128)(2,1)S(1)}, bf16[528,1024]{1,0:T(8,128)(2,1)S(1)}, u32[]{:S(2)}, u32[]{:S(2)}) collective-permute-start(bf16[528,1024]{1,0:T(8,128)(2,1)S(1)} %get-tuple-element.65), channel_id=1, source_target_pairs={{0,12},{1,13},{2,14},{3,15},{4,0},{5,1},{6,2},{7,3},{8,4},{9,5},{1... | collective-permute-start | bytes 3244040 | tf_op jit(solution)/shard_map/ppermute | solution.py:89
  167.9 19.8 %collective-permute-start.52 = (bf16[528,1024]{1,0:T(8,128)(2,1)S(1)}, bf16[528,1024]{1,0:T(8,128)(2,1)S(1)}, u32[]{:S(2)}, u32[]{:S(2)}) collective-permute-start(bf16[528,1024]{1,0:T(8,128)(2,1)S(1)} %get-tuple-element.66), channel_id=1, source_target_pairs={{0,4},{1,5},{2,6},{3,7},{4,8},{5,9},{6,10},{7,11},{8,12},{9,13},{1... | collective-permute-start | bytes 3244040 | tf_op jit(solution)/shard_map/ppermute | solution.py:89
  179.1 20.2 %collective-permute-start.53 = (bf16[528,1024]{1,0:T(8,128)(2,1)S(1)}, bf16[528,1024]{1,0:T(8,128)(2,1)S(1)}, u32[]{:S(2)}, u32[]{:S(2)}) collective-permute-start(bf16[528,1024]{1,0:T(8,128)(2,1)S(1)} %get-tuple-element.62), channel_id=1, source_target_pairs={{0,4},{1,5},{2,6},{3,7},{4,8},{5,9},{6,10},{7,11},{8,12},{9,13},{1... | collective-permute-start | bytes 3244040 | tf_op jit(solution)/shard_map/ppermute | solution.py:89
  179.8 19.5 %collective-permute-start.54 = (bf16[528,1024]{1,0:T(8,128)(2,1)S(1)}, bf16[528,1024]{1,0:T(8,128)(2,1)S(1)}, u32[]{:S(2)}, u32[]{:S(2)}) collective-permute-start(bf16[528,1024]{1,0:T(8,128)(2,1)S(1)} %get-tuple-element.63), channel_id=1, source_target_pairs={{0,12},{1,13},{2,14},{3,15},{4,0},{5,1},{6,2},{7,3},{8,4},{9,5},{1... | collective-permute-start | bytes 3244040 | tf_op jit(solution)/shard_map/ppermute | solution.py:89
  199.8 11.0 %collective-permute-start.55 = (bf16[1040,256]{1,0:T(8,128)(2,1)S(1)}, bf16[1040,256]{1,0:T(8,128)(2,1)S(1)}, u32[]{:S(2)}, u32[]{:S(2)}) collective-permute-start(bf16[1040,256]{1,0:T(8,128)(2,1)S(1)} %get-tuple-element.76), channel_id=1, source_target_pairs={{0,2},{1,3},{2,0},{3,1},{4,6},{5,7},{6,4},{7,5},{8,10},{9,11},{10,... | collective-permute-start | bytes 1597448 | tf_op jit(solution)/shard_map/ppermute | solution.py:85
  201.2 13.2 %collective-permute-start.56 = (bf16[1040,256]{1,0:T(8,128)(2,1)S(1)}, bf16[1040,256]{1,0:T(8,128)(2,1)S(1)}, u32[]{:S(2)}, u32[]{:S(2)}) collective-permute-start(bf16[1040,256]{1,0:T(8,128)(2,1)S(1)} %get-tuple-element.77), channel_id=1, source_target_pairs={{0,3},{1,0},{2,1},{3,2},{4,7},{5,4},{6,5},{7,6},{8,11},{9,8},{10,9... | collective-permute-start | bytes 1597448 | tf_op jit(solution)/shard_map/ppermute | solution.py:85
  202.6 13.7 %collective-permute-start.57 = (bf16[1040,256]{1,0:T(8,128)(2,1)S(1)}, bf16[1040,256]{1,0:T(8,128)(2,1)S(1)}, u32[]{:S(2)}, u32[]{:S(2)}) collective-permute-start(bf16[1040,256]{1,0:T(8,128)(2,1)S(1)} %get-tuple-element.78), channel_id=1, source_target_pairs={{0,1},{1,2},{2,3},{3,0},{4,5},{5,6},{6,7},{7,4},{8,9},{9,10},{10,1... | collective-permute-start | bytes 1597448 | tf_op jit(solution)/shard_map/ppermute | solution.py:85
  (5 other events, 17.6 us)

commit v2 on v1

--- a/solution.py
+++ b/solution.py
@@ -451,7 +451,10 @@
             share = share + more_ref[here, lanes].astype(F32)
         out_ref[here, lanes] = share.astype(out_ref.dtype)
 
-    steps_of(lat_ref.shape[1], WIDE, multiply)
+    if more_ref is not None and out_ref.dtype == BF16:
+        multiply(pl.ds(0, lat_ref.shape[1]))
+    else:
+        steps_of(lat_ref.shape[1], WIDE, multiply)
 
 
 def in_vmem(kernel, name, out_shape, flops, *args):

time: 218 us -> 218 us (level)
  no operation moved by 1% of the time
where the time goes in v2:
time: 218 us; the launch traced here: 217 us
  waiting for transfers between devices  101 us (46%)
  starting transfers between devices  72.1 us (33%)
  Pallas kernels  39.9 us (18%)
  local copies, waits for them, and re-layouts  2.55 us (1%)
    ppermute x12, waiting for transfers between devices, hop_s(): return lax.ppermute(value, BOTH, everywhere([shift_x(by), shift_z(by)]))  32.4 us
    ppermute x6, waiting for transfers between devices, hop_f(): return lax.ppermute(value, BOTH, everywhere([shift_z(by), shift_x(by)]))  25.8 us
    ppermute x12, starting transfers between devices, hop_s(): return lax.ppermute(value, BOTH, everywhere([shift_x(by), shift_z(by)]))  22.6 us
    ppermute x9, starting transfers between devices, around(): far = lax.ppermute(value, axis, opposite)  21.3 us
    pallas_call x10, Pallas kernels, in_vmem(): pl.pallas_call(kernel, in_specs=[pl.BlockSpec(memory_space=pltpu.VMEM)] *...  20.1 us
    ppermute x9, waiting for transfers between devices, around(): far = lax.ppermute(value, axis, opposite)  14.2 us
    ppermute x9, waiting for transfers between devices, around(): near = lax.ppermute(value, axis, spread)  12.2 us
    ppermute x9, starting transfers between devices, around(): near = lax.ppermute(value, axis, spread)  11.1 us
  transfers between devices with their start and end apart: 58, of which 40 were waited for; matrix products, arithmetic and copies ran while one was open for 0% of the time, Pallas kernels for 10%

profile of v2, /device:TPU:0, one launch (start us, length us, event | category | flops | bytes accessed | tf_op | source)
XLA Modules:
  0.0 217.5 jit_solution(4527260843819258186)
XLA Ops:
  0.7 1.7 collective-permute-start.4
  2.5 4.0 %collective-permute-start = (bf16[1024,256]{1,0:T(8,128)(2,1)}, bf16[1024,256]{1,0:T(8,128)(2,1)S(1)}, u32[]{:S(2)}, u32[]{:S(2)}) collective-permute-start(bf16[1024,256]{1,0:T(8,128)(2,1)} %refs_0_.5), channel_id=1, source_target_pairs={{0,3},{1,0},{2,1},{3,2},{4,7},{5,4},{6,5},{7,6},{8,11},{9,8},{10,9... | collective-permute-start | bytes 1572872 | tf_op jit(solution)/shard_map/ppermute | solution.py:85
  6.5 1.9 collective-permute-start.2
  8.4 10.8 %collective-permute-done.refs_1_ = bf16[1024,256]{1,0:T(8,128)(2,1)S(1)} collective-permute-done((bf16[1024,256]{1,0:T(8,128)(2,1)}, bf16[1024,256]{1,0:T(8,128)(2,1)S(1)}, u32[]{:S(2)}, u32[]{:S(2)}) %collective-permute-start) | collective-permute-done | bytes 524320 | tf_op jit(solution)/shard_map/ppermute | solution.py:85
  19.1 1.7 collective-permute-start.5
  20.8 1.9 collective-permute-done.1.refs_2_
  22.7 1.4 copy-done.5
  24.1 1.5 halves.1
  25.6 1.6 collective-permute-start.6
  27.3 2.8 %collective-permute-start.12 = (bf16[2048,256]{1,0:T(8,128)(2,1)}, bf16[2048,256]{1,0:T(8,128)(2,1)S(1)}, u32[]{:S(2)}, u32[]{:S(2)}) collective-permute-start(bf16[2048,256]{1,0:T(8,128)(2,1)} %get-tuple-element.47), channel_id=1, source_target_pairs={{0,12},{1,13},{2,14},{3,15},{4,0},{5,1},{6,2},{7,3},{8,4},{9,5},{1... | collective-permute-start | bytes 3145736 | tf_op jit(solution)/shard_map/ppermute | solution.py:89
  30.0 3.2 %collective-permute-start.14 = (bf16[2048,256]{1,0:T(8,128)(2,1)}, bf16[2048,256]{1,0:T(8,128)(2,1)}, u32[]{:S(2)}, u32[]{:S(2)}) collective-permute-start(bf16[2048,256]{1,0:T(8,128)(2,1)} %get-tuple-element.46), channel_id=1, source_target_pairs={{0,12},{1,13},{2,14},{3,15},{4,0},{5,1},{6,2},{7,3},{8,4},{9,5},{1... | collective-permute-start | bytes 3145736 | tf_op jit(solution)/shard_map/ppermute | solution.py:89
  33.3 7.6 %collective-permute-done.5.refs_12_.refs_4_ = bf16[1024,512]{1,0:T(8,128)(2,1)S(1)} collective-permute-done((bf16[1024,512]{1,0:T(8,128)(2,1)}, bf16[1024,512]{1,0:T(8,128)(2,1)S(1)}, u32[]{:S(2)}, u32[]{:S(2)}) %collective-permute-start.5) | collective-permute-done | bytes 1048608 | tf_op jit(solution)/shard_map/ppermute | solution.py:102
  40.9 4.6 %collective-permute-start.15 = (bf16[2048,256]{1,0:T(8,128)(2,1)}, bf16[2048,256]{1,0:T(8,128)(2,1)}, u32[]{:S(2)}, u32[]{:S(2)}) collective-permute-start(bf16[2048,256]{1,0:T(8,128)(2,1)} %get-tuple-element.47), channel_id=1, source_target_pairs={{0,4},{1,5},{2,6},{3,7},{4,8},{5,9},{6,10},{7,11},{8,12},{9,13},{1... | collective-permute-start | bytes 3145736 | tf_op jit(solution)/shard_map/ppermute | solution.py:89
  47.9 6.0 %collective-permute-done.14 = bf16[2048,256]{1,0:T(8,128)(2,1)} collective-permute-done((bf16[2048,256]{1,0:T(8,128)(2,1)}, bf16[2048,256]{1,0:T(8,128)(2,1)}, u32[]{:S(2)}, u32[]{:S(2)}) %collective-permute-start.14) | collective-permute-done | bytes 1048608 | tf_op jit(solution)/shard_map/ppermute | solution.py:89
  55.1 3.9 %collective-permute-done.15 = bf16[2048,256]{1,0:T(8,128)(2,1)} collective-permute-done((bf16[2048,256]{1,0:T(8,128)(2,1)}, bf16[2048,256]{1,0:T(8,128)(2,1)}, u32[]{:S(2)}, u32[]{:S(2)}) %collective-permute-start.15) | collective-permute-done | bytes 1048608 | tf_op jit(solution)/shard_map/ppermute | solution.py:89
  59.0 2.0 collective-permute-start.13
  61.1 9.9 %cross_near.1 = (f32[1024,1024]{1,0:T(8,128)S(1)}, bf16[1024,1024]{1,0:T(8,128)(2,1)S(1)}) custom-call(s32[16]{0:T(128)S(1)} %fusion.6.spot_ref, bf16[1024,256]{1,0:T(8,128)(2,1)} %refs_0_.5, bf16[1024,256]{1,0:T(8,128)(2,1)} %copy-done.6, bf16[1024,256]{1,0:T(8,128)(2,1)} %copy-done.7, bf16[1024,256]{1,0:T(8,128)(2,1)} %copy-done.8, ...), custom_call_target="tpu_custom_call" | custom-call | flops 25769803776 | bytes 18874368 | tf_op jit(solution)/shard_map/cross_near/pallas_call | solution.py:327
  71.0 3.1 %collective-permute-done.13 = bf16[2048,256]{1,0:T(8,128)(2,1)S(1)} collective-permute-done((bf16[2048,256]{1,0:T(8,128)(2,1)}, bf16[2048,256]{1,0:T(8,128)(2,1)S(1)}, u32[]{:S(2)}, u32[]{:S(2)}) %collective-permute-start.13) | collective-permute-done | bytes 1048608 | tf_op jit(solution)/shard_map/ppermute | solution.py:89
  74.0 4.0 %cross_far.1 = (f32[1024,1024]{1,0:T(8,128)S(1)}, f32[1,1024]{1,0:T(1,128)S(1)}) custom-call(bf16[4,512,256]{2,1,0:T(8,128)(2,1)S(1)} %bitcast.16, bf16[4,512,256]{2,1,0:T(8,128)(2,1)S(1)} %bitcast.17, bf16[1024,1024]{1,0:T(8,128)(2,1)S(1)} %get-tuple-element.52.lat_ref, f32[1024,1024]{1,0:T(8,128)S(1)} %get-tuple-element.53.cross_ref), custom_call_target="tpu_custom_call" | custom-call | flops 2147483648 | bytes 8388608 | tf_op jit(solution)/shard_map/cross_far/pallas_call | solution.py:461
  79.4 4.9 %collective-permute-start.17 = (f32[2,1024]{1,0:T(2,128)S(1)}, f32[2,1024]{1,0:T(2,128)S(1)}, u32[]{:S(2)}, u32[]{:S(2)}) collective-permute-start(f32[2,1024]{1,0:T(2,128)S(1)} %pad_maximum_fusion), channel_id=1, source_target_pairs={{0,2},{1,3},{2,0},{3,1},{4,6},{5,7},{6,4},{7,5},{8,10},{9,11},{10,... | collective-permute-start | bytes 24584 | tf_op jit(solution)/shard_map/ppermute | solution.py:60
  84.5 1.5 collective-permute-done.17
  86.1 1.5 collective-permute-start.21
  87.6 3.4 %collective-permute-start.20 = (f32[2,1024]{1,0:T(2,128)S(1)}, f32[2,1024]{1,0:T(2,128)S(1)}, u32[]{:S(2)}, u32[]{:S(2)}) collective-permute-start(f32[2,1024]{1,0:T(2,128)S(1)} %multiply_add_fusion.5), channel_id=1, source_target_pairs={{0,8},{1,9},{2,10},{3,11},{4,12},{5,13},{6,14},{7,15},{8,0},{9,1},... | collective-permute-start | bytes 24584 | tf_op jit(solution)/shard_map/ppermute | solution.py:60
  91.2 1.6 collective-permute-done.20
  92.8 1.7 col_lse.3
  94.5 1.3 collective-permute-start.23
  96.6 2.7 %collective-permute-start.25 = (f32[1,1024]{1,0:T(1,128)S(1)}, f32[1,1024]{1,0:T(1,128)S(1)}, u32[]{:S(2)}, u32[]{:S(2)}) collective-permute-start(f32[1,1024]{1,0:T(1,128)S(1)} %multiply_add_fusion.8), channel_id=1, source_target_pairs={{0,32},{16,112},{32,64},{48,16},{64,96},{80,48},{96,0},{112,80},{1... | collective-permute-start | bytes 12296 | tf_op jit(solution)/shard_map/ppermute | solution.py:61
  99.3 1.5 collective-permute-start.24
  101.5 2.9 %collective-permute-done.24 = f32[1,1024]{1,0:T(1,128)S(1)} collective-permute-done((f32[1,1024]{1,0:T(1,128)S(1)}, f32[1,1024]{1,0:T(1,128)S(1)}, u32[]{:S(2)}, u32[]{:S(2)}) %collective-permute-start.24) | collective-permute-done | bytes 4128 | tf_op jit(solution)/shard_map/ppermute | solution.py:60
  104.5 1.7 row_lse.2
  107.5 2.9 %collective-permute-start.28 = (f32[2,1024]{1,0:T(2,128)S(1)}, f32[2,1024]{1,0:T(2,128)S(1)}, u32[]{:S(2)}, u32[]{:S(2)}) collective-permute-start(f32[2,1024]{1,0:T(2,128)S(1)} %pad_maximum_fusion.1), channel_id=1, source_target_pairs={{0,2},{1,3},{2,0},{3,1},{4,6},{5,7},{6,4},{7,5},{8,10},{9,11},{10,... | collective-permute-start | bytes 24584 | tf_op jit(solution)/shard_map/ppermute | solution.py:60
  110.4 1.9 collective-permute-done.29
  113.6 1.3 collective-permute-start.32
  114.9 1.4 collective-permute-start.31
  116.3 2.2 %collective-permute-done.32 = f32[2,1024]{1,0:T(2,128)S(1)} collective-permute-done((f32[2,1024]{1,0:T(2,128)S(1)}, f32[2,1024]{1,0:T(2,128)S(1)}, u32[]{:S(2)}, u32[]{:S(2)}) %collective-permute-start.32) | collective-permute-done | bytes 8224 | tf_op jit(solution)/shard_map/ppermute | solution.py:61
  118.5 1.5 collective-permute-done.31
  120.1 1.7 col_lse.4
  123.1 1.4 collective-permute-start.36
  125.0 2.9 %collective-permute-done.36 = f32[1,1024]{1,0:T(1,128)S(1)} collective-permute-done((f32[1,1024]{1,0:T(1,128)S(1)}, f32[1,1024]{1,0:T(1,128)S(1)}, u32[]{:S(2)}, u32[]{:S(2)}) %collective-permute-start.36) | collective-permute-done | bytes 4128 | tf_op jit(solution)/shard_map/ppermute | solution.py:61
  128.0 1.6 collective-permute-done.35
  129.6 1.7 row_lse.3
  132.5 2.6 %collective-permute-start.40 = (f32[2,1024]{1,0:T(2,128)S(1)}, f32[2,1024]{1,0:T(2,128)S(1)}, u32[]{:S(2)}, u32[]{:S(2)}) collective-permute-start(f32[2,1024]{1,0:T(2,128)S(1)} %pad_maximum_fusion.2), channel_id=1, source_target_pairs={{0,1},{1,2},{2,3},{3,0},{4,5},{5,6},{6,7},{7,4},{8,9},{9,10},{10,1... | collective-permute-start | bytes 24584 | tf_op jit(solution)/shard_map/ppermute | solution.py:61
  137.5 2.8 %collective-permute-done.39 = f32[2,1024]{1,0:T(2,128)S(1)} collective-permute-done((f32[2,1024]{1,0:T(2,128)S(1)}, f32[2,1024]{1,0:T(2,128)S(1)}, u32[]{:S(2)}, u32[]{:S(2)}) %collective-permute-start.39) | collective-permute-done | bytes 8224 | tf_op jit(solution)/shard_map/ppermute | solution.py:60
  141.6 1.9 collective-permute-start.42
  143.6 1.7 collective-permute-done.43
  145.3 1.5 collective-permute-done.42
  146.9 1.7 col_lse.5
  150.0 3.3 %collective-permute-start.46 = (f32[1,1024]{1,0:T(1,128)S(1)}, f32[1,1024]{1,0:T(1,128)S(1)}, u32[]{:S(2)}, u32[]{:S(2)}) collective-permute-start(f32[1,1024]{1,0:T(1,128)S(1)} %multiply_add_fusion.6), channel_id=1, source_target_pairs={{0,64},{16,80},{32,96},{48,112},{64,0},{80,16},{96,32},{112,48},{1... | collective-permute-start | bytes 12296 | tf_op jit(solution)/shard_map/ppermute | solution.py:60
  153.3 1.4 collective-permute-done.47
  155.9 3.8 %plan.1 = (bf16[1024,1024]{1,0:T(8,128)(2,1)S(1)}, f32[1,1024]{1,0:T(1,128)S(1)}, bf16[528,1024]{1,0:T(8,128)(2,1)S(1)}, bf16[528,1024]{1,0:T(8,128)(2,1)S(1)}) custom-call(f32[1024,1024]{1,0:T(8,128)S(1)} %get-tuple-element.54.logits_ref, f32[1,1024]{1,0:T(1,128)S(1)} %fusion.2.rowpot_ref, f32[1,1024]{1,0:T(1,128)S(1)} %add_subtract_fusion.colpot_ref, ...), custom_call_target="tpu_custom_call" | custom-call | flops 2147483648 | bytes 6299648 | tf_op jit(solution)/shard_map/plan/pallas_call | solution.py:461
  159.8 3.1 %collective-permute-start.50 = (bf16[528,1024]{1,0:T(8,128)(2,1)S(1)}, bf16[528,1024]{1,0:T(8,128)(2,1)S(1)}, u32[]{:S(2)}, u32[]{:S(2)}) collective-permute-start(bf16[528,1024]{1,0:T(8,128)(2,1)S(1)} %get-tuple-element.61), channel_id=1, source_target_pairs={{0,12},{1,13},{2,14},{3,15},{4,0},{5,1},{6,2},{7,3},{8,4},{9,5},{1... | collective-permute-start | bytes 3244040 | tf_op jit(solution)/shard_map/ppermute | solution.py:89
  163.0 4.7 %share.1 = (bf16[528,1024]{1,0:T(8,128)(2,1)S(1)}, bf16[528,1024]{1,0:T(8,128)(2,1)S(1)}, bf16[1024,1024]{1,0:T(8,128)(2,1)S(1)}, bf16[1024,1024]{1,0:T(8,128)(2,1)S(1)}) custom-call(s32[16]{0:T(128)S(1)} %fusion.6.spot_ref, bf16[1024,512]{1,0:T(8,128)(2,1)S(1)} %copy-done, bf16[1024,512]{1,0:T(8,128)(2,1)S(1)} %collective-permute-done.3.refs_9_.refs_1_, ...), custom_call_target="tpu_custom_call" | custom-call | flops 2147483648 | bytes 2101248 | tf_op jit(solution)/shard_map/share/pallas_call | solution.py:493
  167.9 1.9 collective-permute-start.52
  169.8 6.3 %collective-permute-done.49.top_more = bf16[528,1024]{1,0:T(8,128)(2,1)S(1)} collective-permute-done((bf16[528,1024]{1,0:T(8,128)(2,1)S(1)}, bf16[528,1024]{1,0:T(8,128)(2,1)S(1)}, u32[]{:S(2)}, u32[]{:S(2)}) %collective-permute-start.49) | collective-permute-done | bytes 1081376 | tf_op jit(solution)/shard_map/ppermute | solution.py:89
  176.1 2.4 %onward.1 = (bf16[528,1024]{1,0:T(8,128)(2,1)S(1)}, bf16[528,1024]{1,0:T(8,128)(2,1)S(1)}) custom-call(bf16[1024,1024]{1,0:T(8,128)(2,1)S(1)} %get-tuple-element.64.refs_8_.plan_ref, bf16[1024,1024]{1,0:T(8,128)(2,1)S(1)} %get-tuple-element.58.after_ref, bf16[1024,1024]{1,0:T(8,128)(2,1)S(1)} %get-tuple-element.59.before_ref, ...), custom_call_target="tpu_custom_call" | custom-call | flops 2147483648 | bytes 8458240 | tf_op jit(solution)/shard_map/onward/pallas_call | solution.py:461
  179.2 2.7 %collective-permute-start.54 = (bf16[528,1024]{1,0:T(8,128)(2,1)S(1)}, bf16[528,1024]{1,0:T(8,128)(2,1)S(1)}, u32[]{:S(2)}, u32[]{:S(2)}) collective-permute-start(bf16[528,1024]{1,0:T(8,128)(2,1)S(1)} %get-tuple-element.63), channel_id=1, source_target_pairs={{0,12},{1,13},{2,14},{3,15},{4,0},{5,1},{6,2},{7,3},{8,4},{9,5},{1... | collective-permute-start | bytes 3244040 | tf_op jit(solution)/shard_map/ppermute | solution.py:89
  181.9 5.4 %collective-permute-done.51.refs_10_ = bf16[528,1024]{1,0:T(8,128)(2,1)S(1)} collective-permute-done((bf16[528,1024]{1,0:T(8,128)(2,1)S(1)}, bf16[528,1024]{1,0:T(8,128)(2,1)S(1)}, u32[]{:S(2)}, u32[]{:S(2)}) %collective-permute-start.51) | collective-permute-done | bytes 1081376 | tf_op jit(solution)/shard_map/ppermute | solution.py:89
  187.7 3.8 %own.1 = (f32[1024,1024]{1,0:T(8,128)S(1)}, f32[1,1024]{1,0:T(1,128)S(1)}) custom-call(s32[16]{0:T(128)S(1)} %fusion.6.spot_ref, bf16[1024,512]{1,0:T(8,128)(2,1)S(1)} %copy-done, bf16[1024,512]{1,0:T(8,128)(2,1)S(1)} %collective-permute-done.3.refs_9_.refs_1_, bf16[1024,512]{1,0:T(8,128)(2,1)S(1)} %copy-done.2, ...), custom_call_target="tpu_custom_call" | custom-call | flops 2147483648 | bytes 4263936 | tf_op jit(solution)/shard_map/own/pallas_call | solution.py:493
  192.1 7.2 %collective-permute-done.53.top_ref = bf16[528,1024]{1,0:T(8,128)(2,1)S(1)} collective-permute-done((bf16[528,1024]{1,0:T(8,128)(2,1)S(1)}, bf16[528,1024]{1,0:T(8,128)(2,1)S(1)}, u32[]{:S(2)}, u32[]{:S(2)}) %collective-permute-start.53) | collective-permute-done | bytes 1081376 | tf_op jit(solution)/shard_map/ppermute | solution.py:89
  199.8 1.4 collective-permute-start.55
  201.2 1.5 collective-permute-start.56
  203.2 7.6 %collective-permute-done.55.refs_0_ = bf16[1040,256]{1,0:T(8,128)(2,1)S(1)} collective-permute-done((bf16[1040,256]{1,0:T(8,128)(2,1)S(1)}, bf16[1040,256]{1,0:T(8,128)(2,1)S(1)}, u32[]{:S(2)}, u32[]{:S(2)}) %collective-permute-start.55) | collective-permute-done | bytes 532512 | tf_op jit(solution)/shard_map/ppermute | solution.py:85
  210.8 3.7 %collective-permute-done.56.refs_1_ = bf16[1040,256]{1,0:T(8,128)(2,1)S(1)} collective-permute-done((bf16[1040,256]{1,0:T(8,128)(2,1)S(1)}, bf16[1040,256]{1,0:T(8,128)(2,1)S(1)}, u32[]{:S(2)}, u32[]{:S(2)}) %collective-permute-start.56) | collective-permute-done | bytes 532512 | tf_op jit(solution)/shard_map/ppermute | solution.py:85
  214.4 1.9 collective-permute-done.57.refs_2_
  (115 shorter events, 23.6 us)
Async XLA Ops:
  0.6 22.1 %collective-permute-start.3 = (bf16[1024,512]{1,0:T(8,128)(2,1)}, bf16[1024,512]{1,0:T(8,128)(2,1)S(1)}, u32[]{:S(2)}, u32[]{:S(2)}) collective-permute-start(bf16[1024,512]{1,0:T(8,128)(2,1)} %refs_0_.7), channel_id=1, source_target_pairs={{0,16},{16,0},{32,48},{48,32},{64,80},{80,64},{96,112},{112,96},{1... | collective-permute-start | bytes 3145736 | tf_op jit(solution)/shard_map/ppermute | solution.py:95
  0.7 24.9 %collective-permute-start.4 = (bf16[1024,512]{1,0:T(8,128)(2,1)}, bf16[1024,512]{1,0:T(8,128)(2,1)S(1)}, u32[]{:S(2)}, u32[]{:S(2)}) collective-permute-start(bf16[1024,512]{1,0:T(8,128)(2,1)} %refs_0_.7), channel_id=1, source_target_pairs={{0,32},{16,112},{32,64},{48,16},{64,96},{80,48},{96,0},{112,80},{1... | collective-permute-start | bytes 3145736 | tf_op jit(solution)/shard_map/ppermute | solution.py:101
  2.5 16.7 %collective-permute-start = (bf16[1024,256]{1,0:T(8,128)(2,1)}, bf16[1024,256]{1,0:T(8,128)(2,1)S(1)}, u32[]{:S(2)}, u32[]{:S(2)}) collective-permute-start(bf16[1024,256]{1,0:T(8,128)(2,1)} %refs_0_.5), channel_id=1, source_target_pairs={{0,3},{1,0},{2,1},{3,2},{4,7},{5,4},{6,5},{7,6},{8,11},{9,8},{10,9... | collective-permute-start | bytes 1572872 | tf_op jit(solution)/shard_map/ppermute | solution.py:85
  6.5 16.2 %collective-permute-start.1 = (bf16[1024,256]{1,0:T(8,128)(2,1)}, bf16[1024,256]{1,0:T(8,128)(2,1)S(1)}, u32[]{:S(2)}, u32[]{:S(2)}) collective-permute-start(bf16[1024,256]{1,0:T(8,128)(2,1)} %refs_0_.5), channel_id=1, source_target_pairs={{0,1},{1,2},{2,3},{3,0},{4,5},{5,6},{6,7},{7,4},{8,9},{9,10},{10,1... | collective-permute-start | bytes 1572872 | tf_op jit(solution)/shard_map/ppermute | solution.py:85
  6.5 16.2 %collective-permute-start.2 = (bf16[1024,256]{1,0:T(8,128)(2,1)}, bf16[1024,256]{1,0:T(8,128)(2,1)S(1)}, u32[]{:S(2)}, u32[]{:S(2)}) collective-permute-start(bf16[1024,256]{1,0:T(8,128)(2,1)} %refs_0_.5), channel_id=1, source_target_pairs={{0,2},{1,3},{2,0},{3,1},{4,6},{5,7},{6,4},{7,5},{8,10},{9,11},{10,... | collective-permute-start | bytes 1572872 | tf_op jit(solution)/shard_map/ppermute | solution.py:85
  19.1 26.5 %copy-start.6 = (bf16[1024,256]{1,0:T(8,128)(2,1)}, bf16[1024,256]{1,0:T(8,128)(2,1)S(1)}, u32[]{:S(2)}) copy-start(bf16[1024,256]{1,0:T(8,128)(2,1)S(1)} %collective-permute-done.refs_1_) | copy-start | bytes 1572868
  19.1 21.8 %collective-permute-start.5 = (bf16[1024,512]{1,0:T(8,128)(2,1)}, bf16[1024,512]{1,0:T(8,128)(2,1)S(1)}, u32[]{:S(2)}, u32[]{:S(2)}) collective-permute-start(bf16[1024,512]{1,0:T(8,128)(2,1)} %refs_0_.7), channel_id=1, source_target_pairs={{32,0},{112,16},{64,32},{16,48},{96,64},{48,80},{0,96},{80,112},{3... | collective-permute-start | bytes 3145736 | tf_op jit(solution)/shard_map/ppermute | solution.py:102
  22.7 22.9 %copy-start.7 = (bf16[1024,256]{1,0:T(8,128)(2,1)}, bf16[1024,256]{1,0:T(8,128)(2,1)S(1)}, u32[]{:S(2)}) copy-start(bf16[1024,256]{1,0:T(8,128)(2,1)S(1)} %collective-permute-done.1.refs_2_) | copy-start | bytes 1572868
  22.7 23.4 %copy-start.8 = (bf16[1024,256]{1,0:T(8,128)(2,1)}, bf16[1024,256]{1,0:T(8,128)(2,1)S(1)}, u32[]{:S(2)}) copy-start(bf16[1024,256]{1,0:T(8,128)(2,1)S(1)} %collective-permute-done.2.refs_3_) | copy-start | bytes 1572868
  25.6 35.4 %copy-start.1 = (bf16[1024,512]{1,0:T(8,128)(2,1)}, bf16[1024,512]{1,0:T(8,128)(2,1)S(1)}, u32[]{:S(2)}) copy-start(bf16[1024,512]{1,0:T(8,128)(2,1)S(1)} %collective-permute-done.4.refs_10_.refs_2_) | copy-start | bytes 3145732
  25.6 19.9 %collective-permute-start.6 = (bf16[1024,512]{1,0:T(8,128)(2,1)S(1)}, bf16[1024,512]{1,0:T(8,128)(2,1)}, u32[]{:S(2)}, u32[]{:S(2)}) collective-permute-start(bf16[1024,512]{1,0:T(8,128)(2,1)S(1)} %collective-permute-done.4.refs_10_.refs_2_), channel_id=1, source_target_pairs={{0,32},{16,112},{32,64},{48,16},{64,96},{80,48},{96,0},{112,80},{1... | collective-permute-start | bytes 3145736 | tf_op jit(solution)/shard_map/ppermute | solution.py:105
  27.3 18.3 %collective-permute-start.12 = (bf16[2048,256]{1,0:T(8,128)(2,1)}, bf16[2048,256]{1,0:T(8,128)(2,1)S(1)}, u32[]{:S(2)}, u32[]{:S(2)}) collective-permute-start(bf16[2048,256]{1,0:T(8,128)(2,1)} %get-tuple-element.47), channel_id=1, source_target_pairs={{0,12},{1,13},{2,14},{3,15},{4,0},{5,1},{6,2},{7,3},{8,4},{9,5},{1... | collective-permute-start | bytes 3145736 | tf_op jit(solution)/shard_map/ppermute | solution.py:89
  30.0 16.2 %collective-permute-start.10 = (bf16[2048,256]{1,0:T(8,128)(2,1)}, bf16[2048,256]{1,0:T(8,128)(2,1)S(1)}, u32[]{:S(2)}, u32[]{:S(2)}) collective-permute-start(bf16[2048,256]{1,0:T(8,128)(2,1)} %get-tuple-element.46), channel_id=1, source_target_pairs={{0,4},{1,5},{2,6},{3,7},{4,8},{5,9},{6,10},{7,11},{8,12},{9,13},{1... | collective-permute-start | bytes 3145736 | tf_op jit(solution)/shard_map/ppermute | solution.py:89
  30.0 23.9 %collective-permute-start.14 = (bf16[2048,256]{1,0:T(8,128)(2,1)}, bf16[2048,256]{1,0:T(8,128)(2,1)}, u32[]{:S(2)}, u32[]{:S(2)}) collective-permute-start(bf16[2048,256]{1,0:T(8,128)(2,1)} %get-tuple-element.46), channel_id=1, source_target_pairs={{0,12},{1,13},{2,14},{3,15},{4,0},{5,1},{6,2},{7,3},{8,4},{9,5},{1... | collective-permute-start | bytes 3145736 | tf_op jit(solution)/shard_map/ppermute | solution.py:89
  40.9 20.1 %copy-start.3 = (bf16[1024,512]{1,0:T(8,128)(2,1)}, bf16[1024,512]{1,0:T(8,128)(2,1)S(1)}, u32[]{:S(2)}) copy-start(bf16[1024,512]{1,0:T(8,128)(2,1)S(1)} %collective-permute-done.5.refs_12_.refs_4_) | copy-start | bytes 3145732
  40.9 18.1 %collective-permute-start.15 = (bf16[2048,256]{1,0:T(8,128)(2,1)}, bf16[2048,256]{1,0:T(8,128)(2,1)}, u32[]{:S(2)}, u32[]{:S(2)}) collective-permute-start(bf16[2048,256]{1,0:T(8,128)(2,1)} %get-tuple-element.47), channel_id=1, source_target_pairs={{0,4},{1,5},{2,6},{3,7},{4,8},{5,9},{6,10},{7,11},{8,12},{9,13},{1... | collective-permute-start | bytes 3145736 | tf_op jit(solution)/shard_map/ppermute | solution.py:89
  45.5 15.5 %collective-permute-start.7 = (bf16[1024,512]{1,0:T(8,128)(2,1)S(1)}, bf16[1024,512]{1,0:T(8,128)(2,1)}, u32[]{:S(2)}, u32[]{:S(2)}) collective-permute-start(bf16[1024,512]{1,0:T(8,128)(2,1)S(1)} %collective-permute-done.4.refs_10_.refs_2_), channel_id=1, source_target_pairs={{0,16},{16,0},{32,48},{48,32},{64,80},{80,64},{96,112},{112,96},{1... | collective-permute-start | bytes 3145736 | tf_op jit(solution)/shard_map/ppermute | solution.py:95
  45.6 15.4 %collective-permute-start.8 = (bf16[1024,512]{1,0:T(8,128)(2,1)S(1)}, bf16[1024,512]{1,0:T(8,128)(2,1)}, u32[]{:S(2)}, u32[]{:S(2)}) collective-permute-start(bf16[1024,512]{1,0:T(8,128)(2,1)S(1)} %collective-permute-done.5.refs_12_.refs_4_), channel_id=1, source_target_pairs={{0,16},{16,0},{32,48},{48,32},{64,80},{80,64},{96,112},{112,96},{1... | collective-permute-start | bytes 3145736 | tf_op jit(solution)/shard_map/ppermute | solution.py:95
  46.6 14.5 %collective-permute-start.9 = (bf16[1024,512]{1,0:T(8,128)(2,1)}, bf16[1024,512]{1,0:T(8,128)(2,1)}, u32[]{:S(2)}, u32[]{:S(2)}) collective-permute-start(bf16[1024,512]{1,0:T(8,128)(2,1)} %collective-permute-done.6.refs_14_.refs_6_), channel_id=1, source_target_pairs={{0,16},{16,0},{32,48},{48,32},{64,80},{80,64},{96,112},{112,96},{1... | collective-permute-start | bytes 3145736 | tf_op jit(solution)/shard_map/ppermute | solution.py:95
  53.9 17.0 %collective-permute-start.11 = (bf16[2048,256]{1,0:T(8,128)(2,1)}, bf16[2048,256]{1,0:T(8,128)(2,1)S(1)}, u32[]{:S(2)}, u32[]{:S(2)}) collective-permute-start(bf16[2048,256]{1,0:T(8,128)(2,1)} %copy-done.10), channel_id=1, source_target_pairs={{0,4},{1,5},{2,6},{3,7},{4,8},{5,9},{6,10},{7,11},{8,12},{9,13},{1... | collective-permute-start | bytes 3145736 | tf_op jit(solution)/shard_map/ppermute | solution.py:89
  59.0 15.0 %collective-permute-start.13 = (bf16[2048,256]{1,0:T(8,128)(2,1)}, bf16[2048,256]{1,0:T(8,128)(2,1)S(1)}, u32[]{:S(2)}, u32[]{:S(2)}) collective-permute-start(bf16[2048,256]{1,0:T(8,128)(2,1)} %copy-done.9), channel_id=1, source_target_pairs={{0,12},{1,13},{2,14},{3,15},{4,0},{5,1},{6,2},{7,3},{8,4},{9,5},{1... | collective-permute-start | bytes 3145736 | tf_op jit(solution)/shard_map/ppermute | solution.py:89
  78.0 1.2 collective-permute-start.16
  79.3 5.1 %collective-permute-start.18 = (f32[2,1024]{1,0:T(2,128)S(1)}, f32[2,1024]{1,0:T(2,128)S(1)}, u32[]{:S(2)}, u32[]{:S(2)}) collective-permute-start(f32[2,1024]{1,0:T(2,128)S(1)} %pad_maximum_fusion), channel_id=1, source_target_pairs={{0,1},{1,2},{2,3},{3,0},{4,5},{5,6},{6,7},{7,4},{8,9},{9,10},{10,1... | collective-permute-start | bytes 24584 | tf_op jit(solution)/shard_map/ppermute | solution.py:61
  79.4 6.6 %collective-permute-start.17 = (f32[2,1024]{1,0:T(2,128)S(1)}, f32[2,1024]{1,0:T(2,128)S(1)}, u32[]{:S(2)}, u32[]{:S(2)}) collective-permute-start(f32[2,1024]{1,0:T(2,128)S(1)} %pad_maximum_fusion), channel_id=1, source_target_pairs={{0,2},{1,3},{2,0},{3,1},{4,6},{5,7},{6,4},{7,5},{8,10},{9,11},{10,... | collective-permute-start | bytes 24584 | tf_op jit(solution)/shard_map/ppermute | solution.py:60
  84.4 1.5 collective-permute-start.19
  86.1 5.1 %collective-permute-start.21 = (f32[2,1024]{1,0:T(2,128)S(1)}, f32[2,1024]{1,0:T(2,128)S(1)}, u32[]{:S(2)}, u32[]{:S(2)}) collective-permute-start(f32[2,1024]{1,0:T(2,128)S(1)} %multiply_add_fusion.5), channel_id=1, source_target_pairs={{0,4},{1,5},{2,6},{3,7},{4,8},{5,9},{6,10},{7,11},{8,12},{9,13},{1... | collective-permute-start | bytes 24584 | tf_op jit(solution)/shard_map/ppermute | solution.py:61
  87.6 5.2 %collective-permute-start.20 = (f32[2,1024]{1,0:T(2,128)S(1)}, f32[2,1024]{1,0:T(2,128)S(1)}, u32[]{:S(2)}, u32[]{:S(2)}) collective-permute-start(f32[2,1024]{1,0:T(2,128)S(1)} %multiply_add_fusion.5), channel_id=1, source_target_pairs={{0,8},{1,9},{2,10},{3,11},{4,12},{5,13},{6,14},{7,15},{8,0},{9,1},... | collective-permute-start | bytes 24584 | tf_op jit(solution)/shard_map/ppermute | solution.py:60
  91.2 1.6 collective-permute-start.22
  94.5 2.1 collective-permute-start.23
  96.6 4.9 %collective-permute-start.25 = (f32[1,1024]{1,0:T(1,128)S(1)}, f32[1,1024]{1,0:T(1,128)S(1)}, u32[]{:S(2)}, u32[]{:S(2)}) collective-permute-start(f32[1,1024]{1,0:T(1,128)S(1)} %multiply_add_fusion.8), channel_id=1, source_target_pairs={{0,32},{16,112},{32,64},{48,16},{64,96},{80,48},{96,0},{112,80},{1... | collective-permute-start | bytes 12296 | tf_op jit(solution)/shard_map/ppermute | solution.py:61
  99.3 5.1 %collective-permute-start.24 = (f32[1,1024]{1,0:T(1,128)S(1)}, f32[1,1024]{1,0:T(1,128)S(1)}, u32[]{:S(2)}, u32[]{:S(2)}) collective-permute-start(f32[1,1024]{1,0:T(1,128)S(1)} %multiply_add_fusion.8), channel_id=1, source_target_pairs={{0,64},{16,80},{32,96},{48,112},{64,0},{80,16},{96,32},{112,48},{1... | collective-permute-start | bytes 12296 | tf_op jit(solution)/shard_map/ppermute | solution.py:60
  101.5 2.9 %collective-permute-start.26 = (f32[1,1024]{1,0:T(1,128)S(1)}, f32[1,1024]{1,0:T(1,128)S(1)}, u32[]{:S(2)}, u32[]{:S(2)}) collective-permute-start(f32[1,1024]{1,0:T(1,128)S(1)} %collective-permute-done.25), channel_id=1, source_target_pairs={{0,16},{16,0},{32,48},{48,32},{64,80},{80,64},{96,112},{112,96},{1... | collective-permute-start | bytes 12296 | tf_op jit(solution)/shard_map/ppermute | solution.py:62
  106.2 1.2 collective-permute-start.27
  107.4 4.9 %collective-permute-start.29 = (f32[2,1024]{1,0:T(2,128)S(1)}, f32[2,1024]{1,0:T(2,128)S(1)}, u32[]{:S(2)}, u32[]{:S(2)}) collective-permute-start(f32[2,1024]{1,0:T(2,128)S(1)} %pad_maximum_fusion.1), channel_id=1, source_target_pairs={{0,1},{1,2},{2,3},{3,0},{4,5},{5,6},{6,7},{7,4},{8,9},{9,10},{10,1... | collective-permute-start | bytes 24584 | tf_op jit(solution)/shard_map/ppermute | solution.py:61
  107.5 5.2 %collective-permute-start.28 = (f32[2,1024]{1,0:T(2,128)S(1)}, f32[2,1024]{1,0:T(2,128)S(1)}, u32[]{:S(2)}, u32[]{:S(2)}) collective-permute-start(f32[2,1024]{1,0:T(2,128)S(1)} %pad_maximum_fusion.1), channel_id=1, source_target_pairs={{0,2},{1,3},{2,0},{3,1},{4,6},{5,7},{6,4},{7,5},{8,10},{9,11},{10,... | collective-permute-start | bytes 24584 | tf_op jit(solution)/shard_map/ppermute | solution.py:60
  112.4 1.2 collective-permute-start.30
  113.6 4.9 %collective-permute-start.32 = (f32[2,1024]{1,0:T(2,128)S(1)}, f32[2,1024]{1,0:T(2,128)S(1)}, u32[]{:S(2)}, u32[]{:S(2)}) collective-permute-start(f32[2,1024]{1,0:T(2,128)S(1)} %multiply_add_fusion.3), channel_id=1, source_target_pairs={{0,4},{1,5},{2,6},{3,7},{4,8},{5,9},{6,10},{7,11},{8,12},{9,13},{1... | collective-permute-start | bytes 24584 | tf_op jit(solution)/shard_map/ppermute | solution.py:61
  114.9 5.2 %collective-permute-start.31 = (f32[2,1024]{1,0:T(2,128)S(1)}, f32[2,1024]{1,0:T(2,128)S(1)}, u32[]{:S(2)}, u32[]{:S(2)}) collective-permute-start(f32[2,1024]{1,0:T(2,128)S(1)} %multiply_add_fusion.3), channel_id=1, source_target_pairs={{0,8},{1,9},{2,10},{3,11},{4,12},{5,13},{6,14},{7,15},{8,0},{9,1},... | collective-permute-start | bytes 24584 | tf_op jit(solution)/shard_map/ppermute | solution.py:60
  118.5 1.5 collective-permute-start.33
  121.8 1.2 collective-permute-start.34
  123.1 4.9 %collective-permute-start.36 = (f32[1,1024]{1,0:T(1,128)S(1)}, f32[1,1024]{1,0:T(1,128)S(1)}, u32[]{:S(2)}, u32[]{:S(2)}) collective-permute-start(f32[1,1024]{1,0:T(1,128)S(1)} %multiply_add_fusion.7), channel_id=1, source_target_pairs={{0,32},{16,112},{32,64},{48,16},{64,96},{80,48},{96,0},{112,80},{1... | collective-permute-start | bytes 12296 | tf_op jit(solution)/shard_map/ppermute | solution.py:61
  124.4 5.1 %collective-permute-start.35 = (f32[1,1024]{1,0:T(1,128)S(1)}, f32[1,1024]{1,0:T(1,128)S(1)}, u32[]{:S(2)}, u32[]{:S(2)}) collective-permute-start(f32[1,1024]{1,0:T(1,128)S(1)} %multiply_add_fusion.7), channel_id=1, source_target_pairs={{0,64},{16,80},{32,96},{48,112},{64,0},{80,16},{96,32},{112,48},{1... | collective-permute-start | bytes 12296 | tf_op jit(solution)/shard_map/ppermute | solution.py:60
  128.0 1.6 collective-permute-start.37
  131.3 1.2 collective-permute-start.38
  132.5 4.9 %collective-permute-start.40 = (f32[2,1024]{1,0:T(2,128)S(1)}, f32[2,1024]{1,0:T(2,128)S(1)}, u32[]{:S(2)}, u32[]{:S(2)}) collective-permute-start(f32[2,1024]{1,0:T(2,128)S(1)} %pad_maximum_fusion.2), channel_id=1, source_target_pairs={{0,1},{1,2},{2,3},{3,0},{4,5},{5,6},{6,7},{7,4},{8,9},{9,10},{10,1... | collective-permute-start | bytes 24584 | tf_op jit(solution)/shard_map/ppermute | solution.py:61
  135.1 5.2 %collective-permute-start.39 = (f32[2,1024]{1,0:T(2,128)S(1)}, f32[2,1024]{1,0:T(2,128)S(1)}, u32[]{:S(2)}, u32[]{:S(2)}) collective-permute-start(f32[2,1024]{1,0:T(2,128)S(1)} %pad_maximum_fusion.2), channel_id=1, source_target_pairs={{0,2},{1,3},{2,0},{3,1},{4,6},{5,7},{6,4},{7,5},{8,10},{9,11},{10,... | collective-permute-start | bytes 24584 | tf_op jit(solution)/shard_map/ppermute | solution.py:60
  137.5 2.8 %collective-permute-start.41 = (f32[2,1024]{1,0:T(2,128)S(1)}, f32[2,1024]{1,0:T(2,128)S(1)}, u32[]{:S(2)}, u32[]{:S(2)}) collective-permute-start(f32[2,1024]{1,0:T(2,128)S(1)} %collective-permute-done.40), channel_id=1, source_target_pairs={{0,16},{16,0},{32,48},{48,32},{64,80},{80,64},{96,112},{112,96},{1... | collective-permute-start | bytes 24584 | tf_op jit(solution)/shard_map/ppermute | solution.py:62
  140.4 4.9 %collective-permute-start.43 = (f32[2,1024]{1,0:T(2,128)S(1)}, f32[2,1024]{1,0:T(2,128)S(1)}, u32[]{:S(2)}, u32[]{:S(2)}) collective-permute-start(f32[2,1024]{1,0:T(2,128)S(1)} %multiply_add_fusion.1), channel_id=1, source_target_pairs={{0,4},{1,5},{2,6},{3,7},{4,8},{5,9},{6,10},{7,11},{8,12},{9,13},{1... | collective-permute-start | bytes 24584 | tf_op jit(solution)/shard_map/ppermute | solution.py:61
  141.6 5.2 %collective-permute-start.42 = (f32[2,1024]{1,0:T(2,128)S(1)}, f32[2,1024]{1,0:T(2,128)S(1)}, u32[]{:S(2)}, u32[]{:S(2)}) collective-permute-start(f32[2,1024]{1,0:T(2,128)S(1)} %multiply_add_fusion.1), channel_id=1, source_target_pairs={{0,8},{1,9},{2,10},{3,11},{4,12},{5,13},{6,14},{7,15},{8,0},{9,1},... | collective-permute-start | bytes 24584 | tf_op jit(solution)/shard_map/ppermute | solution.py:60
  145.3 1.5 collective-permute-start.44
  148.5 1.2 collective-permute-start.45
  149.8 4.9 %collective-permute-start.47 = (f32[1,1024]{1,0:T(1,128)S(1)}, f32[1,1024]{1,0:T(1,128)S(1)}, u32[]{:S(2)}, u32[]{:S(2)}) collective-permute-start(f32[1,1024]{1,0:T(1,128)S(1)} %multiply_add_fusion.6), channel_id=1, source_target_pairs={{0,32},{16,112},{32,64},{48,16},{64,96},{80,48},{96,0},{112,80},{1... | collective-permute-start | bytes 12296 | tf_op jit(solution)/shard_map/ppermute | solution.py:61
  150.0 5.1 %collective-permute-start.46 = (f32[1,1024]{1,0:T(1,128)S(1)}, f32[1,1024]{1,0:T(1,128)S(1)}, u32[]{:S(2)}, u32[]{:S(2)}) collective-permute-start(f32[1,1024]{1,0:T(1,128)S(1)} %multiply_add_fusion.6), channel_id=1, source_target_pairs={{0,64},{16,80},{32,96},{48,112},{64,0},{80,16},{96,32},{112,48},{1... | collective-permute-start | bytes 12296 | tf_op jit(solution)/shard_map/ppermute | solution.py:60
  154.7 1.2 collective-permute-start.48
  155.9 7.1 %copy-start = (bf16[1024,512]{1,0:T(8,128)(2,1)S(1)}, bf16[1024,512]{1,0:T(8,128)(2,1)}, u32[]{:S(2)}) copy-start(bf16[1024,512]{1,0:T(8,128)(2,1)} %refs_0_.7) | copy-start | bytes 3145732
  159.7 16.4 %collective-permute-start.49 = (bf16[528,1024]{1,0:T(8,128)(2,1)S(1)}, bf16[528,1024]{1,0:T(8,128)(2,1)S(1)}, u32[]{:S(2)}, u32[]{:S(2)}) collective-permute-start(bf16[528,1024]{1,0:T(8,128)(2,1)S(1)} %get-tuple-element.60), channel_id=1, source_target_pairs={{0,4},{1,5},{2,6},{3,7},{4,8},{5,9},{6,10},{7,11},{8,12},{9,13},{1... | collective-permute-start | bytes 3244040 | tf_op jit(solution)/shard_map/ppermute | solution.py:89
  159.8 16.3 %collective-permute-start.50 = (bf16[528,1024]{1,0:T(8,128)(2,1)S(1)}, bf16[528,1024]{1,0:T(8,128)(2,1)S(1)}, u32[]{:S(2)}, u32[]{:S(2)}) collective-permute-start(bf16[528,1024]{1,0:T(8,128)(2,1)S(1)} %get-tuple-element.61), channel_id=1, source_target_pairs={{0,12},{1,13},{2,14},{3,15},{4,0},{5,1},{6,2},{7,3},{8,4},{9,5},{1... | collective-permute-start | bytes 3244040 | tf_op jit(solution)/shard_map/ppermute | solution.py:89
  167.8 19.5 %collective-permute-start.51 = (bf16[528,1024]{1,0:T(8,128)(2,1)S(1)}, bf16[528,1024]{1,0:T(8,128)(2,1)S(1)}, u32[]{:S(2)}, u32[]{:S(2)}) collective-permute-start(bf16[528,1024]{1,0:T(8,128)(2,1)S(1)} %get-tuple-element.65), channel_id=1, source_target_pairs={{0,12},{1,13},{2,14},{3,15},{4,0},{5,1},{6,2},{7,3},{8,4},{9,5},{1... | collective-permute-start | bytes 3244040 | tf_op jit(solution)/shard_map/ppermute | solution.py:89
  167.9 19.8 %collective-permute-start.52 = (bf16[528,1024]{1,0:T(8,128)(2,1)S(1)}, bf16[528,1024]{1,0:T(8,128)(2,1)S(1)}, u32[]{:S(2)}, u32[]{:S(2)}) collective-permute-start(bf16[528,1024]{1,0:T(8,128)(2,1)S(1)} %get-tuple-element.66), channel_id=1, source_target_pairs={{0,4},{1,5},{2,6},{3,7},{4,8},{5,9},{6,10},{7,11},{8,12},{9,13},{1... | collective-permute-start | bytes 3244040 | tf_op jit(solution)/shard_map/ppermute | solution.py:89
  178.5 20.8 %collective-permute-start.53 = (bf16[528,1024]{1,0:T(8,128)(2,1)S(1)}, bf16[528,1024]{1,0:T(8,128)(2,1)S(1)}, u32[]{:S(2)}, u32[]{:S(2)}) collective-permute-start(bf16[528,1024]{1,0:T(8,128)(2,1)S(1)} %get-tuple-element.62), channel_id=1, source_target_pairs={{0,4},{1,5},{2,6},{3,7},{4,8},{5,9},{6,10},{7,11},{8,12},{9,13},{1... | collective-permute-start | bytes 3244040 | tf_op jit(solution)/shard_map/ppermute | solution.py:89
  179.2 20.1 %collective-permute-start.54 = (bf16[528,1024]{1,0:T(8,128)(2,1)S(1)}, bf16[528,1024]{1,0:T(8,128)(2,1)S(1)}, u32[]{:S(2)}, u32[]{:S(2)}) collective-permute-start(bf16[528,1024]{1,0:T(8,128)(2,1)S(1)} %get-tuple-element.63), channel_id=1, source_target_pairs={{0,12},{1,13},{2,14},{3,15},{4,0},{5,1},{6,2},{7,3},{8,4},{9,5},{1... | collective-permute-start | bytes 3244040 | tf_op jit(solution)/shard_map/ppermute | solution.py:89
  199.8 11.0 %collective-permute-start.55 = (bf16[1040,256]{1,0:T(8,128)(2,1)S(1)}, bf16[1040,256]{1,0:T(8,128)(2,1)S(1)}, u32[]{:S(2)}, u32[]{:S(2)}) collective-permute-start(bf16[1040,256]{1,0:T(8,128)(2,1)S(1)} %get-tuple-element.76), channel_id=1, source_target_pairs={{0,2},{1,3},{2,0},{3,1},{4,6},{5,7},{6,4},{7,5},{8,10},{9,11},{10,... | collective-permute-start | bytes 1597448 | tf_op jit(solution)/shard_map/ppermute | solution.py:85
  201.2 13.2 %collective-permute-start.56 = (bf16[1040,256]{1,0:T(8,128)(2,1)S(1)}, bf16[1040,256]{1,0:T(8,128)(2,1)S(1)}, u32[]{:S(2)}, u32[]{:S(2)}) collective-permute-start(bf16[1040,256]{1,0:T(8,128)(2,1)S(1)} %get-tuple-element.77), channel_id=1, source_target_pairs={{0,3},{1,0},{2,1},{3,2},{4,7},{5,4},{6,5},{7,6},{8,11},{9,8},{10,9... | collective-permute-start | bytes 1597448 | tf_op jit(solution)/shard_map/ppermute | solution.py:85
  202.6 13.7 %collective-permute-start.57 = (bf16[1040,256]{1,0:T(8,128)(2,1)S(1)}, bf16[1040,256]{1,0:T(8,128)(2,1)S(1)}, u32[]{:S(2)}, u32[]{:S(2)}) collective-permute-start(bf16[1040,256]{1,0:T(8,128)(2,1)S(1)} %get-tuple-element.78), channel_id=1, source_target_pairs={{0,1},{1,2},{2,3},{3,0},{4,5},{5,6},{6,7},{7,4},{8,9},{9,10},{10,1... | collective-permute-start | bytes 1597448 | tf_op jit(solution)/shard_map/ppermute | solution.py:85
  (5 other events, 17.6 us)

commit v3 on v1

--- a/solution.py
+++ b/solution.py
@@ -359,7 +359,8 @@
             noise, lat_ref[...], (((1,), (1,)), ((), ())), preferred_element_type=F32
         )
         logits_ref[rows, :] = (cross_ref[rows, :] + cross) * scale
-    steps_of(logits_ref.shape[0], 256, lambda rows: row_lse_block(logits_ref, rows, 0.0, lse_ref))
+        for at in range(start, start + half, 256):
+            row_lse_block(logits_ref, pl.ds(at, 256), 0.0, lse_ref)
 
 
 def far_call(far, lat, cross, scale):

time: 218 us -> 219 us (level)
  transfers between devices with their start and end apart: 58 -> 58, of which waited for: 40 -> 40; matrix products, arithmetic and copies ran while one was open for 0% -> 0% of each run, Pallas kernels for 10% -> 11%
where the time goes in v3:
time: 219 us; the launch traced here: 216 us
  waiting for transfers between devices  100 us (46%)
  starting transfers between devices  71.9 us (33%)
  Pallas kernels  39.6 us (18%)
  local copies, waits for them, and re-layouts  2.55 us (1%)
    ppermute x12, waiting for transfers between devices, hop_s(): return lax.ppermute(value, BOTH, everywhere([shift_x(by), shift_z(by)]))  31.8 us
    ppermute x6, waiting for transfers between devices, hop_f(): return lax.ppermute(value, BOTH, everywhere([shift_z(by), shift_x(by)]))  25.8 us
    ppermute x12, starting transfers between devices, hop_s(): return lax.ppermute(value, BOTH, everywhere([shift_x(by), shift_z(by)]))  22.6 us
    ppermute x9, starting transfers between devices, around(): far = lax.ppermute(value, axis, opposite)  21.3 us
    pallas_call x10, Pallas kernels, in_vmem(): pl.pallas_call(kernel, in_specs=[pl.BlockSpec(memory_space=pltpu.VMEM)] *...  19.7 us
    ppermute x9, waiting for transfers between devices, around(): far = lax.ppermute(value, axis, opposite)  14.2 us
    ppermute x9, waiting for transfers between devices, around(): near = lax.ppermute(value, axis, spread)  12.2 us
    ppermute x9, starting transfers between devices, around(): near = lax.ppermute(value, axis, spread)  10.9 us
  transfers between devices with their start and end apart: 58, of which 40 were waited for; matrix products, arithmetic and copies ran while one was open for 0% of the time, Pallas kernels for 11%

profile of v3, /device:TPU:0, one launch (start us, length us, event | category | flops | bytes accessed | tf_op | source)
XLA Modules:
  0.0 216.3 jit_solution(8111131644060242630)
XLA Ops:
  0.7 1.7 collective-permute-start.4
  2.5 4.0 %collective-permute-start = (bf16[1024,256]{1,0:T(8,128)(2,1)}, bf16[1024,256]{1,0:T(8,128)(2,1)S(1)}, u32[]{:S(2)}, u32[]{:S(2)}) collective-permute-start(bf16[1024,256]{1,0:T(8,128)(2,1)} %refs_0_.5), channel_id=1, source_target_pairs={{0,3},{1,0},{2,1},{3,2},{4,7},{5,4},{6,5},{7,6},{8,11},{9,8},{10,9... | collective-permute-start | bytes 1572872 | tf_op jit(solution)/shard_map/ppermute | solution.py:85
  6.5 1.9 collective-permute-start.2
  8.4 10.8 %collective-permute-done.refs_1_ = bf16[1024,256]{1,0:T(8,128)(2,1)S(1)} collective-permute-done((bf16[1024,256]{1,0:T(8,128)(2,1)}, bf16[1024,256]{1,0:T(8,128)(2,1)S(1)}, u32[]{:S(2)}, u32[]{:S(2)}) %collective-permute-start) | collective-permute-done | bytes 524320 | tf_op jit(solution)/shard_map/ppermute | solution.py:85
  19.1 1.7 collective-permute-start.5
  20.8 1.9 collective-permute-done.1.refs_2_
  22.7 1.4 copy-done.5
  24.1 1.5 halves.1
  25.6 1.6 collective-permute-start.6
  27.3 2.8 %collective-permute-start.12 = (bf16[2048,256]{1,0:T(8,128)(2,1)}, bf16[2048,256]{1,0:T(8,128)(2,1)S(1)}, u32[]{:S(2)}, u32[]{:S(2)}) collective-permute-start(bf16[2048,256]{1,0:T(8,128)(2,1)} %get-tuple-element.47), channel_id=1, source_target_pairs={{0,12},{1,13},{2,14},{3,15},{4,0},{5,1},{6,2},{7,3},{8,4},{9,5},{1... | collective-permute-start | bytes 3145736 | tf_op jit(solution)/shard_map/ppermute | solution.py:89
  30.0 3.2 %collective-permute-start.14 = (bf16[2048,256]{1,0:T(8,128)(2,1)}, bf16[2048,256]{1,0:T(8,128)(2,1)}, u32[]{:S(2)}, u32[]{:S(2)}) collective-permute-start(bf16[2048,256]{1,0:T(8,128)(2,1)} %get-tuple-element.46), channel_id=1, source_target_pairs={{0,12},{1,13},{2,14},{3,15},{4,0},{5,1},{6,2},{7,3},{8,4},{9,5},{1... | collective-permute-start | bytes 3145736 | tf_op jit(solution)/shard_map/ppermute | solution.py:89
  33.3 7.6 %collective-permute-done.5.refs_12_.refs_4_ = bf16[1024,512]{1,0:T(8,128)(2,1)S(1)} collective-permute-done((bf16[1024,512]{1,0:T(8,128)(2,1)}, bf16[1024,512]{1,0:T(8,128)(2,1)S(1)}, u32[]{:S(2)}, u32[]{:S(2)}) %collective-permute-start.5) | collective-permute-done | bytes 1048608 | tf_op jit(solution)/shard_map/ppermute | solution.py:102
  40.9 4.6 %collective-permute-start.15 = (bf16[2048,256]{1,0:T(8,128)(2,1)}, bf16[2048,256]{1,0:T(8,128)(2,1)}, u32[]{:S(2)}, u32[]{:S(2)}) collective-permute-start(bf16[2048,256]{1,0:T(8,128)(2,1)} %get-tuple-element.47), channel_id=1, source_target_pairs={{0,4},{1,5},{2,6},{3,7},{4,8},{5,9},{6,10},{7,11},{8,12},{9,13},{1... | collective-permute-start | bytes 3145736 | tf_op jit(solution)/shard_map/ppermute | solution.py:89
  47.9 6.0 %collective-permute-done.14 = bf16[2048,256]{1,0:T(8,128)(2,1)} collective-permute-done((bf16[2048,256]{1,0:T(8,128)(2,1)}, bf16[2048,256]{1,0:T(8,128)(2,1)}, u32[]{:S(2)}, u32[]{:S(2)}) %collective-permute-start.14) | collective-permute-done | bytes 1048608 | tf_op jit(solution)/shard_map/ppermute | solution.py:89
  55.1 3.9 %collective-permute-done.15 = bf16[2048,256]{1,0:T(8,128)(2,1)} collective-permute-done((bf16[2048,256]{1,0:T(8,128)(2,1)}, bf16[2048,256]{1,0:T(8,128)(2,1)}, u32[]{:S(2)}, u32[]{:S(2)}) %collective-permute-start.15) | collective-permute-done | bytes 1048608 | tf_op jit(solution)/shard_map/ppermute | solution.py:89
  59.0 2.0 collective-permute-start.13
  61.1 9.9 %cross_near.1 = (f32[1024,1024]{1,0:T(8,128)S(1)}, bf16[1024,1024]{1,0:T(8,128)(2,1)S(1)}) custom-call(s32[16]{0:T(128)S(1)} %fusion.6.spot_ref, bf16[1024,256]{1,0:T(8,128)(2,1)} %refs_0_.5, bf16[1024,256]{1,0:T(8,128)(2,1)} %copy-done.6, bf16[1024,256]{1,0:T(8,128)(2,1)} %copy-done.7, bf16[1024,256]{1,0:T(8,128)(2,1)} %copy-done.8, ...), custom_call_target="tpu_custom_call" | custom-call | flops 25769803776 | bytes 18874368 | tf_op jit(solution)/shard_map/cross_near/pallas_call | solution.py:327
  71.0 3.1 %collective-permute-done.13 = bf16[2048,256]{1,0:T(8,128)(2,1)S(1)} collective-permute-done((bf16[2048,256]{1,0:T(8,128)(2,1)}, bf16[2048,256]{1,0:T(8,128)(2,1)S(1)}, u32[]{:S(2)}, u32[]{:S(2)}) %collective-permute-start.13) | collective-permute-done | bytes 1048608 | tf_op jit(solution)/shard_map/ppermute | solution.py:89
  74.0 3.1 %cross_far.1 = (f32[1024,1024]{1,0:T(8,128)S(1)}, f32[1,1024]{1,0:T(1,128)S(1)}) custom-call(bf16[4,512,256]{2,1,0:T(8,128)(2,1)S(1)} %bitcast.16, bf16[4,512,256]{2,1,0:T(8,128)(2,1)S(1)} %bitcast.17, bf16[1024,1024]{1,0:T(8,128)(2,1)S(1)} %get-tuple-element.52.lat_ref, f32[1024,1024]{1,0:T(8,128)S(1)} %get-tuple-element.53.cross_ref), custom_call_target="tpu_custom_call" | custom-call | flops 2147483648 | bytes 8388608 | tf_op jit(solution)/shard_map/cross_far/pallas_call | solution.py:459
  78.4 4.9 %collective-permute-start.17 = (f32[2,1024]{1,0:T(2,128)S(1)}, f32[2,1024]{1,0:T(2,128)S(1)}, u32[]{:S(2)}, u32[]{:S(2)}) collective-permute-start(f32[2,1024]{1,0:T(2,128)S(1)} %pad_maximum_fusion), channel_id=1, source_target_pairs={{0,2},{1,3},{2,0},{3,1},{4,6},{5,7},{6,4},{7,5},{8,10},{9,11},{10,... | collective-permute-start | bytes 24584 | tf_op jit(solution)/shard_map/ppermute | solution.py:60
  83.5 1.5 collective-permute-done.17
  85.1 1.4 collective-permute-start.21
  86.5 3.4 %collective-permute-start.20 = (f32[2,1024]{1,0:T(2,128)S(1)}, f32[2,1024]{1,0:T(2,128)S(1)}, u32[]{:S(2)}, u32[]{:S(2)}) collective-permute-start(f32[2,1024]{1,0:T(2,128)S(1)} %multiply_add_fusion.5), channel_id=1, source_target_pairs={{0,8},{1,9},{2,10},{3,11},{4,12},{5,13},{6,14},{7,15},{8,0},{9,1},... | collective-permute-start | bytes 24584 | tf_op jit(solution)/shard_map/ppermute | solution.py:60
  90.0 1.6 collective-permute-done.20
  91.7 1.7 col_lse.3
  93.3 1.3 collective-permute-start.23
  95.5 2.7 %collective-permute-start.25 = (f32[1,1024]{1,0:T(1,128)S(1)}, f32[1,1024]{1,0:T(1,128)S(1)}, u32[]{:S(2)}, u32[]{:S(2)}) collective-permute-start(f32[1,1024]{1,0:T(1,128)S(1)} %multiply_add_fusion.8), channel_id=1, source_target_pairs={{0,32},{16,112},{32,64},{48,16},{64,96},{80,48},{96,0},{112,80},{1... | collective-permute-start | bytes 12296 | tf_op jit(solution)/shard_map/ppermute | solution.py:61
  98.2 1.5 collective-permute-start.24
  100.4 2.9 %collective-permute-done.24 = f32[1,1024]{1,0:T(1,128)S(1)} collective-permute-done((f32[1,1024]{1,0:T(1,128)S(1)}, f32[1,1024]{1,0:T(1,128)S(1)}, u32[]{:S(2)}, u32[]{:S(2)}) %collective-permute-start.24) | collective-permute-done | bytes 4128 | tf_op jit(solution)/shard_map/ppermute | solution.py:60
  103.3 1.7 row_lse.2
  106.4 2.9 %collective-permute-start.28 = (f32[2,1024]{1,0:T(2,128)S(1)}, f32[2,1024]{1,0:T(2,128)S(1)}, u32[]{:S(2)}, u32[]{:S(2)}) collective-permute-start(f32[2,1024]{1,0:T(2,128)S(1)} %pad_maximum_fusion.1), channel_id=1, source_target_pairs={{0,2},{1,3},{2,0},{3,1},{4,6},{5,7},{6,4},{7,5},{8,10},{9,11},{10,... | collective-permute-start | bytes 24584 | tf_op jit(solution)/shard_map/ppermute | solution.py:60
  109.3 1.9 collective-permute-done.29
  112.5 1.3 collective-permute-start.32
  113.8 1.4 collective-permute-start.31
  115.1 2.2 %collective-permute-done.32 = f32[2,1024]{1,0:T(2,128)S(1)} collective-permute-done((f32[2,1024]{1,0:T(2,128)S(1)}, f32[2,1024]{1,0:T(2,128)S(1)}, u32[]{:S(2)}, u32[]{:S(2)}) %collective-permute-start.32) | collective-permute-done | bytes 8224 | tf_op jit(solution)/shard_map/ppermute | solution.py:61
  117.4 1.5 collective-permute-done.31
  119.0 1.7 col_lse.4
  121.9 1.4 collective-permute-start.36
  123.9 2.9 %collective-permute-done.36 = f32[1,1024]{1,0:T(1,128)S(1)} collective-permute-done((f32[1,1024]{1,0:T(1,128)S(1)}, f32[1,1024]{1,0:T(1,128)S(1)}, u32[]{:S(2)}, u32[]{:S(2)}) %collective-permute-start.36) | collective-permute-done | bytes 4128 | tf_op jit(solution)/shard_map/ppermute | solution.py:61
  126.8 1.6 collective-permute-done.35
  128.5 1.7 row_lse.3
  131.4 2.6 %collective-permute-start.40 = (f32[2,1024]{1,0:T(2,128)S(1)}, f32[2,1024]{1,0:T(2,128)S(1)}, u32[]{:S(2)}, u32[]{:S(2)}) collective-permute-start(f32[2,1024]{1,0:T(2,128)S(1)} %pad_maximum_fusion.2), channel_id=1, source_target_pairs={{0,1},{1,2},{2,3},{3,0},{4,5},{5,6},{6,7},{7,4},{8,9},{9,10},{10,1... | collective-permute-start | bytes 24584 | tf_op jit(solution)/shard_map/ppermute | solution.py:61
  136.3 2.8 %collective-permute-done.39 = f32[2,1024]{1,0:T(2,128)S(1)} collective-permute-done((f32[2,1024]{1,0:T(2,128)S(1)}, f32[2,1024]{1,0:T(2,128)S(1)}, u32[]{:S(2)}, u32[]{:S(2)}) %collective-permute-start.39) | collective-permute-done | bytes 8224 | tf_op jit(solution)/shard_map/ppermute | solution.py:60
  140.5 1.9 collective-permute-start.42
  142.4 1.7 collective-permute-done.43
  144.2 1.5 collective-permute-done.42
  145.7 1.7 col_lse.5
  148.8 3.3 %collective-permute-start.46 = (f32[1,1024]{1,0:T(1,128)S(1)}, f32[1,1024]{1,0:T(1,128)S(1)}, u32[]{:S(2)}, u32[]{:S(2)}) collective-permute-start(f32[1,1024]{1,0:T(1,128)S(1)} %multiply_add_fusion.6), channel_id=1, source_target_pairs={{0,64},{16,80},{32,96},{48,112},{64,0},{80,16},{96,32},{112,48},{1... | collective-permute-start | bytes 12296 | tf_op jit(solution)/shard_map/ppermute | solution.py:60
  152.2 1.4 collective-permute-done.47
  154.8 3.7 %plan.1 = (bf16[1024,1024]{1,0:T(8,128)(2,1)S(1)}, f32[1,1024]{1,0:T(1,128)S(1)}, bf16[528,1024]{1,0:T(8,128)(2,1)S(1)}, bf16[528,1024]{1,0:T(8,128)(2,1)S(1)}) custom-call(f32[1024,1024]{1,0:T(8,128)S(1)} %get-tuple-element.54.logits_ref, f32[1,1024]{1,0:T(1,128)S(1)} %fusion.2.rowpot_ref, f32[1,1024]{1,0:T(1,128)S(1)} %add_subtract_fusion.colpot_ref, ...), custom_call_target="tpu_custom_call" | custom-call | flops 2147483648 | bytes 6299648 | tf_op jit(solution)/shard_map/plan/pallas_call | solution.py:459
  158.7 3.1 %collective-permute-start.50 = (bf16[528,1024]{1,0:T(8,128)(2,1)S(1)}, bf16[528,1024]{1,0:T(8,128)(2,1)S(1)}, u32[]{:S(2)}, u32[]{:S(2)}) collective-permute-start(bf16[528,1024]{1,0:T(8,128)(2,1)S(1)} %get-tuple-element.61), channel_id=1, source_target_pairs={{0,12},{1,13},{2,14},{3,15},{4,0},{5,1},{6,2},{7,3},{8,4},{9,5},{1... | collective-permute-start | bytes 3244040 | tf_op jit(solution)/shard_map/ppermute | solution.py:89
  161.9 4.7 %share.1 = (bf16[528,1024]{1,0:T(8,128)(2,1)S(1)}, bf16[528,1024]{1,0:T(8,128)(2,1)S(1)}, bf16[1024,1024]{1,0:T(8,128)(2,1)S(1)}, bf16[1024,1024]{1,0:T(8,128)(2,1)S(1)}) custom-call(s32[16]{0:T(128)S(1)} %fusion.6.spot_ref, bf16[1024,512]{1,0:T(8,128)(2,1)S(1)} %copy-done, bf16[1024,512]{1,0:T(8,128)(2,1)S(1)} %collective-permute-done.3.refs_9_.refs_1_, ...), custom_call_target="tpu_custom_call" | custom-call | flops 2147483648 | bytes 2101248 | tf_op jit(solution)/shard_map/share/pallas_call | solution.py:491
  166.8 1.9 collective-permute-start.52
  168.7 6.3 %collective-permute-done.49.top_more = bf16[528,1024]{1,0:T(8,128)(2,1)S(1)} collective-permute-done((bf16[528,1024]{1,0:T(8,128)(2,1)S(1)}, bf16[528,1024]{1,0:T(8,128)(2,1)S(1)}, u32[]{:S(2)}, u32[]{:S(2)}) %collective-permute-start.49) | collective-permute-done | bytes 1081376 | tf_op jit(solution)/shard_map/ppermute | solution.py:89
  175.0 2.9 %onward.1 = (bf16[528,1024]{1,0:T(8,128)(2,1)S(1)}, bf16[528,1024]{1,0:T(8,128)(2,1)S(1)}) custom-call(bf16[1024,1024]{1,0:T(8,128)(2,1)S(1)} %get-tuple-element.64.refs_8_.plan_ref, bf16[1024,1024]{1,0:T(8,128)(2,1)S(1)} %get-tuple-element.58.after_ref, bf16[1024,1024]{1,0:T(8,128)(2,1)S(1)} %get-tuple-element.59.before_ref, ...), custom_call_target="tpu_custom_call" | custom-call | flops 2147483648 | bytes 8458240 | tf_op jit(solution)/shard_map/onward/pallas_call | solution.py:459
  178.7 2.6 %collective-permute-start.54 = (bf16[528,1024]{1,0:T(8,128)(2,1)S(1)}, bf16[528,1024]{1,0:T(8,128)(2,1)S(1)}, u32[]{:S(2)}, u32[]{:S(2)}) collective-permute-start(bf16[528,1024]{1,0:T(8,128)(2,1)S(1)} %get-tuple-element.63), channel_id=1, source_target_pairs={{0,12},{1,13},{2,14},{3,15},{4,0},{5,1},{6,2},{7,3},{8,4},{9,5},{1... | collective-permute-start | bytes 3244040 | tf_op jit(solution)/shard_map/ppermute | solution.py:89
  181.3 4.8 %collective-permute-done.51.refs_10_ = bf16[528,1024]{1,0:T(8,128)(2,1)S(1)} collective-permute-done((bf16[528,1024]{1,0:T(8,128)(2,1)S(1)}, bf16[528,1024]{1,0:T(8,128)(2,1)S(1)}, u32[]{:S(2)}, u32[]{:S(2)}) %collective-permute-start.51) | collective-permute-done | bytes 1081376 | tf_op jit(solution)/shard_map/ppermute | solution.py:89
  186.6 3.8 %own.1 = (f32[1024,1024]{1,0:T(8,128)S(1)}, f32[1,1024]{1,0:T(1,128)S(1)}) custom-call(s32[16]{0:T(128)S(1)} %fusion.6.spot_ref, bf16[1024,512]{1,0:T(8,128)(2,1)S(1)} %copy-done, bf16[1024,512]{1,0:T(8,128)(2,1)S(1)} %collective-permute-done.3.refs_9_.refs_1_, bf16[1024,512]{1,0:T(8,128)(2,1)S(1)} %copy-done.2, ...), custom_call_target="tpu_custom_call" | custom-call | flops 2147483648 | bytes 4263936 | tf_op jit(solution)/shard_map/own/pallas_call | solution.py:491
  191.0 7.1 %collective-permute-done.53.top_ref = bf16[528,1024]{1,0:T(8,128)(2,1)S(1)} collective-permute-done((bf16[528,1024]{1,0:T(8,128)(2,1)S(1)}, bf16[528,1024]{1,0:T(8,128)(2,1)S(1)}, u32[]{:S(2)}, u32[]{:S(2)}) %collective-permute-start.53) | collective-permute-done | bytes 1081376 | tf_op jit(solution)/shard_map/ppermute | solution.py:89
  198.7 1.4 collective-permute-start.55
  200.0 1.5 collective-permute-start.56
  202.1 7.5 %collective-permute-done.55.refs_0_ = bf16[1040,256]{1,0:T(8,128)(2,1)S(1)} collective-permute-done((bf16[1040,256]{1,0:T(8,128)(2,1)S(1)}, bf16[1040,256]{1,0:T(8,128)(2,1)S(1)}, u32[]{:S(2)}, u32[]{:S(2)}) %collective-permute-start.55) | collective-permute-done | bytes 532512 | tf_op jit(solution)/shard_map/ppermute | solution.py:85
  209.6 3.7 %collective-permute-done.56.refs_1_ = bf16[1040,256]{1,0:T(8,128)(2,1)S(1)} collective-permute-done((bf16[1040,256]{1,0:T(8,128)(2,1)S(1)}, bf16[1040,256]{1,0:T(8,128)(2,1)S(1)}, u32[]{:S(2)}, u32[]{:S(2)}) %collective-permute-start.56) | collective-permute-done | bytes 532512 | tf_op jit(solution)/shard_map/ppermute | solution.py:85
  213.3 1.9 collective-permute-done.57.refs_2_
  (115 shorter events, 23.6 us)
Async XLA Ops:
  0.6 22.1 %collective-permute-start.3 = (bf16[1024,512]{1,0:T(8,128)(2,1)}, bf16[1024,512]{1,0:T(8,128)(2,1)S(1)}, u32[]{:S(2)}, u32[]{:S(2)}) collective-permute-start(bf16[1024,512]{1,0:T(8,128)(2,1)} %refs_0_.7), channel_id=1, source_target_pairs={{0,16},{16,0},{32,48},{48,32},{64,80},{80,64},{96,112},{112,96},{1... | collective-permute-start | bytes 3145736 | tf_op jit(solution)/shard_map/ppermute | solution.py:95
  0.7 24.9 %collective-permute-start.4 = (bf16[1024,512]{1,0:T(8,128)(2,1)}, bf16[1024,512]{1,0:T(8,128)(2,1)S(1)}, u32[]{:S(2)}, u32[]{:S(2)}) collective-permute-start(bf16[1024,512]{1,0:T(8,128)(2,1)} %refs_0_.7), channel_id=1, source_target_pairs={{0,32},{16,112},{32,64},{48,16},{64,96},{80,48},{96,0},{112,80},{1... | collective-permute-start | bytes 3145736 | tf_op jit(solution)/shard_map/ppermute | solution.py:101
  2.5 16.7 %collective-permute-start = (bf16[1024,256]{1,0:T(8,128)(2,1)}, bf16[1024,256]{1,0:T(8,128)(2,1)S(1)}, u32[]{:S(2)}, u32[]{:S(2)}) collective-permute-start(bf16[1024,256]{1,0:T(8,128)(2,1)} %refs_0_.5), channel_id=1, source_target_pairs={{0,3},{1,0},{2,1},{3,2},{4,7},{5,4},{6,5},{7,6},{8,11},{9,8},{10,9... | collective-permute-start | bytes 1572872 | tf_op jit(solution)/shard_map/ppermute | solution.py:85
  6.5 16.2 %collective-permute-start.1 = (bf16[1024,256]{1,0:T(8,128)(2,1)}, bf16[1024,256]{1,0:T(8,128)(2,1)S(1)}, u32[]{:S(2)}, u32[]{:S(2)}) collective-permute-start(bf16[1024,256]{1,0:T(8,128)(2,1)} %refs_0_.5), channel_id=1, source_target_pairs={{0,1},{1,2},{2,3},{3,0},{4,5},{5,6},{6,7},{7,4},{8,9},{9,10},{10,1... | collective-permute-start | bytes 1572872 | tf_op jit(solution)/shard_map/ppermute | solution.py:85
  6.5 16.2 %collective-permute-start.2 = (bf16[1024,256]{1,0:T(8,128)(2,1)}, bf16[1024,256]{1,0:T(8,128)(2,1)S(1)}, u32[]{:S(2)}, u32[]{:S(2)}) collective-permute-start(bf16[1024,256]{1,0:T(8,128)(2,1)} %refs_0_.5), channel_id=1, source_target_pairs={{0,2},{1,3},{2,0},{3,1},{4,6},{5,7},{6,4},{7,5},{8,10},{9,11},{10,... | collective-permute-start | bytes 1572872 | tf_op jit(solution)/shard_map/ppermute | solution.py:85
  19.1 26.5 %copy-start.6 = (bf16[1024,256]{1,0:T(8,128)(2,1)}, bf16[1024,256]{1,0:T(8,128)(2,1)S(1)}, u32[]{:S(2)}) copy-start(bf16[1024,256]{1,0:T(8,128)(2,1)S(1)} %collective-permute-done.refs_1_) | copy-start | bytes 1572868
  19.1 21.8 %collective-permute-start.5 = (bf16[1024,512]{1,0:T(8,128)(2,1)}, bf16[1024,512]{1,0:T(8,128)(2,1)S(1)}, u32[]{:S(2)}, u32[]{:S(2)}) collective-permute-start(bf16[1024,512]{1,0:T(8,128)(2,1)} %refs_0_.7), channel_id=1, source_target_pairs={{32,0},{112,16},{64,32},{16,48},{96,64},{48,80},{0,96},{80,112},{3... | collective-permute-start | bytes 3145736 | tf_op jit(solution)/shard_map/ppermute | solution.py:102
  22.7 22.9 %copy-start.7 = (bf16[1024,256]{1,0:T(8,128)(2,1)}, bf16[1024,256]{1,0:T(8,128)(2,1)S(1)}, u32[]{:S(2)}) copy-start(bf16[1024,256]{1,0:T(8,128)(2,1)S(1)} %collective-permute-done.1.refs_2_) | copy-start | bytes 1572868
  22.7 23.4 %copy-start.8 = (bf16[1024,256]{1,0:T(8,128)(2,1)}, bf16[1024,256]{1,0:T(8,128)(2,1)S(1)}, u32[]{:S(2)}) copy-start(bf16[1024,256]{1,0:T(8,128)(2,1)S(1)} %collective-permute-done.2.refs_3_) | copy-start | bytes 1572868
  25.6 35.4 %copy-start.1 = (bf16[1024,512]{1,0:T(8,128)(2,1)}, bf16[1024,512]{1,0:T(8,128)(2,1)S(1)}, u32[]{:S(2)}) copy-start(bf16[1024,512]{1,0:T(8,128)(2,1)S(1)} %collective-permute-done.4.refs_10_.refs_2_) | copy-start | bytes 3145732
  25.6 19.9 %collective-permute-start.6 = (bf16[1024,512]{1,0:T(8,128)(2,1)S(1)}, bf16[1024,512]{1,0:T(8,128)(2,1)}, u32[]{:S(2)}, u32[]{:S(2)}) collective-permute-start(bf16[1024,512]{1,0:T(8,128)(2,1)S(1)} %collective-permute-done.4.refs_10_.refs_2_), channel_id=1, source_target_pairs={{0,32},{16,112},{32,64},{48,16},{64,96},{80,48},{96,0},{112,80},{1... | collective-permute-start | bytes 3145736 | tf_op jit(solution)/shard_map/ppermute | solution.py:105
  27.3 18.3 %collective-permute-start.12 = (bf16[2048,256]{1,0:T(8,128)(2,1)}, bf16[2048,256]{1,0:T(8,128)(2,1)S(1)}, u32[]{:S(2)}, u32[]{:S(2)}) collective-permute-start(bf16[2048,256]{1,0:T(8,128)(2,1)} %get-tuple-element.47), channel_id=1, source_target_pairs={{0,12},{1,13},{2,14},{3,15},{4,0},{5,1},{6,2},{7,3},{8,4},{9,5},{1... | collective-permute-start | bytes 3145736 | tf_op jit(solution)/shard_map/ppermute | solution.py:89
  30.0 16.2 %collective-permute-start.10 = (bf16[2048,256]{1,0:T(8,128)(2,1)}, bf16[2048,256]{1,0:T(8,128)(2,1)S(1)}, u32[]{:S(2)}, u32[]{:S(2)}) collective-permute-start(bf16[2048,256]{1,0:T(8,128)(2,1)} %get-tuple-element.46), channel_id=1, source_target_pairs={{0,4},{1,5},{2,6},{3,7},{4,8},{5,9},{6,10},{7,11},{8,12},{9,13},{1... | collective-permute-start | bytes 3145736 | tf_op jit(solution)/shard_map/ppermute | solution.py:89
  30.0 23.9 %collective-permute-start.14 = (bf16[2048,256]{1,0:T(8,128)(2,1)}, bf16[2048,256]{1,0:T(8,128)(2,1)}, u32[]{:S(2)}, u32[]{:S(2)}) collective-permute-start(bf16[2048,256]{1,0:T(8,128)(2,1)} %get-tuple-element.46), channel_id=1, source_target_pairs={{0,12},{1,13},{2,14},{3,15},{4,0},{5,1},{6,2},{7,3},{8,4},{9,5},{1... | collective-permute-start | bytes 3145736 | tf_op jit(solution)/shard_map/ppermute | solution.py:89
  40.9 20.1 %copy-start.3 = (bf16[1024,512]{1,0:T(8,128)(2,1)}, bf16[1024,512]{1,0:T(8,128)(2,1)S(1)}, u32[]{:S(2)}) copy-start(bf16[1024,512]{1,0:T(8,128)(2,1)S(1)} %collective-permute-done.5.refs_12_.refs_4_) | copy-start | bytes 3145732
  40.9 18.1 %collective-permute-start.15 = (bf16[2048,256]{1,0:T(8,128)(2,1)}, bf16[2048,256]{1,0:T(8,128)(2,1)}, u32[]{:S(2)}, u32[]{:S(2)}) collective-permute-start(bf16[2048,256]{1,0:T(8,128)(2,1)} %get-tuple-element.47), channel_id=1, source_target_pairs={{0,4},{1,5},{2,6},{3,7},{4,8},{5,9},{6,10},{7,11},{8,12},{9,13},{1... | collective-permute-start | bytes 3145736 | tf_op jit(solution)/shard_map/ppermute | solution.py:89
  45.5 15.5 %collective-permute-start.7 = (bf16[1024,512]{1,0:T(8,128)(2,1)S(1)}, bf16[1024,512]{1,0:T(8,128)(2,1)}, u32[]{:S(2)}, u32[]{:S(2)}) collective-permute-start(bf16[1024,512]{1,0:T(8,128)(2,1)S(1)} %collective-permute-done.4.refs_10_.refs_2_), channel_id=1, source_target_pairs={{0,16},{16,0},{32,48},{48,32},{64,80},{80,64},{96,112},{112,96},{1... | collective-permute-start | bytes 3145736 | tf_op jit(solution)/shard_map/ppermute | solution.py:95
  45.6 15.4 %collective-permute-start.8 = (bf16[1024,512]{1,0:T(8,128)(2,1)S(1)}, bf16[1024,512]{1,0:T(8,128)(2,1)}, u32[]{:S(2)}, u32[]{:S(2)}) collective-permute-start(bf16[1024,512]{1,0:T(8,128)(2,1)S(1)} %collective-permute-done.5.refs_12_.refs_4_), channel_id=1, source_target_pairs={{0,16},{16,0},{32,48},{48,32},{64,80},{80,64},{96,112},{112,96},{1... | collective-permute-start | bytes 3145736 | tf_op jit(solution)/shard_map/ppermute | solution.py:95
  46.6 14.5 %collective-permute-start.9 = (bf16[1024,512]{1,0:T(8,128)(2,1)}, bf16[1024,512]{1,0:T(8,128)(2,1)}, u32[]{:S(2)}, u32[]{:S(2)}) collective-permute-start(bf16[1024,512]{1,0:T(8,128)(2,1)} %collective-permute-done.6.refs_14_.refs_6_), channel_id=1, source_target_pairs={{0,16},{16,0},{32,48},{48,32},{64,80},{80,64},{96,112},{112,96},{1... | collective-permute-start | bytes 3145736 | tf_op jit(solution)/shard_map/ppermute | solution.py:95
  53.9 17.0 %collective-permute-start.11 = (bf16[2048,256]{1,0:T(8,128)(2,1)}, bf16[2048,256]{1,0:T(8,128)(2,1)S(1)}, u32[]{:S(2)}, u32[]{:S(2)}) collective-permute-start(bf16[2048,256]{1,0:T(8,128)(2,1)} %copy-done.10), channel_id=1, source_target_pairs={{0,4},{1,5},{2,6},{3,7},{4,8},{5,9},{6,10},{7,11},{8,12},{9,13},{1... | collective-permute-start | bytes 3145736 | tf_op jit(solution)/shard_map/ppermute | solution.py:89
  59.0 15.0 %collective-permute-start.13 = (bf16[2048,256]{1,0:T(8,128)(2,1)}, bf16[2048,256]{1,0:T(8,128)(2,1)S(1)}, u32[]{:S(2)}, u32[]{:S(2)}) collective-permute-start(bf16[2048,256]{1,0:T(8,128)(2,1)} %copy-done.9), channel_id=1, source_target_pairs={{0,12},{1,13},{2,14},{3,15},{4,0},{5,1},{6,2},{7,3},{8,4},{9,5},{1... | collective-permute-start | bytes 3145736 | tf_op jit(solution)/shard_map/ppermute | solution.py:89
  77.1 1.2 collective-permute-start.16
  78.4 5.1 %collective-permute-start.18 = (f32[2,1024]{1,0:T(2,128)S(1)}, f32[2,1024]{1,0:T(2,128)S(1)}, u32[]{:S(2)}, u32[]{:S(2)}) collective-permute-start(f32[2,1024]{1,0:T(2,128)S(1)} %pad_maximum_fusion), channel_id=1, source_target_pairs={{0,1},{1,2},{2,3},{3,0},{4,5},{5,6},{6,7},{7,4},{8,9},{9,10},{10,1... | collective-permute-start | bytes 24584 | tf_op jit(solution)/shard_map/ppermute | solution.py:61
  78.4 6.6 %collective-permute-start.17 = (f32[2,1024]{1,0:T(2,128)S(1)}, f32[2,1024]{1,0:T(2,128)S(1)}, u32[]{:S(2)}, u32[]{:S(2)}) collective-permute-start(f32[2,1024]{1,0:T(2,128)S(1)} %pad_maximum_fusion), channel_id=1, source_target_pairs={{0,2},{1,3},{2,0},{3,1},{4,6},{5,7},{6,4},{7,5},{8,10},{9,11},{10,... | collective-permute-start | bytes 24584 | tf_op jit(solution)/shard_map/ppermute | solution.py:60
  83.5 1.5 collective-permute-start.19
  85.1 4.9 %collective-permute-start.21 = (f32[2,1024]{1,0:T(2,128)S(1)}, f32[2,1024]{1,0:T(2,128)S(1)}, u32[]{:S(2)}, u32[]{:S(2)}) collective-permute-start(f32[2,1024]{1,0:T(2,128)S(1)} %multiply_add_fusion.5), channel_id=1, source_target_pairs={{0,4},{1,5},{2,6},{3,7},{4,8},{5,9},{6,10},{7,11},{8,12},{9,13},{1... | collective-permute-start | bytes 24584 | tf_op jit(solution)/shard_map/ppermute | solution.py:61
  86.5 5.2 %collective-permute-start.20 = (f32[2,1024]{1,0:T(2,128)S(1)}, f32[2,1024]{1,0:T(2,128)S(1)}, u32[]{:S(2)}, u32[]{:S(2)}) collective-permute-start(f32[2,1024]{1,0:T(2,128)S(1)} %multiply_add_fusion.5), channel_id=1, source_target_pairs={{0,8},{1,9},{2,10},{3,11},{4,12},{5,13},{6,14},{7,15},{8,0},{9,1},... | collective-permute-start | bytes 24584 | tf_op jit(solution)/shard_map/ppermute | solution.py:60
  90.0 1.6 collective-permute-start.22
  93.3 2.1 collective-permute-start.23
  95.5 4.9 %collective-permute-start.25 = (f32[1,1024]{1,0:T(1,128)S(1)}, f32[1,1024]{1,0:T(1,128)S(1)}, u32[]{:S(2)}, u32[]{:S(2)}) collective-permute-start(f32[1,1024]{1,0:T(1,128)S(1)} %multiply_add_fusion.8), channel_id=1, source_target_pairs={{0,32},{16,112},{32,64},{48,16},{64,96},{80,48},{96,0},{112,80},{1... | collective-permute-start | bytes 12296 | tf_op jit(solution)/shard_map/ppermute | solution.py:61
  98.2 5.1 %collective-permute-start.24 = (f32[1,1024]{1,0:T(1,128)S(1)}, f32[1,1024]{1,0:T(1,128)S(1)}, u32[]{:S(2)}, u32[]{:S(2)}) collective-permute-start(f32[1,1024]{1,0:T(1,128)S(1)} %multiply_add_fusion.8), channel_id=1, source_target_pairs={{0,64},{16,80},{32,96},{48,112},{64,0},{80,16},{96,32},{112,48},{1... | collective-permute-start | bytes 12296 | tf_op jit(solution)/shard_map/ppermute | solution.py:60
  100.4 2.9 %collective-permute-start.26 = (f32[1,1024]{1,0:T(1,128)S(1)}, f32[1,1024]{1,0:T(1,128)S(1)}, u32[]{:S(2)}, u32[]{:S(2)}) collective-permute-start(f32[1,1024]{1,0:T(1,128)S(1)} %collective-permute-done.25), channel_id=1, source_target_pairs={{0,16},{16,0},{32,48},{48,32},{64,80},{80,64},{96,112},{112,96},{1... | collective-permute-start | bytes 12296 | tf_op jit(solution)/shard_map/ppermute | solution.py:62
  105.0 1.2 collective-permute-start.27
  106.3 4.9 %collective-permute-start.29 = (f32[2,1024]{1,0:T(2,128)S(1)}, f32[2,1024]{1,0:T(2,128)S(1)}, u32[]{:S(2)}, u32[]{:S(2)}) collective-permute-start(f32[2,1024]{1,0:T(2,128)S(1)} %pad_maximum_fusion.1), channel_id=1, source_target_pairs={{0,1},{1,2},{2,3},{3,0},{4,5},{5,6},{6,7},{7,4},{8,9},{9,10},{10,1... | collective-permute-start | bytes 24584 | tf_op jit(solution)/shard_map/ppermute | solution.py:61
  106.4 5.2 %collective-permute-start.28 = (f32[2,1024]{1,0:T(2,128)S(1)}, f32[2,1024]{1,0:T(2,128)S(1)}, u32[]{:S(2)}, u32[]{:S(2)}) collective-permute-start(f32[2,1024]{1,0:T(2,128)S(1)} %pad_maximum_fusion.1), channel_id=1, source_target_pairs={{0,2},{1,3},{2,0},{3,1},{4,6},{5,7},{6,4},{7,5},{8,10},{9,11},{10,... | collective-permute-start | bytes 24584 | tf_op jit(solution)/shard_map/ppermute | solution.py:60
  111.2 1.2 collective-permute-start.30
  112.5 4.9 %collective-permute-start.32 = (f32[2,1024]{1,0:T(2,128)S(1)}, f32[2,1024]{1,0:T(2,128)S(1)}, u32[]{:S(2)}, u32[]{:S(2)}) collective-permute-start(f32[2,1024]{1,0:T(2,128)S(1)} %multiply_add_fusion.3), channel_id=1, source_target_pairs={{0,4},{1,5},{2,6},{3,7},{4,8},{5,9},{6,10},{7,11},{8,12},{9,13},{1... | collective-permute-start | bytes 24584 | tf_op jit(solution)/shard_map/ppermute | solution.py:61
  113.8 5.2 %collective-permute-start.31 = (f32[2,1024]{1,0:T(2,128)S(1)}, f32[2,1024]{1,0:T(2,128)S(1)}, u32[]{:S(2)}, u32[]{:S(2)}) collective-permute-start(f32[2,1024]{1,0:T(2,128)S(1)} %multiply_add_fusion.3), channel_id=1, source_target_pairs={{0,8},{1,9},{2,10},{3,11},{4,12},{5,13},{6,14},{7,15},{8,0},{9,1},... | collective-permute-start | bytes 24584 | tf_op jit(solution)/shard_map/ppermute | solution.py:60
  117.4 1.5 collective-permute-start.33
  120.7 1.2 collective-permute-start.34
  121.9 4.9 %collective-permute-start.36 = (f32[1,1024]{1,0:T(1,128)S(1)}, f32[1,1024]{1,0:T(1,128)S(1)}, u32[]{:S(2)}, u32[]{:S(2)}) collective-permute-start(f32[1,1024]{1,0:T(1,128)S(1)} %multiply_add_fusion.7), channel_id=1, source_target_pairs={{0,32},{16,112},{32,64},{48,16},{64,96},{80,48},{96,0},{112,80},{1... | collective-permute-start | bytes 12296 | tf_op jit(solution)/shard_map/ppermute | solution.py:61
  123.3 5.1 %collective-permute-start.35 = (f32[1,1024]{1,0:T(1,128)S(1)}, f32[1,1024]{1,0:T(1,128)S(1)}, u32[]{:S(2)}, u32[]{:S(2)}) collective-permute-start(f32[1,1024]{1,0:T(1,128)S(1)} %multiply_add_fusion.7), channel_id=1, source_target_pairs={{0,64},{16,80},{32,96},{48,112},{64,0},{80,16},{96,32},{112,48},{1... | collective-permute-start | bytes 12296 | tf_op jit(solution)/shard_map/ppermute | solution.py:60
  126.8 1.6 collective-permute-start.37
  130.1 1.2 collective-permute-start.38
  131.4 4.9 %collective-permute-start.40 = (f32[2,1024]{1,0:T(2,128)S(1)}, f32[2,1024]{1,0:T(2,128)S(1)}, u32[]{:S(2)}, u32[]{:S(2)}) collective-permute-start(f32[2,1024]{1,0:T(2,128)S(1)} %pad_maximum_fusion.2), channel_id=1, source_target_pairs={{0,1},{1,2},{2,3},{3,0},{4,5},{5,6},{6,7},{7,4},{8,9},{9,10},{10,1... | collective-permute-start | bytes 24584 | tf_op jit(solution)/shard_map/ppermute | solution.py:61
  134.0 5.2 %collective-permute-start.39 = (f32[2,1024]{1,0:T(2,128)S(1)}, f32[2,1024]{1,0:T(2,128)S(1)}, u32[]{:S(2)}, u32[]{:S(2)}) collective-permute-start(f32[2,1024]{1,0:T(2,128)S(1)} %pad_maximum_fusion.2), channel_id=1, source_target_pairs={{0,2},{1,3},{2,0},{3,1},{4,6},{5,7},{6,4},{7,5},{8,10},{9,11},{10,... | collective-permute-start | bytes 24584 | tf_op jit(solution)/shard_map/ppermute | solution.py:60
  136.3 2.8 %collective-permute-start.41 = (f32[2,1024]{1,0:T(2,128)S(1)}, f32[2,1024]{1,0:T(2,128)S(1)}, u32[]{:S(2)}, u32[]{:S(2)}) collective-permute-start(f32[2,1024]{1,0:T(2,128)S(1)} %collective-permute-done.40), channel_id=1, source_target_pairs={{0,16},{16,0},{32,48},{48,32},{64,80},{80,64},{96,112},{112,96},{1... | collective-permute-start | bytes 24584 | tf_op jit(solution)/shard_map/ppermute | solution.py:62
  139.2 4.9 %collective-permute-start.43 = (f32[2,1024]{1,0:T(2,128)S(1)}, f32[2,1024]{1,0:T(2,128)S(1)}, u32[]{:S(2)}, u32[]{:S(2)}) collective-permute-start(f32[2,1024]{1,0:T(2,128)S(1)} %multiply_add_fusion.1), channel_id=1, source_target_pairs={{0,4},{1,5},{2,6},{3,7},{4,8},{5,9},{6,10},{7,11},{8,12},{9,13},{1... | collective-permute-start | bytes 24584 | tf_op jit(solution)/shard_map/ppermute | solution.py:61
  140.5 5.2 %collective-permute-start.42 = (f32[2,1024]{1,0:T(2,128)S(1)}, f32[2,1024]{1,0:T(2,128)S(1)}, u32[]{:S(2)}, u32[]{:S(2)}) collective-permute-start(f32[2,1024]{1,0:T(2,128)S(1)} %multiply_add_fusion.1), channel_id=1, source_target_pairs={{0,8},{1,9},{2,10},{3,11},{4,12},{5,13},{6,14},{7,15},{8,0},{9,1},... | collective-permute-start | bytes 24584 | tf_op jit(solution)/shard_map/ppermute | solution.py:60
  144.2 1.5 collective-permute-start.44
  147.4 1.2 collective-permute-start.45
  148.7 4.9 %collective-permute-start.47 = (f32[1,1024]{1,0:T(1,128)S(1)}, f32[1,1024]{1,0:T(1,128)S(1)}, u32[]{:S(2)}, u32[]{:S(2)}) collective-permute-start(f32[1,1024]{1,0:T(1,128)S(1)} %multiply_add_fusion.6), channel_id=1, source_target_pairs={{0,32},{16,112},{32,64},{48,16},{64,96},{80,48},{96,0},{112,80},{1... | collective-permute-start | bytes 12296 | tf_op jit(solution)/shard_map/ppermute | solution.py:61
  148.8 5.1 %collective-permute-start.46 = (f32[1,1024]{1,0:T(1,128)S(1)}, f32[1,1024]{1,0:T(1,128)S(1)}, u32[]{:S(2)}, u32[]{:S(2)}) collective-permute-start(f32[1,1024]{1,0:T(1,128)S(1)} %multiply_add_fusion.6), channel_id=1, source_target_pairs={{0,64},{16,80},{32,96},{48,112},{64,0},{80,16},{96,32},{112,48},{1... | collective-permute-start | bytes 12296 | tf_op jit(solution)/shard_map/ppermute | solution.py:60
  153.5 1.2 collective-permute-start.48
  154.8 7.1 %copy-start = (bf16[1024,512]{1,0:T(8,128)(2,1)S(1)}, bf16[1024,512]{1,0:T(8,128)(2,1)}, u32[]{:S(2)}) copy-start(bf16[1024,512]{1,0:T(8,128)(2,1)} %refs_0_.7) | copy-start | bytes 3145732
  158.6 16.4 %collective-permute-start.49 = (bf16[528,1024]{1,0:T(8,128)(2,1)S(1)}, bf16[528,1024]{1,0:T(8,128)(2,1)S(1)}, u32[]{:S(2)}, u32[]{:S(2)}) collective-permute-start(bf16[528,1024]{1,0:T(8,128)(2,1)S(1)} %get-tuple-element.60), channel_id=1, source_target_pairs={{0,4},{1,5},{2,6},{3,7},{4,8},{5,9},{6,10},{7,11},{8,12},{9,13},{1... | collective-permute-start | bytes 3244040 | tf_op jit(solution)/shard_map/ppermute | solution.py:89
  158.7 16.3 %collective-permute-start.50 = (bf16[528,1024]{1,0:T(8,128)(2,1)S(1)}, bf16[528,1024]{1,0:T(8,128)(2,1)S(1)}, u32[]{:S(2)}, u32[]{:S(2)}) collective-permute-start(bf16[528,1024]{1,0:T(8,128)(2,1)S(1)} %get-tuple-element.61), channel_id=1, source_target_pairs={{0,12},{1,13},{2,14},{3,15},{4,0},{5,1},{6,2},{7,3},{8,4},{9,5},{1... | collective-permute-start | bytes 3244040 | tf_op jit(solution)/shard_map/ppermute | solution.py:89
  166.6 19.5 %collective-permute-start.51 = (bf16[528,1024]{1,0:T(8,128)(2,1)S(1)}, bf16[528,1024]{1,0:T(8,128)(2,1)S(1)}, u32[]{:S(2)}, u32[]{:S(2)}) collective-permute-start(bf16[528,1024]{1,0:T(8,128)(2,1)S(1)} %get-tuple-element.65), channel_id=1, source_target_pairs={{0,12},{1,13},{2,14},{3,15},{4,0},{5,1},{6,2},{7,3},{8,4},{9,5},{1... | collective-permute-start | bytes 3244040 | tf_op jit(solution)/shard_map/ppermute | solution.py:89
  166.8 19.8 %collective-permute-start.52 = (bf16[528,1024]{1,0:T(8,128)(2,1)S(1)}, bf16[528,1024]{1,0:T(8,128)(2,1)S(1)}, u32[]{:S(2)}, u32[]{:S(2)}) collective-permute-start(bf16[528,1024]{1,0:T(8,128)(2,1)S(1)} %get-tuple-element.66), channel_id=1, source_target_pairs={{0,4},{1,5},{2,6},{3,7},{4,8},{5,9},{6,10},{7,11},{8,12},{9,13},{1... | collective-permute-start | bytes 3244040 | tf_op jit(solution)/shard_map/ppermute | solution.py:89
  177.9 20.2 %collective-permute-start.53 = (bf16[528,1024]{1,0:T(8,128)(2,1)S(1)}, bf16[528,1024]{1,0:T(8,128)(2,1)S(1)}, u32[]{:S(2)}, u32[]{:S(2)}) collective-permute-start(bf16[528,1024]{1,0:T(8,128)(2,1)S(1)} %get-tuple-element.62), channel_id=1, source_target_pairs={{0,4},{1,5},{2,6},{3,7},{4,8},{5,9},{6,10},{7,11},{8,12},{9,13},{1... | collective-permute-start | bytes 3244040 | tf_op jit(solution)/shard_map/ppermute | solution.py:89
  178.7 19.5 %collective-permute-start.54 = (bf16[528,1024]{1,0:T(8,128)(2,1)S(1)}, bf16[528,1024]{1,0:T(8,128)(2,1)S(1)}, u32[]{:S(2)}, u32[]{:S(2)}) collective-permute-start(bf16[528,1024]{1,0:T(8,128)(2,1)S(1)} %get-tuple-element.63), channel_id=1, source_target_pairs={{0,12},{1,13},{2,14},{3,15},{4,0},{5,1},{6,2},{7,3},{8,4},{9,5},{1... | collective-permute-start | bytes 3244040 | tf_op jit(solution)/shard_map/ppermute | solution.py:89
  198.7 11.0 %collective-permute-start.55 = (bf16[1040,256]{1,0:T(8,128)(2,1)S(1)}, bf16[1040,256]{1,0:T(8,128)(2,1)S(1)}, u32[]{:S(2)}, u32[]{:S(2)}) collective-permute-start(bf16[1040,256]{1,0:T(8,128)(2,1)S(1)} %get-tuple-element.76), channel_id=1, source_target_pairs={{0,2},{1,3},{2,0},{3,1},{4,6},{5,7},{6,4},{7,5},{8,10},{9,11},{10,... | collective-permute-start | bytes 1597448 | tf_op jit(solution)/shard_map/ppermute | solution.py:85
  200.0 13.2 %collective-permute-start.56 = (bf16[1040,256]{1,0:T(8,128)(2,1)S(1)}, bf16[1040,256]{1,0:T(8,128)(2,1)S(1)}, u32[]{:S(2)}, u32[]{:S(2)}) collective-permute-start(bf16[1040,256]{1,0:T(8,128)(2,1)S(1)} %get-tuple-element.77), channel_id=1, source_target_pairs={{0,3},{1,0},{2,1},{3,2},{4,7},{5,4},{6,5},{7,6},{8,11},{9,8},{10,9... | collective-permute-start | bytes 1597448 | tf_op jit(solution)/shard_map/ppermute | solution.py:85
  201.5 13.7 %collective-permute-start.57 = (bf16[1040,256]{1,0:T(8,128)(2,1)S(1)}, bf16[1040,256]{1,0:T(8,128)(2,1)S(1)}, u32[]{:S(2)}, u32[]{:S(2)}) collective-permute-start(bf16[1040,256]{1,0:T(8,128)(2,1)S(1)} %get-tuple-element.78), channel_id=1, source_target_pairs={{0,1},{1,2},{2,3},{3,0},{4,5},{5,6},{6,7},{7,4},{8,9},{9,10},{10,1... | collective-permute-start | bytes 1597448 | tf_op jit(solution)/shard_map/ppermute | solution.py:85
  (5 other events, 17.6 us)
